TPU v7x, 512 devices: a whole 4x4x16 slice. The times are simulated.
512 devices in a mesh: group: 4 (over x), sec: 128 (over z, y, core).
Axes of the slice: x: 4, y: 4, z: 16, core: 2. Of those that a mesh axis runs over, the one named last changes fastest.
Arguments:
- fixed_desc: bfloat16 [128, 64, 64, 512], P('sec', 'group'), may hold values from -16 to 16
- moving_desc: bfloat16 [128, 64, 64, 512], P('sec', 'group'), may hold values from -16 to 16
- offsets: int32 [128, 64, 2, 64], P('sec', 'group'), may hold values from -8 to 8
- owner: int32 [128, 64], P('sec', 'group'), may hold values from 0 to 31
- counts: int32 [128, 4], P('sec', 'group'), may hold values from 1 to 16, 40 in all within a row
- vert: float32 [128, 64, 1024], P('sec', 'group'), may hold values from 0.5 to 2
- hori: float32 [128, 64, 1024], P('sec', 'group'), may hold values from 0.5 to 2
Outputs:
- displacement: float32 [128, 2, 64, 1024], P('sec', None, 'group')
- residual: float32 [128, 2, 64, 1024], P('sec', None, 'group')
Inputs may be any that keep to these rules, and one draw needn't show every extreme that they name: The counts of one section sum to 40, and in every section some block holds 16.
All inputs are finite; a program needn't handle non-finite values.
Results may differ from a plain program's by a relative error of at most 0.0003.
Values may be sent and summed in bfloat16 or wider, within the bound.
No kernel may reach another device: no remote copies, remote signals or barrier semaphores. Data moves between devices by JAX's collectives and lax.ppermute only.
A program may use at most 64 MiB of HBM per device.

v0:
```python
import math

import jax
import jax.numpy as jnp
from jax import lax
from jax.sharding import PartitionSpec as P

TILE_W = 128
OUTER = 2


spread_sq = 4.0
highest = lax.Precision.HIGHEST


def from_behind(block, axis, distance):
    devices = range(lax.axis_size(axis))
    route = [(i - distance, i) for i in devices if i - distance in devices]
    return lax.ppermute(block, axis, route)


def with_halo(cells, sides, width):
    for axis, dim in sides:
        count = lax.axis_size(axis)
        ends = count - 1
        head = lax.slice_in_dim(cells, 0, width, axis=dim)
        tail = lax.slice_in_dim(cells, cells.shape[dim] - width, cells.shape[dim], axis=dim)
        cells = jnp.concatenate(
            [
                lax.ppermute(tail, axis, [(i, (i + 1) % count) for i in range(ends)]),
                cells,
                lax.ppermute(head, axis, [((i + 1) % count, i) for i in range(ends)]),
            ],
            axis=dim,
        )
    return cells


def squares(field):
    return lax.psum(jnp.sum(field * field), ("group", "sec"))


def body(fixed_desc, moving_desc, offsets, owner, counts, vert, hori):
    sec_count = lax.axis_size("sec")
    sec_index = lax.axis_index("sec")
    group_count = lax.axis_size("group")
    patch_count = fixed_desc.shape[1]
    corr_len = fixed_desc.shape[3]
    row_count = vert.shape[1]
    col_count = vert.shape[2]
    tile_local = col_count // TILE_W
    tile_total = tile_local * group_count
    partner = from_behind(moving_desc, "sec", -1)
    scores = jnp.einsum(
        "pic,pjc->pij", fixed_desc[0], partner[0], preferred_element_type=jnp.float32
    ) / math.sqrt(corr_len)
    likely = jax.nn.softmax(scores, axis=-1)
    flow_rows = jnp.einsum(
        "pij,pkj->pki", likely, offsets[0].astype(jnp.float32), precision=highest
    )
    targets = jnp.transpose(jnp.mean(flow_rows, axis=-1))
    validity = (jnp.arange(patch_count) < counts[0, 0]).astype(jnp.float32)
    vert_local = vert[0]
    hori_local = hori[0]
    vert_above = from_behind(vert_local[-1:], "group", 1)
    vert_up = jnp.concatenate([vert_above, vert_local[:-1]], 0)
    hori_left = jnp.concatenate([jnp.zeros((row_count, 1), jnp.float32), hori_local[:, :-1]], 1)
    not_last = (sec_index < sec_count - 1).astype(jnp.float32)
    zero_col = jnp.zeros((2, row_count, 1), jnp.float32)
    one_hot = (owner[0][:, None] == jnp.arange(tile_total)[None, :]).astype(jnp.float32)

    def spread(values):
        count = values.shape[0]
        wide = jnp.broadcast_to(values[:, None, :, None], (count, row_count, tile_local, TILE_W))
        return wide.reshape(count, row_count, col_count)

    def neighbour_terms(field):
        padded = with_halo(field[None], (("group", 2), ("sec", 0)), 1)
        centre = padded[1]
        below = centre[:, 2:]
        above = centre[:, :-2]
        upper = padded[2, :, 1:-1]
        lower = padded[0, :, 1:-1]
        right = jnp.concatenate([field[:, :, 1:], zero_col], 2)
        left = jnp.concatenate([zero_col, field[:, :, :-1]], 2)
        spring = (
            vert_local * (field - below)
            + vert_up * (field - above)
            + hori_local * (field - right)
            + hori_left * (field - left)
        )
        return (spring, upper, lower)

    displacement = jnp.zeros((2, row_count, col_count), jnp.float32)
    residual = displacement
    for outer_step in range(OUTER):
        spring, upper, lower = neighbour_terms(displacement)
        gap = displacement - upper
        means = jnp.mean(gap.reshape(2, row_count, tile_local, TILE_W), axis=(1, 3))
        all_means = lax.all_gather(means, "group", axis=1, tiled=True)
        look = jnp.dot(all_means, one_hot.T, precision=highest)
        mismatch = look - targets
        weight = validity / (1.0 + jnp.sum(mismatch * mismatch, axis=0) / spread_sq)
        terms = jnp.concatenate([weight[None], weight[None] * targets], 0)
        tile_sum = lax.psum_scatter(
            jnp.dot(terms, one_hot, precision=highest), "group", scatter_dimension=1, tiled=True
        )
        tile_sum = tile_sum * not_last
        tile_below = from_behind(tile_sum, "sec", 1)
        wfield = spread(tile_sum[0:1])
        efield = spread(tile_sum[1:3])
        wprev = spread(tile_below[0:1])
        eprev = spread(tile_below[1:3])
        rhs = efield - eprev
        image = spring + wfield * (displacement - upper) + wprev * (displacement - lower)
        residual = rhs - image
        direction = residual
        norm_now = squares(residual)
        spring_part, upper_part, lower_part = neighbour_terms(direction)
        image = spring_part + wfield * (direction - upper_part) + wprev * (direction - lower_part)
        alpha = norm_now / lax.psum(jnp.sum(direction * image), ("group", "sec"))
        displacement = displacement + alpha * direction
        residual = residual - alpha * image
        norm_next = squares(residual)
        direction = residual + norm_next / norm_now * direction
        norm_now = norm_next
    return (displacement[None], residual[None])


def solution(mesh):
    in_specs = (
        P("sec", "group", None, None),
        P("sec", "group", None, None),
        P("sec", "group", None, None),
        P("sec", "group"),
        P("sec", "group"),
        P("sec", "group", None),
        P("sec", "group", None),
    )
    out_specs = (P("sec", None, "group", None), P("sec", None, "group", None))
    return jax.shard_map(body, mesh=mesh, in_specs=in_specs, out_specs=out_specs, check_vma=False)
```

profile of v0, /device:TPU:1, one launch (start us, length us, event | category | flops | bytes accessed | tf_op | source)
XLA Modules:
  0.0 349.6 jit_solution(14696046750092716895)
XLA Ops:
  0.7 4.1 %collective-permute-start = (f32[1,2,1,1024]{3,2,1,0:T(1,128)S(1)}, f32[1,2,1,1024]{3,2,1,0:T(1,128)S(1)}, u32[]{:S(2)}, u32[]{:S(2)}) collective-permute-start(f32[1,2,1,1024]{3,2,1,0:T(1,128)S(1)} %broadcast.149), channel_id=1, source_target_pairs={{0,128},{128,256},{256,384},{1,129},{129,257},{257,385},{2,130},{1... | collective-permute-start | bytes 24584 | tf_op jit(solution)/shard_map/ppermute | solution.py:30
  6.0 6.1 %collective-permute-start.3 = (bf16[1,16,64,512]{3,2,1,0:T(8,128)(2,1)}, bf16[1,16,64,512]{3,2,1,0:T(8,128)(2,1)S(1)}, u32[]{:S(2)}, u32[]{:S(2)}) collective-permute-start(bf16[1,16,64,512]{3,2,1,0:T(8,128)(2,1)} %param.8), channel_id=1, source_target_pairs={{1,0},{2,1},{3,2},{4,3},{5,4},{6,5},{7,6},{8,7},{9,8},{10,9},{11,1... | collective-permute-start | bytes 3145736 | tf_op jit(solution)/shard_map/ppermute | solution.py:19
  13.0 4.4 %collective-permute-start.5 = (f32[1,1024]{1,0:T(1,128)S(1)}, f32[1,1024]{1,0:T(1,128)S(1)}, u32[]{:S(2)}, u32[]{:S(2)}) collective-permute-start(f32[1,1024]{1,0:T(1,128)S(1)} %slice_bitcast_fusion.7), channel_id=1, source_target_pairs={{0,128},{128,256},{256,384},{1,129},{129,257},{257,385},{2,130},{1... | collective-permute-start | bytes 12296 | tf_op jit(solution)/shard_map/ppermute | solution.py:19
  18.3 1.9 collective-permute-start.2
  22.9 3.6 %collective-permute-start.6 = (f32[1,2,18,1024]{3,2,1,0:T(8,128)S(1)}, f32[1,2,18,1024]{3,2,1,0:T(8,128)S(1)}, u32[]{:S(2)}, u32[]{:S(2)}) collective-permute-start(f32[1,2,18,1024]{3,2,1,0:T(8,128)S(1)} %get-tuple-element.18), channel_id=1, source_target_pairs={{0,1},{1,2},{2,3},{3,4},{4,5},{5,6},{6,7},{7,8},{8,9},{9,10},{10,1... | collective-permute-start | bytes 442376 | tf_op jit(solution)/shard_map/ppermute | solution.py:30
  26.7 7.1 %all-gather = f32[4,8,2]{1,2,0:T(2,128)S(1)} all-gather(f32[1,8,2]{1,2,0:T(2,128)S(1)} %multiply_bitcast_fusion.3), channel_id=1, replica_groups=mesh['group'=4,'sec'=128] {'group'}, dimensions={0}, use_global_device_ids=true | all-gather | bytes 320 | tf_op jit(solution)/shard_map/all_gather | solution.py:100
  37.2 6.0 %all-reduce.7 = f32[3,32]{1,0:T(4,128)S(1)} all-reduce(f32[3,32]{1,0:T(4,128)S(1)} %fusion.61), channel_id=2, replica_groups=mesh['group'=4,'sec'=128] {'group'}, use_global_device_ids=true, to_apply=%region_6.0.clone | all-reduce | flops 96 | bytes 768
  43.2 5.5 %collective-permute-start.4 = (f32[3,8]{1,0:T(4,128)S(1)}, f32[3,8]{1,0:T(4,128)S(1)}, u32[]{:S(2)}, u32[]{:S(2)}) collective-permute-start(f32[3,8]{1,0:T(4,128)S(1)} %dynamic-slice_multiply_fusion.1), channel_id=1, source_target_pairs={{0,1},{1,2},{2,3},{3,4},{4,5},{5,6},{6,7},{7,8},{8,9},{9,10},{10,1... | collective-permute-start | bytes 296 | tf_op jit(solution)/shard_map/ppermute | solution.py:19
  49.7 3.6 %collective-permute-start.7 = (f32[1,2,1,1024]{3,2,1,0:T(1,128)S(1)}, f32[1,2,1,1024]{3,2,1,0:T(1,128)S(1)}, u32[]{:S(2)}, u32[]{:S(2)}) collective-permute-start(f32[1,2,1,1024]{3,2,1,0:T(1,128)S(1)} %get-tuple-element.31), channel_id=1, source_target_pairs={{0,128},{128,256},{256,384},{1,129},{129,257},{257,385},{2,130},{1... | collective-permute-start | bytes 24584 | tf_op jit(solution)/shard_map/ppermute | solution.py:30
  54.7 3.1 collective-permute-done.8
  57.8 5.6 %collective-permute-start.10 = (f32[1,2,18,1024]{3,2,1,0:T(8,128)S(1)}, f32[1,2,18,1024]{3,2,1,0:T(8,128)S(1)}, u32[]{:S(2)}, u32[]{:S(2)}) collective-permute-start(f32[1,2,18,1024]{3,2,1,0:T(8,128)S(1)} %get-tuple-element.16), channel_id=1, source_target_pairs={{0,1},{1,2},{2,3},{3,4},{4,5},{5,6},{6,7},{7,8},{8,9},{9,10},{10,1... | collective-permute-start | bytes 442376 | tf_op jit(solution)/shard_map/ppermute | solution.py:30
  63.4 1.9 collective-permute-start.9
  66.0 4.4 %collective-permute-done.9 = f32[1,2,18,1024]{3,2,1,0:T(8,128)S(1)} collective-permute-done((f32[1,2,18,1024]{3,2,1,0:T(8,128)S(1)}, f32[1,2,18,1024]{3,2,1,0:T(8,128)S(1)}, u32[]{:S(2)}, u32[]{:S(2)}) %collective-permute-start.9) | collective-permute-done | bytes 147488 | tf_op jit(solution)/shard_map/ppermute | solution.py:32
  71.3 117.3 %all-reduce.10 = (f32[]{:T(128)}, f32[]{:T(128)}) all-reduce(f32[]{:T(128)} %get-tuple-element.5, f32[]{:T(128)} %get-tuple-element.4), channel_id=1, replica_groups=mesh['group'=4,'sec'=128] {'group','sec'}, use_global_device_ids=true, to_apply=%region_8.0 | all-reduce | flops 2 | bytes 16 | tf_op jit(solution)/shard_map/psum | solution.py:40
  189.9 3.1 collective-permute-start.11
  194.3 3.1 collective-permute-done.12
  197.4 4.0 %collective-permute-start.13 = (f32[1,2,18,1024]{3,2,1,0:T(8,128)S(1)}, f32[1,2,18,1024]{3,2,1,0:T(8,128)S(1)}, u32[]{:S(2)}, u32[]{:S(2)}) collective-permute-start(f32[1,2,18,1024]{3,2,1,0:T(8,128)S(1)} %get-tuple-element.14), channel_id=1, source_target_pairs={{1,0},{2,1},{3,2},{4,3},{5,4},{6,5},{7,6},{8,7},{9,8},{10,9},{11,1... | collective-permute-start | bytes 442376 | tf_op jit(solution)/shard_map/ppermute | solution.py:32
  204.5 6.6 %all-gather.1 = f32[4,8,2]{1,2,0:T(2,128)S(1)} all-gather(f32[1,8,2]{1,2,0:T(2,128)S(1)} %multiply_bitcast_fusion.2), channel_id=1, replica_groups=mesh['group'=4,'sec'=128] {'group'}, dimensions={0}, use_global_device_ids=true | all-gather | bytes 320 | tf_op jit(solution)/shard_map/all_gather | solution.py:100
  211.8 6.1 %all-reduce.8 = f32[3,32]{1,0:T(4,128)S(1)} all-reduce(f32[3,32]{1,0:T(4,128)S(1)} %fusion.60), channel_id=3, replica_groups=mesh['group'=4,'sec'=128] {'group'}, use_global_device_ids=true, to_apply=%region_14.0.clone | all-reduce | flops 96 | bytes 768
  217.9 5.8 %collective-permute-start.14 = (f32[3,8]{1,0:T(4,128)S(1)}, f32[3,8]{1,0:T(4,128)S(1)}, u32[]{:S(2)}, u32[]{:S(2)}) collective-permute-start(f32[3,8]{1,0:T(4,128)S(1)} %dynamic-slice_multiply_fusion), channel_id=1, source_target_pairs={{0,1},{1,2},{2,3},{3,4},{4,5},{5,6},{6,7},{7,8},{8,9},{9,10},{10,1... | collective-permute-start | bytes 296 | tf_op jit(solution)/shard_map/ppermute | solution.py:19
  224.8 3.3 collective-permute-start.16
  229.4 3.1 collective-permute-done.17
  234.4 5.6 %collective-permute-start.19 = (f32[1,2,18,1024]{3,2,1,0:T(8,128)S(1)}, f32[1,2,18,1024]{3,2,1,0:T(8,128)S(1)}, u32[]{:S(2)}, u32[]{:S(2)}) collective-permute-start(f32[1,2,18,1024]{3,2,1,0:T(8,128)S(1)} %get-tuple-element.12), channel_id=1, source_target_pairs={{0,1},{1,2},{2,3},{3,4},{4,5},{5,6},{6,7},{7,8},{8,9},{9,10},{10,1... | collective-permute-start | bytes 442376 | tf_op jit(solution)/shard_map/ppermute | solution.py:30
  243.4 104.2 %all-reduce.9 = (f32[]{:T(128)}, f32[]{:T(128)}) all-reduce(f32[]{:T(128)} %get-tuple-element.3, f32[]{:T(128)} %get-tuple-element.2), channel_id=1, replica_groups=mesh['group'=4,'sec'=128] {'group','sec'}, use_global_device_ids=true, to_apply=%region_16.0 | all-reduce | flops 2 | bytes 16 | tf_op jit(solution)/shard_map/psum | solution.py:40
  (100 shorter events, 25.2 us)
Async XLA Ops:
  0.6 33.3 %copy-start = (bf16[1,16,64,512]{3,2,1,0:T(8,128)(2,1)S(1)}, bf16[1,16,64,512]{3,2,1,0:T(8,128)(2,1)}, u32[]{:S(2)}) copy-start(bf16[1,16,64,512]{3,2,1,0:T(8,128)(2,1)} %param.7) | copy-start | bytes 3145732
  0.7 17.6 %collective-permute-start = (f32[1,2,1,1024]{3,2,1,0:T(1,128)S(1)}, f32[1,2,1,1024]{3,2,1,0:T(1,128)S(1)}, u32[]{:S(2)}, u32[]{:S(2)}) collective-permute-start(f32[1,2,1,1024]{3,2,1,0:T(1,128)S(1)} %broadcast.149), channel_id=1, source_target_pairs={{0,128},{128,256},{256,384},{1,129},{129,257},{257,385},{2,130},{1... | collective-permute-start | bytes 24584 | tf_op jit(solution)/shard_map/ppermute | solution.py:30
  4.7 13.5 %collective-permute-start.1 = (f32[1,2,1,1024]{3,2,1,0:T(1,128)S(1)}, f32[1,2,1,1024]{3,2,1,0:T(1,128)S(1)}, u32[]{:S(2)}, u32[]{:S(2)}) collective-permute-start(f32[1,2,1,1024]{3,2,1,0:T(1,128)S(1)} %broadcast.149), channel_id=1, source_target_pairs={{128,0},{256,128},{384,256},{129,1},{257,129},{385,257},{130,2},{2... | collective-permute-start | bytes 24584 | tf_op jit(solution)/shard_map/ppermute | solution.py:32
  6.0 27.9 %collective-permute-start.3 = (bf16[1,16,64,512]{3,2,1,0:T(8,128)(2,1)}, bf16[1,16,64,512]{3,2,1,0:T(8,128)(2,1)S(1)}, u32[]{:S(2)}, u32[]{:S(2)}) collective-permute-start(bf16[1,16,64,512]{3,2,1,0:T(8,128)(2,1)} %param.8), channel_id=1, source_target_pairs={{1,0},{2,1},{3,2},{4,3},{5,4},{6,5},{7,6},{8,7},{9,8},{10,9},{11,1... | collective-permute-start | bytes 3145736 | tf_op jit(solution)/shard_map/ppermute | solution.py:19
  13.0 5.2 %copy-start.2 = (f32[1,16,1024]{2,1,0:T(8,128)S(1)}, f32[1,16,1024]{2,1,0:T(8,128)}, u32[]{:S(2)}) copy-start(f32[1,16,1024]{2,1,0:T(8,128)} %param.13) | copy-start | bytes 196612
  13.0 9.9 %collective-permute-start.5 = (f32[1,1024]{1,0:T(1,128)S(1)}, f32[1,1024]{1,0:T(1,128)S(1)}, u32[]{:S(2)}, u32[]{:S(2)}) collective-permute-start(f32[1,1024]{1,0:T(1,128)S(1)} %slice_bitcast_fusion.7), channel_id=1, source_target_pairs={{0,128},{128,256},{256,384},{1,129},{129,257},{257,385},{2,130},{1... | collective-permute-start | bytes 12296 | tf_op jit(solution)/shard_map/ppermute | solution.py:19
  18.3 8.3 %collective-permute-start.2 = (f32[1,2,18,1024]{3,2,1,0:T(8,128)S(1)}, f32[1,2,18,1024]{3,2,1,0:T(8,128)S(1)}, u32[]{:S(2)}, u32[]{:S(2)}) collective-permute-start(f32[1,2,18,1024]{3,2,1,0:T(8,128)S(1)} %get-tuple-element.18), channel_id=1, source_target_pairs={{1,0},{2,1},{3,2},{4,3},{5,4},{6,5},{7,6},{8,7},{9,8},{10,9},{11,1... | collective-permute-start | bytes 442376 | tf_op jit(solution)/shard_map/ppermute | solution.py:32
  22.9 26.7 %collective-permute-start.6 = (f32[1,2,18,1024]{3,2,1,0:T(8,128)S(1)}, f32[1,2,18,1024]{3,2,1,0:T(8,128)S(1)}, u32[]{:S(2)}, u32[]{:S(2)}) collective-permute-start(f32[1,2,18,1024]{3,2,1,0:T(8,128)S(1)} %get-tuple-element.18), channel_id=1, source_target_pairs={{0,1},{1,2},{2,3},{3,4},{4,5},{5,6},{6,7},{7,8},{8,9},{9,10},{10,1... | collective-permute-start | bytes 442376 | tf_op jit(solution)/shard_map/ppermute | solution.py:30
  34.4 0.7 copy-start.3
  36.9 12.7 %copy-start.1 = (f32[1,16,1024]{2,1,0:T(8,128)S(1)}, f32[1,16,1024]{2,1,0:T(8,128)}, u32[]{:S(2)}) copy-start(f32[1,16,1024]{2,1,0:T(8,128)} %param.12) | copy-start | bytes 196612
  43.2 6.2 %collective-permute-start.4 = (f32[3,8]{1,0:T(4,128)S(1)}, f32[3,8]{1,0:T(4,128)S(1)}, u32[]{:S(2)}, u32[]{:S(2)}) collective-permute-start(f32[3,8]{1,0:T(4,128)S(1)} %dynamic-slice_multiply_fusion.1), channel_id=1, source_target_pairs={{0,1},{1,2},{2,3},{3,4},{4,5},{5,6},{6,7},{7,8},{8,9},{9,10},{10,1... | collective-permute-start | bytes 296 | tf_op jit(solution)/shard_map/ppermute | solution.py:19
  49.7 4.9 %collective-permute-start.7 = (f32[1,2,1,1024]{3,2,1,0:T(1,128)S(1)}, f32[1,2,1,1024]{3,2,1,0:T(1,128)S(1)}, u32[]{:S(2)}, u32[]{:S(2)}) collective-permute-start(f32[1,2,1,1024]{3,2,1,0:T(1,128)S(1)} %get-tuple-element.31), channel_id=1, source_target_pairs={{0,128},{128,256},{256,384},{1,129},{129,257},{257,385},{2,130},{1... | collective-permute-start | bytes 24584 | tf_op jit(solution)/shard_map/ppermute | solution.py:30
  53.4 4.4 %collective-permute-start.8 = (f32[1,2,1,1024]{3,2,1,0:T(1,128)S(1)}, f32[1,2,1,1024]{3,2,1,0:T(1,128)S(1)}, u32[]{:S(2)}, u32[]{:S(2)}) collective-permute-start(f32[1,2,1,1024]{3,2,1,0:T(1,128)S(1)} %get-tuple-element.32), channel_id=1, source_target_pairs={{128,0},{256,128},{384,256},{129,1},{257,129},{385,257},{130,2},{2... | collective-permute-start | bytes 24584 | tf_op jit(solution)/shard_map/ppermute | solution.py:32
  57.8 8.2 %collective-permute-start.10 = (f32[1,2,18,1024]{3,2,1,0:T(8,128)S(1)}, f32[1,2,18,1024]{3,2,1,0:T(8,128)S(1)}, u32[]{:S(2)}, u32[]{:S(2)}) collective-permute-start(f32[1,2,18,1024]{3,2,1,0:T(8,128)S(1)} %get-tuple-element.16), channel_id=1, source_target_pairs={{0,1},{1,2},{2,3},{3,4},{4,5},{5,6},{6,7},{7,8},{8,9},{9,10},{10,1... | collective-permute-start | bytes 442376 | tf_op jit(solution)/shard_map/ppermute | solution.py:30
  63.4 7.0 %collective-permute-start.9 = (f32[1,2,18,1024]{3,2,1,0:T(8,128)S(1)}, f32[1,2,18,1024]{3,2,1,0:T(8,128)S(1)}, u32[]{:S(2)}, u32[]{:S(2)}) collective-permute-start(f32[1,2,18,1024]{3,2,1,0:T(8,128)S(1)} %get-tuple-element.16), channel_id=1, source_target_pairs={{1,0},{2,1},{3,2},{4,3},{5,4},{6,5},{7,6},{8,7},{9,8},{10,9},{11,1... | collective-permute-start | bytes 442376 | tf_op jit(solution)/shard_map/ppermute | solution.py:32
  189.9 4.4 %collective-permute-start.11 = (f32[1,2,1,1024]{3,2,1,0:T(1,128)S(1)}, f32[1,2,1,1024]{3,2,1,0:T(1,128)S(1)}, u32[]{:S(2)}, u32[]{:S(2)}) collective-permute-start(f32[1,2,1,1024]{3,2,1,0:T(1,128)S(1)} %get-tuple-element.27), channel_id=1, source_target_pairs={{0,128},{128,256},{256,384},{1,129},{129,257},{257,385},{2,130},{1... | collective-permute-start | bytes 24584 | tf_op jit(solution)/shard_map/ppermute | solution.py:30
  193.0 4.4 %collective-permute-start.12 = (f32[1,2,1,1024]{3,2,1,0:T(1,128)S(1)}, f32[1,2,1,1024]{3,2,1,0:T(1,128)S(1)}, u32[]{:S(2)}, u32[]{:S(2)}) collective-permute-start(f32[1,2,1,1024]{3,2,1,0:T(1,128)S(1)} %get-tuple-element.28), channel_id=1, source_target_pairs={{128,0},{256,128},{384,256},{129,1},{257,129},{385,257},{130,2},{2... | collective-permute-start | bytes 24584 | tf_op jit(solution)/shard_map/ppermute | solution.py:32
  197.4 7.0 %collective-permute-start.13 = (f32[1,2,18,1024]{3,2,1,0:T(8,128)S(1)}, f32[1,2,18,1024]{3,2,1,0:T(8,128)S(1)}, u32[]{:S(2)}, u32[]{:S(2)}) collective-permute-start(f32[1,2,18,1024]{3,2,1,0:T(8,128)S(1)} %get-tuple-element.14), channel_id=1, source_target_pairs={{1,0},{2,1},{3,2},{4,3},{5,4},{6,5},{7,6},{8,7},{9,8},{10,9},{11,1... | collective-permute-start | bytes 442376 | tf_op jit(solution)/shard_map/ppermute | solution.py:32
  201.5 23.1 %collective-permute-start.15 = (f32[1,2,18,1024]{3,2,1,0:T(8,128)S(1)}, f32[1,2,18,1024]{3,2,1,0:T(8,128)S(1)}, u32[]{:S(2)}, u32[]{:S(2)}) collective-permute-start(f32[1,2,18,1024]{3,2,1,0:T(8,128)S(1)} %get-tuple-element.14), channel_id=1, source_target_pairs={{0,1},{1,2},{2,3},{3,4},{4,5},{5,6},{6,7},{7,8},{8,9},{9,10},{10,1... | collective-permute-start | bytes 442376 | tf_op jit(solution)/shard_map/ppermute | solution.py:30
  217.9 6.5 %collective-permute-start.14 = (f32[3,8]{1,0:T(4,128)S(1)}, f32[3,8]{1,0:T(4,128)S(1)}, u32[]{:S(2)}, u32[]{:S(2)}) collective-permute-start(f32[3,8]{1,0:T(4,128)S(1)} %dynamic-slice_multiply_fusion), channel_id=1, source_target_pairs={{0,1},{1,2},{2,3},{3,4},{4,5},{5,6},{6,7},{7,8},{8,9},{9,10},{10,1... | collective-permute-start | bytes 296 | tf_op jit(solution)/shard_map/ppermute | solution.py:19
  224.8 4.6 %collective-permute-start.16 = (f32[1,2,1,1024]{3,2,1,0:T(1,128)S(1)}, f32[1,2,1,1024]{3,2,1,0:T(1,128)S(1)}, u32[]{:S(2)}, u32[]{:S(2)}) collective-permute-start(f32[1,2,1,1024]{3,2,1,0:T(1,128)S(1)} %get-tuple-element.23), channel_id=1, source_target_pairs={{0,128},{128,256},{256,384},{1,129},{129,257},{257,385},{2,130},{1... | collective-permute-start | bytes 24584 | tf_op jit(solution)/shard_map/ppermute | solution.py:30
  228.0 4.4 %collective-permute-start.17 = (f32[1,2,1,1024]{3,2,1,0:T(1,128)S(1)}, f32[1,2,1,1024]{3,2,1,0:T(1,128)S(1)}, u32[]{:S(2)}, u32[]{:S(2)}) collective-permute-start(f32[1,2,1,1024]{3,2,1,0:T(1,128)S(1)} %get-tuple-element.24), channel_id=1, source_target_pairs={{128,0},{256,128},{384,256},{129,1},{257,129},{385,257},{130,2},{2... | collective-permute-start | bytes 24584 | tf_op jit(solution)/shard_map/ppermute | solution.py:32
  232.5 9.0 %collective-permute-start.18 = (f32[1,2,18,1024]{3,2,1,0:T(8,128)S(1)}, f32[1,2,18,1024]{3,2,1,0:T(8,128)S(1)}, u32[]{:S(2)}, u32[]{:S(2)}) collective-permute-start(f32[1,2,18,1024]{3,2,1,0:T(8,128)S(1)} %get-tuple-element.12), channel_id=1, source_target_pairs={{1,0},{2,1},{3,2},{4,3},{5,4},{6,5},{7,6},{8,7},{9,8},{10,9},{11,1... | collective-permute-start | bytes 442376 | tf_op jit(solution)/shard_map/ppermute | solution.py:32
  234.4 8.2 %collective-permute-start.19 = (f32[1,2,18,1024]{3,2,1,0:T(8,128)S(1)}, f32[1,2,18,1024]{3,2,1,0:T(8,128)S(1)}, u32[]{:S(2)}, u32[]{:S(2)}) collective-permute-start(f32[1,2,18,1024]{3,2,1,0:T(8,128)S(1)} %get-tuple-element.12), channel_id=1, source_target_pairs={{0,1},{1,2},{2,3},{3,4},{4,5},{5,6},{6,7},{7,8},{8,9},{9,10},{10,1... | collective-permute-start | bytes 442376 | tf_op jit(solution)/shard_map/ppermute | solution.py:30
  (1 other events, 0.7 us)
where the time goes:
time: 351 us; the launch traced here: 350 us
  blocking collectives  247 us (70%)
  starting transfers between devices  67.6 us (19%)
  waiting for transfers between devices  18.9 us (5%)
  local copies, waits for them, and re-layouts  5.37 us (2%)
  between operations  4.98 us (1%)
  other arithmetic  3.55 us (1%)
    psum x2, blocking collectives, squares(): return lax.psum(jnp.sum(field * field), ('group', 'sec'))  221 us
    ppermute x8, starting transfers between devices, with_halo(): lax.ppermute(tail, axis, [(i, (i + 1) % count) for i in range(ends)])  30.8 us
    ppermute x4, starting transfers between devices, from_behind(): return lax.ppermute(block, axis, route)  21.8 us
    ppermute x8, waiting for transfers between devices, with_halo(): lax.ppermute(head, axis, [((i + 1) % count, i) for i in range(ends)])  15.9 us
    ppermute x8, starting transfers between devices, with_halo(): lax.ppermute(head, axis, [((i + 1) % count, i) for i in range(ends)])  15 us
    all_gather x2, blocking collectives, body(): all_means = lax.all_gather(means, 'group', axis=1, tiled=True)  13.7 us
    unnamed x2, blocking collectives  12.1 us
  transfers between devices with their start and end apart: 20, of which 10 were waited for; matrix products, arithmetic and copies ran while one was open for 2% of the time, Pallas kernels for 0%

commit v1 on v0

v1 whole, which is shorter than its diff:
```python
import math

import jax
import jax.numpy as jnp
from jax import lax
from jax.experimental import pallas as pl
from jax.experimental.pallas import tpu as pltpu
from jax.sharding import Mesh, PartitionSpec as P

TILE_W = 128
SPREAD_SQ = 4.0
CHIPS_Y = 4
CORES = 2
SEC = ("z", "y", "core")
F32 = jnp.float32

COLUMN_KV, COLUMN_K2V, COLUMN_KXV, COLUMN_VL, COLUMN_VR, COLUMN_HT, COLUMN_HB = range(7)
COLUMN_DV, COLUMN_XBR, COLUMN_XBL, COLUMN_XTR, COLUMN_XTL = range(7, 12)
COLUMN_KH, COLUMN_K2H, COLUMN_KXH, COLUMN_DH, COLUMN_DT = range(12, 17)
COLUMN_OWNER = 17
COLUMN_NEAR = 19
COLUMN_FAR = 21
GROUP_LANES = 32


def iota(shape, axis):
    return lax.broadcasted_iota(jnp.int32, shape, axis)


def lane_sum(x):
    return jnp.sum(x, axis=1, keepdims=True)


def row_sum(x):
    return jnp.sum(x, axis=0, keepdims=True)


def total(x):
    return lane_sum(row_sum(x))


def edge_kernel(vert_ref, hori_ref, above_ref, out_ref):
    rows, cols = hori_ref.shape
    tiles = cols // TILE_W
    lane = iota((rows, TILE_W), 1)
    last = jnp.zeros((rows, TILE_W), F32)
    for j in range(tiles):
        out_ref[j : j + 1, :] = vert_ref[rows - 1 : rows, j * TILE_W : (j + 1) * TILE_W]
        column = hori_ref[:, (j + 1) * TILE_W - 1 : (j + 1) * TILE_W]
        last = jnp.where(lane == j, column, last)
    out_ref[tiles : 2 * tiles, :] = above_ref[...]
    out_ref[2 * tiles : 2 * tiles + rows, :] = last


def border_kernel(group_ref, vert_ref, hori_ref, own_ref, next_ref, owner_ref, out_ref, stack):
    rows, cols = hori_ref.shape
    tiles = cols // TILE_W
    last_group = group_ref[0] == group_ref[1]
    bottom = jnp.where(last_group, 1.0, 4.0).astype(F32)

    v_last = own_ref[0:tiles, :]
    v_above = own_ref[tiles : 2 * tiles, :]
    for j in range(tiles):
        span = slice(j * TILE_W, (j + 1) * TILE_W)
        stack[j : j + 1, :] = vert_ref[rows - 2 : rows - 1, span]
        stack[tiles + j : tiles + j + 1, :] = vert_ref[0:1, span]
        stack[2 * tiles + j : 2 * tiles + j + 1, :] = hori_ref[rows - 1 : rows, span]
        stack[3 * tiles + j : 3 * tiles + j + 1, :] = hori_ref[0:1, span]
    v_second, v_first = stack[0:tiles, :], stack[tiles : 2 * tiles, :]
    h_last, h_first = stack[2 * tiles : 3 * tiles, :], stack[3 * tiles : 4 * tiles, :]
    lane = iota((tiles, TILE_W), 1)
    inside = lane < TILE_W - 1
    square = v_last * v_last
    step_last = v_last - pltpu.roll(v_last, TILE_W - 1, 1)
    step_above = v_above - pltpu.roll(v_above, TILE_W - 1, 1)
    dh = lane_sum(
        bottom * square * v_last
        + v_second * square
        + jnp.where(inside, h_last * step_last * step_last, 0.0)
    )
    dt = lane_sum(
        v_first * v_above * v_above + jnp.where(inside, h_first * step_above * step_above, 0.0)
    )
    table = owner_ref[...]
    for column, value in (
        (COLUMN_KH, lane_sum(v_last)),
        (COLUMN_K2H, lane_sum(square)),
        (COLUMN_KXH, lane_sum(v_last * next_ref[0:tiles, :])),
        (COLUMN_DH, dh),
        (COLUMN_DT, dt),
    ):
        table = jnp.where(lane == column, value, table)

    tall = iota((rows, TILE_W), 1)
    zero = jnp.zeros((rows, TILE_W), F32)
    picked = {}
    for name, ref, column in (
        ("h0", hori_ref, 0),
        ("h126", hori_ref, TILE_W - 2),
        ("v0", vert_ref, 0),
        ("v1", vert_ref, 1),
        ("v126", vert_ref, TILE_W - 2),
        ("v127", vert_ref, TILE_W - 1),
    ):
        value = zero
        for j in range(tiles):
            at = j * TILE_W + column
            value = jnp.where(tall == j, ref[:, at : at + 1], value)
        picked[name] = value
    wide = iota((tiles, TILE_W), 0)
    diagonal = iota((tiles, TILE_W), 1) == wide

    def above_at(column):
        return row_sum(jnp.where(diagonal, v_above[:, column : column + 1], 0.0))

    a0, a1 = above_at(0), above_at(1)
    a126, a127 = above_at(TILE_W - 2), above_at(TILE_W - 1)
    right = own_ref[2 * tiles : 2 * tiles + rows, :]
    left = pltpu.roll(right, 1, 1)
    row = iota((rows, TILE_W), 0)
    within = row < rows - 1
    inner_tile = iota((1, TILE_W), 1) < tiles - 1
    step_right = right - pltpu.roll(right, rows - 1, 0)
    step_left = left - pltpu.roll(left, rows - 1, 0)
    right_sq, left_sq = right * right, left * left
    side_right = row_sum(
        picked["h126"] * right_sq + jnp.where(within, picked["v127"] * step_right * step_right, 0.0)
    )
    side_left = row_sum(
        picked["h0"] * left_sq + jnp.where(within, picked["v0"] * step_left * step_left, 0.0)
    )
    cube = row_sum(right_sq * right)
    dv = side_right + jnp.where(
        inner_tile, pltpu.roll(side_left, TILE_W - 1, 1) + 4.0 * cube, cube
    )
    end, pre = rows - 1, rows - 2
    v0, v1, v126, v127 = (picked[n] for n in ("v0", "v1", "v126", "v127"))
    h0, h126 = picked["h0"], picked["h126"]

    def at(x, r):
        return x[r : r + 1, :]

    xbr = at(h126, end) * (at(v127, end) - at(v126, end)) * at(right, end) + at(v127, pre) * at(
        v127, end
    ) * (at(right, end) - at(right, pre))
    xbl = -(
        at(h0, end) * (at(v0, end) - at(v1, end)) * at(left, end)
        + at(v0, pre) * at(v0, end) * (at(left, end) - at(left, pre))
    )
    xtr = -(
        at(h126, 0) * (a127 - a126) * at(right, 0)
        + at(v127, 0) * a127 * (at(right, 0) - at(right, 1))
    )
    xtl = at(h0, 0) * (a0 - a1) * at(left, 0) + at(v0, 0) * a0 * (at(left, 0) - at(left, 1))
    next_right = next_ref[2 * tiles : 2 * tiles + rows, :]
    stack[...] = jnp.zeros_like(stack)
    for column, value in (
        (COLUMN_KV, row_sum(right)),
        (COLUMN_K2V, row_sum(right_sq)),
        (COLUMN_KXV, row_sum(right * next_right)),
        (COLUMN_VL, at(v0, end)),
        (COLUMN_VR, at(v127, end)),
        (COLUMN_HT, at(right, 0)),
        (COLUMN_HB, at(right, end)),
        (COLUMN_DV, dv),
        (COLUMN_XBR, xbr),
        (COLUMN_XBL, xbl),
        (COLUMN_XTR, xtr),
        (COLUMN_XTL, xtl),
    ):
        stack[column : column + 1, :] = value
    turned = jnp.transpose(stack[...])[0:tiles, :]
    out_ref[...] = jnp.where(lane <= COLUMN_XTL, turned, table)


def match_kernel(column, last, fixed_ref, moving_ref, offsets_ref, table_ref, out_ref):
    patches, flow, corr = fixed_ref.shape[-3:]
    fixed = fixed_ref.reshape(patches * flow, corr)
    moving = moving_ref.reshape(patches * flow, corr)
    pair = 2 * flow
    lane = iota((flow, pair), 1)
    lower = lane < flow
    scale = 1.0 / math.sqrt(corr)
    shifts = offsets_ref[...]
    table = table_ref[...]
    spot_row = iota(table.shape, 0)
    spot_lane = iota(table.shape, 1)
    for first in range(0, patches, 2):
        at = slice(first * flow, (first + 2) * flow)
        scores = lax.dot_general(
            moving[at, :], fixed[at, :], (((1,), (1,)), ((), ())), preferred_element_type=F32
        )
        both = jnp.where(lower, scores[0:flow, :], scores[flow:pair, :])
        top = jnp.max(both, axis=0, keepdims=True)
        likely = jnp.exp((both - top) * scale)
        sums = lax.dot_general(
            shifts,
            likely,
            (((1,), (0,)), ((), ())),
            precision=lax.Precision.HIGHEST,
            preferred_element_type=F32,
        )
        weight = row_sum(likely)
        ratio = sums / (weight * flow)
        for half in range(2):
            keep = (iota((1, pair), 1) < flow) == (half == 0)
            for k in range(2):
                where = 2 * (first + half) + k
                value = lane_sum(jnp.where(keep, ratio[where : where + 1, :], 0.0))
                spot = (spot_row == first + half) & (spot_lane == column + k)
                table = jnp.where(spot, value, table)
    if not last:
        out_ref[...] = table
        return
    per_row = TILE_W // GROUP_LANES
    table = jnp.where(spot_lane < GROUP_LANES, table, 0.0)
    for half in range(table.shape[0] // per_row):
        line = jnp.zeros((1, TILE_W), F32)
        for j in range(per_row):
            source = table[half * per_row + j : half * per_row + j + 1, :]
            line = line + (pltpu.roll(source, j * GROUP_LANES, 1) if j else source)
        out_ref[half : half + 1, :] = line


def stack_kernel(
    dims, place_ref, seen_ref, vert_ref, hori_ref, own_ref, next_ref, prev_ref,
    disp_ref, res_ref, rows_ref, turn_ref, sums_ref, out_ref, field_ref,
):
    groups, sections, rows, tiles, chips_z = dims
    per_chip = sections // chips_z
    halves = tiles * GROUP_LANES // TILE_W
    count = groups * tiles
    nodes = float(rows * TILE_W)
    me, group = place_ref[0], place_ref[1]

    for core in range(CORES):
        for g in range(groups):
            for y in range(per_chip // CORES):
                base = ((core * groups + g) * (per_chip // CORES) + y) * chips_z * halves
                for h in range(halves):
                    rows_ref[g * halves + h, pl.ds(y * CORES + core, chips_z, stride=per_chip), :] = seen_ref[
                        pl.ds(base + h, chips_z, stride=halves), :
                    ]
    for g in range(groups):
        for h in range(halves):
            turn_ref[g, h * TILE_W : (h + 1) * TILE_W, :] = jnp.transpose(rows_ref[g * halves + h])

    def block(g, column):
        return turn_ref[g, pl.ds(column, tiles, stride=GROUP_LANES), :]

    def figure(column):
        return jnp.concatenate([block(g, column) for g in range(groups)], 0)

    def slots(near, far, turn):
        parts = []
        for g in range(groups):
            parts.append(block(g, near))
            other = block(g, far)
            parts.append(pltpu.roll(other, sections - 1, 1) if turn else other)
        return jnp.concatenate(parts, 0)

    lane = iota((count, sections), 1)
    tile_row = iota((count, sections), 0)
    along = lax.rem(tile_row, tiles)
    not_last = lane < sections - 1

    def up(x):
        return jnp.where(not_last, pltpu.roll(x, sections - 1, 1), 0.0)

    def low(x):
        return jnp.where(lane > 0, pltpu.roll(x, 1, 1), 0.0)

    zero_tiles = jnp.zeros((tiles, sections), F32)

    def from_above(x):
        return jnp.concatenate([zero_tiles, x[: count - tiles]], 0)

    def from_below(x):
        return jnp.concatenate([x[tiles:], zero_tiles], 0)

    def from_left(x):
        return jnp.where(along > 0, pltpu.roll(x, 1, 0), 0.0)

    def from_right(x):
        return jnp.where(along < tiles - 1, pltpu.roll(x, count - 1, 0), 0.0)

    owner = slots(COLUMN_OWNER, COLUMN_OWNER + 1, False)
    targets = [slots(COLUMN_NEAR + k, COLUMN_FAR + k, True) for k in range(2)]
    valid = jnp.where(owner >= 0.0, 1.0, 0.0)

    def tile_sums(miss):
        weight = valid / (1.0 + (miss[0] * miss[0] + miss[1] * miss[1]) / SPREAD_SQ)
        terms = (weight, weight * targets[0], weight * targets[1])
        for t in range(count):
            mine = owner == float(t)
            for n, term in enumerate(terms):
                sums_ref[n, t : t + 1, :] = row_sum(jnp.where(mine, term, 0.0))
        return [jnp.where(not_last, sums_ref[n], 0.0) for n in range(3)]

    kh, kv = figure(COLUMN_KH), figure(COLUMN_KV)
    k2h, k2v = figure(COLUMN_K2H), figure(COLUMN_K2V)
    kxh, kxv = figure(COLUMN_KXH), figure(COLUMN_KXV)
    vl, vr = figure(COLUMN_VL), figure(COLUMN_VR)
    ht, hb = figure(COLUMN_HT), figure(COLUMN_HB)
    dh, dt, dv = figure(COLUMN_DH), figure(COLUMN_DT), figure(COLUMN_DV)
    xbr, xbl, xtr, xtl = (figure(c) for c in (COLUMN_XBR, COLUMN_XBL, COLUMN_XTR, COLUMN_XTL))
    fold_h = jnp.where(tile_row < count - tiles, 2.0, 1.0)
    fold_v = jnp.where(along < tiles - 1, 2.0, 1.0)

    def differences(x):
        return x - from_below(x), x - from_right(x)

    def corners(diff_h, diff_v):
        return (
            (vr * diff_h, hb * diff_v),
            (vl * diff_h, -from_left(hb * diff_v)),
            (-from_above(vr * diff_h), ht * diff_v),
            (-from_above(vl * diff_h), -from_left(ht * diff_v)),
        )

    def tile_product(along_h, along_v, first, second):
        value = along_h + from_above(along_h) + along_v + from_left(along_v)
        for (ah, av), (bh, bv) in zip(first, second):
            value = value + ah * bv + av * bh
        return value

    weight, *pull = tile_sums(targets)
    flat = [e - low(e) for e in pull]
    step = [differences(d) for d in flat]
    gap = [d - up(d) for d in flat]
    norm = total(flat[0] * flat[0] + flat[1] * flat[1]) * nodes
    energy = sum(kh * h * h + kv * v * v for h, v in step)
    energy = energy + nodes * weight * (gap[0] * gap[0] + gap[1] * gap[1])
    alpha = norm / total(energy)

    for k in range(2):
        sums_ref[k] = alpha * gap[k]
    look = [jnp.zeros_like(owner), jnp.zeros_like(owner)]
    for t in range(count):
        mine = owner == float(t)
        for k in range(2):
            look[k] = jnp.where(mine, sums_ref[k, t : t + 1, :], look[k])
    weight, *pull = tile_sums([look[k] - targets[k] for k in range(2)])
    weight_low = low(weight)
    const = [
        pull[k] - low(pull[k]) - alpha * (weight * gap[k] - weight_low * low(gap[k]))
        for k in range(2)
    ]
    plain = jnp.zeros_like(kh)
    mixed = jnp.zeros_like(kh)
    quad = jnp.zeros_like(kh)
    p_energy = jnp.zeros_like(kh)
    m_energy = jnp.zeros_like(kh)
    q_energy = jnp.zeros_like(kh)
    for k in range(2):
        c = const[k]
        ch, cv = differences(c)
        h, v = step[k]
        ends = corners(h, v)
        c_ends = corners(ch, cv)
        square = tile_product(k2h * h * h, k2v * v * v, ends, ends)
        across = tile_product(
            kxh * h * up(h), kxv * v * up(v), ends, [(up(a), up(b)) for a, b in ends]
        )
        gap_square = square + up(square) - 2.0 * across
        flux_h, flux_v = kh * h, kv * v
        inner = flux_h - from_above(flux_h) + flux_v - from_left(flux_v)
        gap_c = c - up(c)
        gap_q = inner - up(inner)
        plain = plain + c * c
        mixed = mixed + c * inner
        quad = quad + square
        p_energy = p_energy + kh * ch * ch + kv * cv * cv + nodes * weight * gap_c * gap_c
        m_energy = (
            m_energy
            + tile_product(k2h * ch * h, k2v * cv * v, c_ends, ends)
            + weight * gap_c * gap_q
        )
        above_h, left_v = from_above(h), from_left(v)
        value = dh * h * h + dt * above_h * above_h + dv * v * v
        value = value + 2.0 * (
            xbr * h * v + xbl * h * left_v + xtr * above_h * v + xtl * above_h * left_v
        )
        (br_h, br_v), (bl_h, bl_v), (tr_h, tr_v), (tl_h, tl_v) = ends
        for stiff, part, extra, fold in (
            (vr, br_h, br_v - from_below(tr_v), fold_h),
            (vl, bl_h, bl_v - from_below(tl_v), fold_h),
            (hb, br_v, br_h - from_right(bl_h), fold_v),
            (ht, tr_v, tr_h - from_right(tl_h), fold_v),
        ):
            value = value + stiff * extra * (2.0 * fold * part + extra)
        q_energy = q_energy + value + weight * gap_square
    norm = nodes * total(plain) - 2.0 * alpha * total(mixed) + alpha * alpha * total(quad)
    energy = total(p_energy) - 2.0 * alpha * total(m_energy) + alpha * alpha * total(q_energy)
    beta = norm / energy

    own_figures = (*flat, *const, step[0][0], step[1][0], step[0][1], step[1][1], ht, hb, weight, weight_low)
    beside = (*const, step[0][0], step[1][0], step[0][1], step[1][1])
    wanted = [(x, me) for x in own_figures] + [(x, me + 1) for x in beside] + [(x, me - 1) for x in beside]
    for n, (x, section) in enumerate(wanted):
        out_ref[n, 0:tiles, :] = zero_tiles
        out_ref[n, tiles + count : 2 * tiles + count, :] = zero_tiles
        picked = lane_sum(jnp.where(lane == section, x, 0.0))
        out_ref[n, tiles : tiles + count, :] = jnp.broadcast_to(picked, (count, sections))

    def spread(n, shift):
        start = pl.multiple_of((group + 1 + shift) * tiles, tiles)
        return out_ref[n, pl.ds(start, tiles), :]

    wide_lane = iota((rows, TILE_W), 1)
    wide_row = iota((rows, TILE_W), 0)
    first_lane, last_lane = wide_lane == 0, wide_lane == TILE_W - 1
    first_row, last_row = wide_row == 0, wide_row == rows - 1
    line_first, line_last = first_lane[0:1], last_lane[0:1]
    inside = jnp.where(group < groups - 1, 1.0, 0.0).astype(F32)

    def image(edges, offset, k, j):
        def line(n, shift=0, at=j):
            return spread(offset + n + k, shift)[at : at + 1, :]

        value = jnp.where(last_row, edges[j : j + 1, :] * line(0), 0.0)
        value = value - jnp.where(first_row, edges[tiles + j : tiles + j + 1, :] * line(0, -1), 0.0)
        columns = edges[2 * tiles : 2 * tiles + rows, :]
        value = value + jnp.where(last_lane, columns[:, j : j + 1] * line(2), 0.0)
        if j:
            value = value - jnp.where(first_lane, columns[:, j - 1 : j] * line(2, 0, j - 1), 0.0)
        return value

    own_edges, next_edges, prev_edges = own_ref[...], next_ref[...], prev_ref[...]
    for k in range(2):
        for j in range(tiles):
            span = slice(j * TILE_W, (j + 1) * TILE_W)

            def line(n, shift, at=j):
                return spread(n + k, shift)[at : at + 1, :]

            field_ref[k, tiles : tiles + rows, span] = line(2, 0) - alpha * image(own_edges, 4, k, j)
            near = -inside * own_edges[j : j + 1, :] * line(4, 0)
            near = near + jnp.where(line_last, spread(8, 1)[j : j + 1, :] * line(6, 1), 0.0)
            far = own_edges[tiles + j : tiles + j + 1, :] * line(4, -1)
            far = far + jnp.where(line_last, spread(9, -1)[j : j + 1, :] * line(6, -1), 0.0)
            if j:
                near = near - jnp.where(line_first, spread(8, 1)[j - 1 : j, :] * line(6, 1, j - 1), 0.0)
                far = far - jnp.where(line_first, spread(9, -1)[j - 1 : j, :] * line(6, -1, j - 1), 0.0)
            field_ref[k, tiles + rows : tiles + rows + 1, span] = line(2, 1) - alpha * near
            field_ref[k, tiles - 1 : tiles, span] = line(2, -1) - alpha * far
    weight_rows, weight_low_rows = spread(10, 0), spread(11, 0)
    for k in range(2):
        flux_left = None
        for j in range(tiles):
            span = slice(j * TILE_W, (j + 1) * TILE_W)
            r = field_ref[k, tiles : tiles + rows, span]
            right = pltpu.roll(r, TILE_W - 1, 1)
            if j < tiles - 1:
                beyond = field_ref[k, tiles : tiles + rows, (j + 1) * TILE_W : (j + 2) * TILE_W]
                right = jnp.where(last_lane, pltpu.roll(beyond, TILE_W - 1, 1), right)
            else:
                right = jnp.where(last_lane, 0.0, right)
            flux = hori_ref[:, span] * (r - right)
            turned = pltpu.roll(flux, 1, 1)
            before = jnp.where(first_lane, 0.0 if flux_left is None else flux_left, turned)
            flux_left = turned
            below = field_ref[k, tiles + 1 : tiles + rows + 1, span]
            fall = vert_ref[:, span] * (r - below)
            edge = own_edges[tiles + j : tiles + j + 1, :] * (field_ref[k, tiles - 1 : tiles, span] - r[0:1, :])
            fall_above = jnp.where(first_row, edge, pltpu.roll(fall, 1, 0))
            applied = flux - before + fall - fall_above
            r_next = spread(12 + k, 0)[j : j + 1, :] - alpha * image(next_edges, 14, k, j)
            r_prev = spread(18 + k, 0)[j : j + 1, :] - alpha * image(prev_edges, 20, k, j)
            applied = applied + weight_rows[j : j + 1, :] * (r - r_next) + weight_low_rows[j : j + 1, :] * (r - r_prev)
            disp_ref[k, :, span] = alpha * spread(k, 0)[j : j + 1, :] + beta * r
            res_ref[k, :, span] = r - beta * applied


def from_behind(block, axis, distance):
    devices = range(lax.axis_size(axis))
    route = [(i - distance, i) for i in devices if i - distance in devices]
    return lax.ppermute(block, axis, route)


def gather(block, axis):
    size = lax.axis_size(axis)
    copies = jnp.broadcast_to(block[None], (size,) + block.shape)
    return lax.all_to_all(copies, axis, 0, 0, tiled=True)


def body(fixed_desc, moving_desc, offsets, owner, counts, vert, hori):
    groups = lax.axis_size("group")
    sections = lax.axis_size(SEC)
    chips_z = lax.axis_size("z")
    group = lax.axis_index("group")
    section = lax.axis_index(SEC)
    patches, flow, corr = fixed_desc.shape[1:]
    half = patches // 2
    rows, cols = vert.shape[1:]
    tiles = cols // TILE_W
    vert, hori = vert[0], hori[0]

    moving_near = from_behind(moving_desc[0, :half], SEC, -1)
    fixed_far = from_behind(fixed_desc[0, half:], SEC, 1)
    shifts = offsets[0].astype(F32).reshape(patches * 2, offsets.shape[-1])
    shifts_far = from_behind(shifts[patches:], SEC, 1)
    above = from_behind(vert[rows - 1 :], "group", 1).reshape(tiles, TILE_W)
    edge_rows = 2 * tiles + rows
    edges = pl.pallas_call(
        edge_kernel, out_shape=jax.ShapeDtypeStruct((edge_rows, TILE_W), F32), name="edges"
    )(vert, hori, above)
    edges_next = from_behind(edges, SEC, -1)
    edges_prev = from_behind(edges, SEC, 1)

    live = jnp.where(jnp.arange(patches) < counts[0, 0], owner[0], -1).astype(F32)
    owners = jnp.pad(
        live.reshape(2, half).T, ((0, 0), (COLUMN_OWNER, TILE_W - COLUMN_OWNER - 2))
    )
    table = pl.pallas_call(
        border_kernel,
        out_shape=jax.ShapeDtypeStruct((tiles, TILE_W), F32),
        in_specs=[pl.BlockSpec(memory_space=pltpu.SMEM)] + [pl.BlockSpec(memory_space=pltpu.VMEM)] * 5,
        scratch_shapes=[pltpu.VMEM((TILE_W, TILE_W), F32)],
        name="borders",
    )(jnp.stack([group, jnp.int32(groups - 1)]).astype(jnp.int32), vert, hori, edges, edges_next, owners)

    def match(column, last, fixed, moving, part, known):
        def features(x):
            if x.ndim == 4:
                which = part[0] if x is fixed else part[1]
                return pl.BlockSpec((pl.Squeezed(), half, flow, corr), lambda i, w=which: (0, w, 0, 0))
            return pl.BlockSpec((half, flow, corr), lambda i: (0, 0, 0))

        shape = (tiles * GROUP_LANES // TILE_W if last else tiles, TILE_W)

        def kernel(*refs):
            match_kernel(column, last, *refs)

        return pl.pallas_call(
            kernel,
            grid=(1,),
            out_shape=jax.ShapeDtypeStruct(shape, F32),
            in_specs=[
                features(fixed),
                features(moving),
                pl.BlockSpec((patches, offsets.shape[-1]), lambda i: (0, 0)),
                pl.BlockSpec((tiles, TILE_W), lambda i: (0, 0)),
            ],
            out_specs=pl.BlockSpec(shape, lambda i: (0, 0)),
            name="match_far" if last else "match_near",
        )(fixed, moving, shifts[:patches] if not last else shifts_far, known)

    table = match(COLUMN_NEAR, False, fixed_desc, moving_near, (0, 0), table)
    mine = match(COLUMN_FAR, True, fixed_far, moving_desc, (0, 1), table)

    seen = gather(mine, "z").reshape(-1, TILE_W)
    seen = gather(seen, ("group", "y")).reshape(-1, TILE_W)
    seen = lax.all_gather(seen, "core", axis=0, tiled=True)

    dims = (groups, sections, rows, tiles, chips_z)
    halves = tiles * GROUP_LANES // TILE_W
    count = groups * tiles

    def both_iterations(*refs):
        stack_kernel(dims, *refs)

    field = jax.ShapeDtypeStruct((2, rows, cols), F32)
    displacement, residual = pl.pallas_call(
        both_iterations,
        out_shape=(field, field),
        in_specs=[pl.BlockSpec(memory_space=pltpu.SMEM)] + [pl.BlockSpec(memory_space=pltpu.VMEM)] * 6,
        scratch_shapes=[
            pltpu.VMEM((groups * halves, sections, TILE_W), F32),
            pltpu.VMEM((groups, halves * TILE_W, sections), F32),
            pltpu.VMEM((3, count, sections), F32),
            pltpu.VMEM((24, count + 2 * tiles, sections), F32),
            pltpu.VMEM((2, rows + 2 * tiles, cols), F32),
        ],
        compiler_params=pltpu.CompilerParams(vmem_limit_bytes=32 << 20),
        name="stack",
    )(jnp.stack([section, group]).astype(jnp.int32), seen, vert, hori, edges, edges_next, edges_prev)
    return (displacement[None], residual[None])


def solution(mesh):
    groups, sections = mesh.devices.shape
    devices = mesh.devices.reshape(groups, sections // (CHIPS_Y * CORES), CHIPS_Y, CORES)
    fine = Mesh(devices, ("group",) + SEC)
    in_specs = (
        P(SEC, "group", None, None),
        P(SEC, "group", None, None),
        P(SEC, "group", None, None),
        P(SEC, "group"),
        P(SEC, "group"),
        P(SEC, "group", None),
        P(SEC, "group", None),
    )
    out_specs = (P(SEC, None, "group", None), P(SEC, None, "group", None))
    return jax.shard_map(body, mesh=fine, in_specs=in_specs, out_specs=out_specs, check_vma=False)
```

time: 351 us -> 87.4 us (0.25)
  blocking collectives: 247 us -> 26.8 us
  starting transfers between devices: 67.6 us -> 29 us
  waiting for transfers between devices: 18.9 us -> 6.36 us
  Pallas kernels: 0 us -> 12.2 us
  local copies, waits for them, and re-layouts: 5.37 us -> 9.33 us
  between operations: 4.98 us -> 1.47 us
    psum x2 -> x0, blocking collectives: 221 us -> none  [squares(): return lax.psum(jnp.sum(field * field), ('group', 'sec'))]
    ppermute x16 -> x0, starting transfers between devices: 45.8 us -> none  [the longest x8 30.8 us: with_halo(): lax.ppermute(tail, axis, [(i, (i + 1) % count) for i in range(ends)])]
    all_to_all x0 -> x1, blocking collectives: none -> 24.5 us  [gather(): return lax.all_to_all(copies, axis, 0, 0, tiled=True)]
    ppermute x16 -> x0, waiting for transfers between devices: 17.6 us -> none  [the longest x8 15.9 us: with_halo(): lax.ppermute(head, axis, [((i + 1) % count, i) for i in range(ends)])]
    pallas_call x0 -> x5, Pallas kernels: none -> 12.2 us  [the longest x2 5.43 us: match(): pl.pallas_call(kernel, grid=(1,), out_shape=jax.ShapeDtypeStruct(shape, F...]
    unnamed x2 -> x0, blocking collectives: 12.1 us -> none
    all_gather x2 -> x1, blocking collectives: 13.7 us -> 2.3 us  [body(): seen = lax.all_gather(seen, 'core', axis=0, tiled=True)]
    all_to_all x0 -> x1, starting transfers between devices: none -> 10.7 us  [gather(): return lax.all_to_all(copies, axis, 0, 0, tiled=True)]
  transfers between devices with their start and end apart: 20 -> 7, of which waited for: 10 -> 2; matrix products, arithmetic and copies ran while one was open for 2% -> 5% of each run, Pallas kernels for 0% -> 7%
where the time goes in v1:
time: 87.4 us; the launch traced here: 86.6 us
  starting transfers between devices  29 us (33%)
  blocking collectives  26.8 us (31%)
  Pallas kernels  12.2 us (14%)
  local copies, waits for them, and re-layouts  9.33 us (11%)
  waiting for transfers between devices  6.36 us (7%)
  between operations  1.47 us (2%)
  other arithmetic  1.42 us (2%)
    all_to_all x1, blocking collectives, gather(): return lax.all_to_all(copies, axis, 0, 0, tiled=True)  24.5 us
    ppermute x6, starting transfers between devices, from_behind(): return lax.ppermute(block, axis, route)  18.3 us
    all_to_all x1, starting transfers between devices, gather(): return lax.all_to_all(copies, axis, 0, 0, tiled=True)  10.7 us
    pallas_call x2, Pallas kernels, match(): pl.pallas_call(kernel, grid=(1,), out_shape=jax.ShapeDtypeStruct(shape, F...  5.43 us
    all_to_all x1, waiting for transfers between devices, gather(): return lax.all_to_all(copies, axis, 0, 0, tiled=True)  4.82 us
    unnamed x25, local copies, waits for them, and re-layouts  4.55 us
    pallas_call x1, Pallas kernels, body(): pl.pallas_call(both_iterations, out_shape=(field, field), in_specs=[pl.Bl...  3.4 us
    all_gather x1, blocking collectives, body(): seen = lax.all_gather(seen, 'core', axis=0, tiled=True)  2.3 us
  transfers between devices with their start and end apart: 7, of which 2 were waited for; matrix products, arithmetic and copies ran while one was open for 5% of the time, Pallas kernels for 7%

profile of v1, /device:TPU:1, one launch (start us, length us, event | category | flops | bytes accessed | tf_op | source)
XLA Modules:
  0.0 86.6 jit_solution(1529416172289673631)
XLA Ops:
  0.6 0.9 slice_bitcast_fusion.2
  1.5 3.9 %collective-permute-start.3 = (f32[1,1024]{1,0:T(1,128)S(1)}, f32[1,1024]{1,0:T(1,128)S(1)}, u32[]{:S(2)}, u32[]{:S(2)}) collective-permute-start(f32[1,1024]{1,0:T(1,128)S(1)} %slice_bitcast_fusion.2), channel_id=1, source_target_pairs={{0,128},{128,256},{256,384},{1,129},{129,257},{257,385},{2,130},{1... | collective-permute-start | bytes 12296 | tf_op jit(solution)/shard_map/ppermute | solution.py:478
  5.4 1.1 %slice_bitcast_fusion = bf16[8,64,512]{2,1,0:T(8,128)(2,1)S(1)} fusion(bf16[1,16,64,512]{3,2,1,0:T(8,128)(2,1)} %refs_1_.1), kind=kLoop, calls=%fused_computation | loop fusion | bytes 1048576 | tf_op jit(solution)/shard_map/squeeze | solution.py:499
  6.5 6.1 %collective-permute-start.2 = (bf16[8,64,512]{2,1,0:T(8,128)(2,1)S(1)}, bf16[8,64,512]{2,1,0:T(8,128)(2,1)S(1)}, u32[]{:S(2)}, u32[]{:S(2)}) collective-permute-start(bf16[8,64,512]{2,1,0:T(8,128)(2,1)S(1)} %slice_bitcast_fusion), channel_id=1, source_target_pairs={{1,0},{2,1},{3,2},{4,3},{5,4},{6,5},{7,6},{8,7},{9,8},{10,9},{11,1... | collective-permute-start | bytes 1572872 | tf_op jit(solution)/shard_map/ppermute | solution.py:478
  12.7 1.9 %collective-permute-start = (bf16[8,64,512]{2,1,0:T(8,128)(2,1)S(1)}, bf16[8,64,512]{2,1,0:T(8,128)(2,1)S(1)}, u32[]{:S(2)}, u32[]{:S(2)}) collective-permute-start(bf16[8,64,512]{2,1,0:T(8,128)(2,1)S(1)} %slice_bitcast_fusion.1), channel_id=1, source_target_pairs={{0,1},{1,2},{2,3},{3,4},{4,5},{5,6},{6,7},{7,8},{8,9},{9,10},{10,1... | collective-permute-start | bytes 1572872 | tf_op jit(solution)/shard_map/ppermute | solution.py:478
  15.3 2.0 %collective-permute-start.1 = (f32[16,64]{1,0:T(8,128)S(1)}, f32[16,64]{1,0:T(8,128)S(1)}, u32[]{:S(2)}, u32[]{:S(2)}) collective-permute-start(f32[16,64]{1,0:T(8,128)S(1)} %bitcast.30), channel_id=1, source_target_pairs={{0,1},{1,2},{2,3},{3,4},{4,5},{5,6},{6,7},{7,8},{8,9},{9,10},{10,1... | collective-permute-start | bytes 12296 | tf_op jit(solution)/shard_map/ppermute | solution.py:478
  20.0 1.6 %edges.1.own_ref.refs_4_ = f32[32,128]{1,0:T(8,128)} custom-call(f32[16,1024]{1,0:T(8,128)} %bitcast.21, f32[16,1024]{1,0:T(8,128)} %bitcast.24, f32[8,128]{1,0:T(8,128)} %bitcast.31), custom_call_target="tpu_custom_call" | custom-call | tf_op jit(solution)/shard_map/edges/pallas_call | solution.py:505
  21.5 2.4 %collective-permute-start.4 = (f32[32,128]{1,0:T(8,128)}, f32[32,128]{1,0:T(8,128)S(1)}, u32[]{:S(2)}, u32[]{:S(2)}) collective-permute-start(f32[32,128]{1,0:T(8,128)} %edges.1.own_ref.refs_4_), channel_id=1, source_target_pairs={{1,0},{2,1},{3,2},{4,3},{5,4},{6,5},{7,6},{8,7},{9,8},{10,9},{11,1... | collective-permute-start | bytes 49160 | tf_op jit(solution)/shard_map/ppermute | solution.py:478
  23.9 0.7 pad_add_fusion.1.group_ref
  24.6 0.7 pad.4.owner_ref
  25.3 1.5 %collective-permute-done.4.next_ref.refs_5_ = f32[32,128]{1,0:T(8,128)S(1)} collective-permute-done((f32[32,128]{1,0:T(8,128)}, f32[32,128]{1,0:T(8,128)S(1)}, u32[]{:S(2)}, u32[]{:S(2)}) %collective-permute-start.4) | collective-permute-done | bytes 16416 | tf_op jit(solution)/shard_map/ppermute | solution.py:478
  27.4 1.8 %borders.1.refs_3_ = f32[8,128]{1,0:T(8,128)} custom-call(s32[2]{0:T(128)} %pad_add_fusion.1.group_ref, f32[16,1024]{1,0:T(8,128)} %bitcast.22, f32[16,1024]{1,0:T(8,128)} %bitcast.25, f32[32,128]{1,0:T(8,128)} %edges.1.own_ref.refs_4_, f32[32,128]{1,0:T(8,128)} %copy-done.3, f32[8,128]{1,0:T(8,128)} %pad.4.owner_ref), custom_call_target="tpu_custom_call" | custom-call | tf_op jit(solution)/shard_map/borders/pallas_call | solution.py:515
  29.2 0.8 copy-done.6
  30.0 2.7 %match_near.1.refs_3_ = f32[8,128]{1,0:T(8,128)} custom-call(bf16[1,16,64,512]{3,2,1,0:T(8,128)(2,1)} %refs_0_.1, bf16[8,64,512]{2,1,0:T(8,128)(2,1)} %copy-done.6, f32[16,64]{1,0:T(8,128)} %bitcast.29, f32[8,128]{1,0:T(8,128)} %borders.1.refs_3_), custom_call_target="tpu_custom_call" | custom-call | tf_op jit(solution)/shard_map/match_near/pallas_call | solution.py:535
  33.3 0.8 copy-done.7
  34.1 2.7 %match_far.1 = f32[2,128]{1,0:T(2,128)} custom-call(bf16[8,64,512]{2,1,0:T(8,128)(2,1)} %copy-done.7, bf16[1,16,64,512]{3,2,1,0:T(8,128)(2,1)} %refs_1_.1, f32[16,64]{1,0:T(8,128)} %copy-done.9, f32[8,128]{1,0:T(8,128)} %match_near.1.refs_3_), custom_call_target="tpu_custom_call" | custom-call | tf_op jit(solution)/shard_map/match_far/pallas_call | solution.py:535
  36.9 0.7 broadcast_in_dim.24
  37.5 24.5 %all_to_all.10 = f32[16,2,128]{2,1,0:T(2,128)S(1)} all-to-all(f32[16,2,128]{2,1,0:T(2,128)S(1)} %broadcast_in_dim.24), channel_id=1, replica_groups=mesh['group'=4,'z'=16,'y'=4,'core'=2] {'z'}, dimensions={0} | all-to-all | bytes 32768 | tf_op jit(solution)/shard_map/all_to_all | solution.py:484
  62.0 0.7 broadcast_in_dim.26
  62.7 10.7 %all-to-all-start.1 = ((f32[16,32,128]{2,1,0:T(8,128)}), f32[16,32,128]{2,1,0:T(8,128)S(1)}, u32[]{:S(2)}, u32[]{:S(2)}) async-start(f32[16,32,128]{2,1,0:T(8,128)} %broadcast_in_dim.26), calls=%async_computation.1 | async-start | bytes 524288 | tf_op jit(solution)/shard_map/all_to_all | solution.py:484
  74.2 1.9 %collective-permute-start.5 = (f32[32,128]{1,0:T(8,128)S(1)}, f32[32,128]{1,0:T(8,128)S(1)}, u32[]{:S(2)}, u32[]{:S(2)}) collective-permute-start(f32[32,128]{1,0:T(8,128)S(1)} %copy-done.2), channel_id=1, source_target_pairs={{0,1},{1,2},{2,3},{3,4},{4,5},{5,6},{6,7},{7,8},{8,9},{9,10},{10,1... | collective-permute-start | bytes 49160 | tf_op jit(solution)/shard_map/ppermute | solution.py:478
  76.1 4.8 %all-to-all-done.1 = f32[16,32,128]{2,1,0:T(8,128)S(1)} async-done(((f32[16,32,128]{2,1,0:T(8,128)}), f32[16,32,128]{2,1,0:T(8,128)S(1)}, u32[]{:S(2)}, u32[]{:S(2)}) %all-to-all-start.1) | async-done | bytes 262176 | tf_op jit(solution)/shard_map/all_to_all | solution.py:484
  80.9 2.3 %all_gather.3.refs_1_ = f32[1024,128]{1,0:T(8,128)S(1)} all-gather(f32[512,128]{1,0:T(8,128)S(1)} %bitcast.27), channel_id=1, replica_groups=mesh['group'=4,'z'=16,'y'=4,'core'=2] {'core'}, dimensions={0}, use_global_device_ids=true | all-gather | bytes 786432 | tf_op jit(solution)/shard_map/all_gather | solution.py:554
  83.2 3.4 %stack.18 = (f32[2,16,1024]{2,1,0:T(8,128)}, f32[2,16,1024]{2,1,0:T(8,128)}) custom-call(s32[2]{0:T(128)S(1)} %pad_add_fusion.refs_0_, f32[1024,128]{1,0:T(8,128)S(1)} %all_gather.3.refs_1_, f32[16,1024]{1,0:T(8,128)S(1)} %bitcast.23, f32[16,1024]{1,0:T(8,128)S(1)} %bitcast.26, f32[32,128]{1,0:T(8,128)S(1)} %copy-done.2, f32[32,128]{1,0:T(8,128)S(1)} %copy-done.4, ...), custom_call_target="tpu_custom_call" | custom-call | tf_op jit(solution)/shard_map/stack/pallas_call | solution.py:564
  (36 shorter events, 4.5 us)
Async XLA Ops:
  0.6 12.1 %copy-start.5 = (bf16[1,16,64,512]{3,2,1,0:T(8,128)(2,1)S(1)}, bf16[1,16,64,512]{3,2,1,0:T(8,128)(2,1)}, u32[]{:S(2)}) copy-start(bf16[1,16,64,512]{3,2,1,0:T(8,128)(2,1)} %refs_0_.1) | copy-start | bytes 3145732
  1.5 17.9 %collective-permute-start.3 = (f32[1,1024]{1,0:T(1,128)S(1)}, f32[1,1024]{1,0:T(1,128)S(1)}, u32[]{:S(2)}, u32[]{:S(2)}) collective-permute-start(f32[1,1024]{1,0:T(1,128)S(1)} %slice_bitcast_fusion.2), channel_id=1, source_target_pairs={{0,128},{128,256},{256,384},{1,129},{129,257},{257,385},{2,130},{1... | collective-permute-start | bytes 12296 | tf_op jit(solution)/shard_map/ppermute | solution.py:478
  6.5 8.1 %copy-start.8 = (s32[1,16,2,64]{3,2,1,0:T(2,128)S(1)}, s32[1,16,2,64]{3,2,1,0:T(2,128)}, u32[]{:S(2)}) copy-start(s32[1,16,2,64]{3,2,1,0:T(2,128)} %param.9) | copy-start | bytes 24580
  6.5 22.7 %collective-permute-start.2 = (bf16[8,64,512]{2,1,0:T(8,128)(2,1)S(1)}, bf16[8,64,512]{2,1,0:T(8,128)(2,1)S(1)}, u32[]{:S(2)}, u32[]{:S(2)}) collective-permute-start(bf16[8,64,512]{2,1,0:T(8,128)(2,1)S(1)} %slice_bitcast_fusion), channel_id=1, source_target_pairs={{1,0},{2,1},{3,2},{4,3},{5,4},{6,5},{7,6},{8,7},{9,8},{10,9},{11,1... | collective-permute-start | bytes 1572872 | tf_op jit(solution)/shard_map/ppermute | solution.py:478
  12.7 20.0 %collective-permute-start = (bf16[8,64,512]{2,1,0:T(8,128)(2,1)S(1)}, bf16[8,64,512]{2,1,0:T(8,128)(2,1)S(1)}, u32[]{:S(2)}, u32[]{:S(2)}) collective-permute-start(bf16[8,64,512]{2,1,0:T(8,128)(2,1)S(1)} %slice_bitcast_fusion.1), channel_id=1, source_target_pairs={{0,1},{1,2},{2,3},{3,4},{4,5},{5,6},{6,7},{7,8},{8,9},{9,10},{10,1... | collective-permute-start | bytes 1572872 | tf_op jit(solution)/shard_map/ppermute | solution.py:478
  15.3 2.6 %copy-start.11 = (s32[1,16]{1,0:T(1,128)S(1)}, s32[1,16]{1,0:T(1,128)}, u32[]{:S(2)}) copy-start(s32[1,16]{1,0:T(1,128)} %param.10) | copy-start | bytes 196
  15.3 17.4 %collective-permute-start.1 = (f32[16,64]{1,0:T(8,128)S(1)}, f32[16,64]{1,0:T(8,128)S(1)}, u32[]{:S(2)}, u32[]{:S(2)}) collective-permute-start(f32[16,64]{1,0:T(8,128)S(1)} %bitcast.30), channel_id=1, source_target_pairs={{0,1},{1,2},{2,3},{3,4},{4,5},{5,6},{6,7},{7,8},{8,9},{9,10},{10,1... | collective-permute-start | bytes 12296 | tf_op jit(solution)/shard_map/ppermute | solution.py:478
  19.4 0.6 copy-start.10
  21.5 5.3 %collective-permute-start.4 = (f32[32,128]{1,0:T(8,128)}, f32[32,128]{1,0:T(8,128)S(1)}, u32[]{:S(2)}, u32[]{:S(2)}) collective-permute-start(f32[32,128]{1,0:T(8,128)} %edges.1.own_ref.refs_4_), channel_id=1, source_target_pairs={{1,0},{2,1},{3,2},{4,3},{5,4},{6,5},{7,6},{8,7},{9,8},{10,9},{11,1... | collective-permute-start | bytes 49160 | tf_op jit(solution)/shard_map/ppermute | solution.py:478
  26.8 0.6 copy-start.3
  29.2 0.8 copy-start.6
  32.7 0.6 copy-start.9
  33.3 0.8 copy-start.7
  62.7 18.2 %all-to-all-start.1 = ((f32[16,32,128]{2,1,0:T(8,128)}), f32[16,32,128]{2,1,0:T(8,128)S(1)}, u32[]{:S(2)}, u32[]{:S(2)}) async-start(f32[16,32,128]{2,1,0:T(8,128)} %broadcast_in_dim.26), calls=%async_computation.1 | async-start | bytes 524288 | tf_op jit(solution)/shard_map/all_to_all | solution.py:484
  73.5 0.7 copy-start.2
  74.2 9.0 %collective-permute-start.5 = (f32[32,128]{1,0:T(8,128)S(1)}, f32[32,128]{1,0:T(8,128)S(1)}, u32[]{:S(2)}, u32[]{:S(2)}) collective-permute-start(f32[32,128]{1,0:T(8,128)S(1)} %copy-done.2), channel_id=1, source_target_pairs={{0,1},{1,2},{2,3},{3,4},{4,5},{5,6},{6,7},{7,8},{8,9},{9,10},{10,1... | collective-permute-start | bytes 49160 | tf_op jit(solution)/shard_map/ppermute | solution.py:478
  80.9 2.3 %copy-start = (f32[1,16,1024]{2,1,0:T(8,128)S(1)}, f32[1,16,1024]{2,1,0:T(8,128)}, u32[]{:S(2)}) copy-start(f32[1,16,1024]{2,1,0:T(8,128)} %param.12) | copy-start | bytes 196612
  80.9 2.3 %copy-start.1 = (f32[1,16,1024]{2,1,0:T(8,128)S(1)}, f32[1,16,1024]{2,1,0:T(8,128)}, u32[]{:S(2)}) copy-start(f32[1,16,1024]{2,1,0:T(8,128)} %param.13) | copy-start | bytes 196612
  80.9 2.3 %copy-start.4 = (f32[32,128]{1,0:T(8,128)S(1)}, f32[32,128]{1,0:T(8,128)}, u32[]{:S(2)}) copy-start(f32[32,128]{1,0:T(8,128)} %copy-done.3) | copy-start | bytes 49156

commit v2 on v1

--- a/solution.py
+++ b/solution.py
@@ -21,6 +21,7 @@
 COLUMN_NEAR = 19
 COLUMN_FAR = 21
 GROUP_LANES = 32
+PARTS = 4
 
 
 def iota(shape, axis):
@@ -39,27 +40,81 @@
     return lane_sum(row_sum(x))
 
 
-def edge_kernel(vert_ref, hori_ref, above_ref, out_ref):
+def three_parts(x):
+    high = x.astype(jnp.bfloat16).astype(F32)
+    middle = (x - high).astype(jnp.bfloat16).astype(F32)
+    return high, middle, x - high - middle
+
+
+def pack_kernel(
+    moving_ref, fixed_ref, vert_ref, hori_ref, offsets_ref, near_ref, far_ref, line_ref,
+    vert, hori, offsets, extra, sems,
+):
+    rows, cols = hori.shape
+    tiles = cols // TILE_W
+    length = moving_ref.shape[0] // 2
+    part = length // PARTS
+    copies = []
+    for n in range(PARTS):
+        at = pl.ds(n * part, part)
+        copies.append(pltpu.make_async_copy(moving_ref.at[at], near_ref.at[at], sems.at[2 * n]))
+        behind = pl.ds(length + n * part, part)
+        copies.append(pltpu.make_async_copy(fixed_ref.at[behind], far_ref.at[at], sems.at[2 * n + 1]))
+    first = 2 * PARTS
+    loads = [
+        pltpu.make_async_copy(vert_ref.at[0], vert, sems.at[first]),
+        pltpu.make_async_copy(hori_ref.at[0], hori, sems.at[first + 1]),
+        pltpu.make_async_copy(offsets_ref.at[0], offsets, sems.at[first + 2]),
+    ]
+    for copy in copies + loads:
+        copy.start()
+    for copy in loads:
+        copy.wait()
+    lane = iota((rows, TILE_W), 1)
+    column = jnp.zeros((rows, TILE_W), F32)
+    for j in range(tiles):
+        span = slice(j * TILE_W, (j + 1) * TILE_W)
+        line_ref[j : j + 1, :] = vert[rows - 1 : rows, span]
+        end = (j + 1) * TILE_W - 1
+        column = jnp.where(lane == j, hori[:, end : end + 1], column)
+    high, middle, small = three_parts(column)
+    columns = high + pltpu.roll(middle, tiles, 1) + pltpu.roll(small, 2 * tiles, 1)
+    half = offsets.shape[0] // 2
+    shifts = jnp.concatenate([offsets[half:, 0, :], offsets[half:, 1, :]], 1).astype(F32)
+    blank = jnp.zeros((tiles, TILE_W), F32)
+    for n, value in enumerate(three_parts(line_ref[...])):
+        span = slice(n * TILE_W, (n + 1) * TILE_W)
+        extra[0, :, span] = jnp.concatenate([value, blank], 0).astype(jnp.bfloat16)
+        extra[1, :, span] = jnp.concatenate([value, blank if n else shifts], 0).astype(jnp.bfloat16)
+    for n in range(2):
+        extra[n, :, 3 * TILE_W :] = columns.astype(jnp.bfloat16)
+    tail = [
+        pltpu.make_async_copy(extra.at[n], ref.at[pl.ds(length, rows)], sems.at[first + 3 + n])
+        for n, ref in enumerate((near_ref, far_ref))
+    ]
+    for copy in tail:
+        copy.start()
+    for copy in copies + tail:
+        copy.wait()
+
+
+def unpack(extra, tiles):
+    parts = [extra[:, n * TILE_W : (n + 1) * TILE_W].astype(F32) for n in range(4)]
+    line = parts[0][:tiles] + (parts[1][:tiles] + parts[2][:tiles])
+    columns = parts[3]
+    back = TILE_W - tiles
+    columns = columns + (pltpu.roll(columns, back, 1) + pltpu.roll(columns, back - tiles, 1))
+    return line, columns, parts[0][tiles:]
+
+
+def border_kernel(groups, owner_ref, counts_ref, vert_ref, hori_ref, line_ref, above_ref, out_ref, stack):
     rows, cols = hori_ref.shape
     tiles = cols // TILE_W
-    lane = iota((rows, TILE_W), 1)
-    last = jnp.zeros((rows, TILE_W), F32)
-    for j in range(tiles):
-        out_ref[j : j + 1, :] = vert_ref[rows - 1 : rows, j * TILE_W : (j + 1) * TILE_W]
-        column = hori_ref[:, (j + 1) * TILE_W - 1 : (j + 1) * TILE_W]
-        last = jnp.where(lane == j, column, last)
-    out_ref[tiles : 2 * tiles, :] = above_ref[...]
-    out_ref[2 * tiles : 2 * tiles + rows, :] = last
-
-
-def border_kernel(group_ref, vert_ref, hori_ref, own_ref, next_ref, owner_ref, out_ref, stack):
-    rows, cols = hori_ref.shape
-    tiles = cols // TILE_W
-    last_group = group_ref[0] == group_ref[1]
+    last_group = lax.axis_index("group") == groups - 1
     bottom = jnp.where(last_group, 1.0, 4.0).astype(F32)
 
-    v_last = own_ref[0:tiles, :]
-    v_above = own_ref[tiles : 2 * tiles, :]
+    v_last = line_ref[...]
+    v_above = above_ref[...]
     for j in range(tiles):
         span = slice(j * TILE_W, (j + 1) * TILE_W)
         stack[j : j + 1, :] = vert_ref[rows - 2 : rows - 1, span]
@@ -81,11 +136,15 @@
     dt = lane_sum(
         v_first * v_above * v_above + jnp.where(inside, h_first * step_above * step_above, 0.0)
     )
-    table = owner_ref[...]
+    sub = iota((tiles, TILE_W), 0)
+    table = jnp.zeros((tiles, TILE_W), F32)
+    for p in range(owner_ref.shape[1]):
+        live = jnp.where(p < counts_ref[0, 0], owner_ref[0, p], -1).astype(F32)
+        spot = (sub == p % tiles) & (lane == COLUMN_OWNER + p // tiles)
+        table = jnp.where(spot, live, table)
     for column, value in (
         (COLUMN_KH, lane_sum(v_last)),
         (COLUMN_K2H, lane_sum(square)),
-        (COLUMN_KXH, lane_sum(v_last * next_ref[0:tiles, :])),
         (COLUMN_DH, dh),
         (COLUMN_DT, dt),
     ):
@@ -95,6 +154,7 @@
     zero = jnp.zeros((rows, TILE_W), F32)
     picked = {}
     for name, ref, column in (
+        ("h127", hori_ref, TILE_W - 1),
         ("h0", hori_ref, 0),
         ("h126", hori_ref, TILE_W - 2),
         ("v0", vert_ref, 0),
@@ -115,7 +175,7 @@
 
     a0, a1 = above_at(0), above_at(1)
     a126, a127 = above_at(TILE_W - 2), above_at(TILE_W - 1)
-    right = own_ref[2 * tiles : 2 * tiles + rows, :]
+    right = picked["h127"]
     left = pltpu.roll(right, 1, 1)
     row = iota((rows, TILE_W), 0)
     within = row < rows - 1
@@ -152,12 +212,10 @@
         + at(v127, 0) * a127 * (at(right, 0) - at(right, 1))
     )
     xtl = at(h0, 0) * (a0 - a1) * at(left, 0) + at(v0, 0) * a0 * (at(left, 0) - at(left, 1))
-    next_right = next_ref[2 * tiles : 2 * tiles + rows, :]
     stack[...] = jnp.zeros_like(stack)
     for column, value in (
         (COLUMN_KV, row_sum(right)),
         (COLUMN_K2V, row_sum(right_sq)),
-        (COLUMN_KXV, row_sum(right * next_right)),
         (COLUMN_VL, at(v0, end)),
         (COLUMN_VR, at(v127, end)),
         (COLUMN_HT, at(right, 0)),
@@ -173,57 +231,104 @@
     out_ref[...] = jnp.where(lane <= COLUMN_XTL, turned, table)
 
 
-def match_kernel(column, last, fixed_ref, moving_ref, offsets_ref, table_ref, out_ref):
-    patches, flow, corr = fixed_ref.shape[-3:]
-    fixed = fixed_ref.reshape(patches * flow, corr)
-    moving = moving_ref.reshape(patches * flow, corr)
+def match_kernel(
+    fixed_ref, moving_ref, offsets_ref, table_ref, line_ref, hori_ref, near_ref, far_ref,
+    out_ref, next_line_ref, next_columns_ref, prev_line_ref, prev_columns_ref,
+    near, far, scores_ref, sems,
+):
+    patches, flow, corr = fixed_ref.shape[1:]
+    half = patches // 2
+    length = half * flow
+    part = length // PARTS
+    rows, cols = hori_ref.shape[-2:]
+    tiles = cols // TILE_W
     pair = 2 * flow
-    lane = iota((flow, pair), 1)
-    lower = lane < flow
+    arrivals = [
+        pltpu.make_async_copy(near_ref.at[pl.ds(length, rows)], near.at[pl.ds(length, rows)], sems.at[2 * PARTS]),
+        pltpu.make_async_copy(far_ref.at[pl.ds(length, rows)], far.at[pl.ds(length, rows)], sems.at[2 * PARTS + 1]),
+    ]
+    loads = []
+    for side, (source, target) in enumerate(((near_ref, near), (far_ref, far))):
+        for n in range(PARTS):
+            at = pl.ds(n * part, part)
+            loads.append(pltpu.make_async_copy(source.at[at], target.at[at], sems.at[side * PARTS + n]))
+    for copy in loads + arrivals:
+        copy.start()
+
+    lower = iota((flow, pair), 1) < flow
+    for side in range(2):
+        for n in range(PARTS):
+            loads[side * PARTS + n].wait()
+            for first in range(n * half // PARTS, (n + 1) * half // PARTS, 2):
+                at = slice(first * flow, (first + 2) * flow)
+                if side == 0:
+                    fixed = fixed_ref[0, first : first + 2].reshape(pair, corr)
+                    moving = near[at, :]
+                else:
+                    fixed = far[at, :]
+                    moving = moving_ref[0, half + first : half + first + 2].reshape(pair, corr)
+                scores = lax.dot_general(
+                    moving, fixed, (((1,), (1,)), ((), ())), preferred_element_type=F32
+                )
+                both = jnp.where(lower, scores[0:flow, :], scores[flow:pair, :])
+                scores_ref[side, :, at] = both
+    for copy in arrivals:
+        copy.wait()
+    next_line, next_columns, _ = unpack(near[length : length + rows, :], tiles)
+    prev_line, prev_columns, shifts = unpack(far[length : length + rows, :], tiles)
+    next_line_ref[...] = next_line
+    next_columns_ref[...] = next_columns
+    prev_line_ref[...] = prev_line
+    prev_columns_ref[...] = prev_columns
+
+    table = table_ref[...]
+    lane = iota(table.shape, 1)
+    own_shifts = [offsets_ref[0, 0:half, k, :].astype(F32) for k in range(2)]
+    far_shifts = [shifts[:, 0:flow], shifts[:, flow:pair]]
     scale = 1.0 / math.sqrt(corr)
-    shifts = offsets_ref[...]
-    table = table_ref[...]
-    spot_row = iota(table.shape, 0)
-    spot_lane = iota(table.shape, 1)
-    for first in range(0, patches, 2):
-        at = slice(first * flow, (first + 2) * flow)
-        scores = lax.dot_general(
-            moving[at, :], fixed[at, :], (((1,), (1,)), ((), ())), preferred_element_type=F32
-        )
-        both = jnp.where(lower, scores[0:flow, :], scores[flow:pair, :])
+    slot = lax.rem(iota((2 * half, length), 0), half)
+    mine = slot == lax.div(iota((2 * half, length), 1), flow)
+    for side, offsets in enumerate((own_shifts, far_shifts)):
+        both = scores_ref[side]
         top = jnp.max(both, axis=0, keepdims=True)
         likely = jnp.exp((both - top) * scale)
         sums = lax.dot_general(
-            shifts,
+            jnp.concatenate(offsets, 0),
             likely,
             (((1,), (0,)), ((), ())),
             precision=lax.Precision.HIGHEST,
             preferred_element_type=F32,
         )
         weight = row_sum(likely)
-        ratio = sums / (weight * flow)
-        for half in range(2):
-            keep = (iota((1, pair), 1) < flow) == (half == 0)
-            for k in range(2):
-                where = 2 * (first + half) + k
-                value = lane_sum(jnp.where(keep, ratio[where : where + 1, :], 0.0))
-                spot = (spot_row == first + half) & (spot_lane == column + k)
-                table = jnp.where(spot, value, table)
-    if not last:
-        out_ref[...] = table
-        return
+        ratio = lane_sum(jnp.where(mine, sums, 0.0) / (weight * flow))
+        for k in range(2):
+            column = (COLUMN_FAR if side else COLUMN_NEAR) + k
+            table = jnp.where(lane == column, ratio[k * half : (k + 1) * half], table)
+
+    table = jnp.where(lane == COLUMN_KXH, lane_sum(line_ref[...] * next_line), table)
+    diagonal = iota(table.shape, 0) == lane
+    columns = jnp.zeros((rows, TILE_W), F32)
+    tall = iota((rows, TILE_W), 1)
+    for j in range(tiles):
+        end = (j + 1) * TILE_W - 1
+        columns = jnp.where(tall == j, hori_ref[:, end : end + 1], columns)
+    across = row_sum(columns * next_columns)
+    table = jnp.where(lane == COLUMN_KXV, lane_sum(jnp.where(diagonal, across, 0.0)), table)
+
+    table = jnp.where(lane < GROUP_LANES, table, 0.0)
     per_row = TILE_W // GROUP_LANES
-    table = jnp.where(spot_lane < GROUP_LANES, table, 0.0)
-    for half in range(table.shape[0] // per_row):
+    for part in range(tiles // per_row):
         line = jnp.zeros((1, TILE_W), F32)
         for j in range(per_row):
-            source = table[half * per_row + j : half * per_row + j + 1, :]
+            source = table[part * per_row + j : part * per_row + j + 1, :]
             line = line + (pltpu.roll(source, j * GROUP_LANES, 1) if j else source)
-        out_ref[half : half + 1, :] = line
+        for n in range(out_ref.shape[0]):
+            out_ref[n, part : part + 1, :] = line
 
 
 def stack_kernel(
-    dims, place_ref, seen_ref, vert_ref, hori_ref, own_ref, next_ref, prev_ref,
+    dims, seen_ref, vert_ref, hori_ref, own_line_ref, own_above_ref,
+    next_line_ref, next_above_ref, next_columns_ref, prev_line_ref, prev_above_ref, prev_columns_ref,
     disp_ref, res_ref, rows_ref, turn_ref, sums_ref, out_ref, field_ref,
 ):
     groups, sections, rows, tiles, chips_z = dims
@@ -231,7 +336,7 @@
     halves = tiles * GROUP_LANES // TILE_W
     count = groups * tiles
     nodes = float(rows * TILE_W)
-    me, group = place_ref[0], place_ref[1]
+    me, group = lax.axis_index(SEC), lax.axis_index("group")
 
     for core in range(CORES):
         for g in range(groups):
@@ -415,18 +520,22 @@
     inside = jnp.where(group < groups - 1, 1.0, 0.0).astype(F32)
 
     def image(edges, offset, k, j):
+        last_line, above_line, columns = edges
         def line(n, shift=0, at=j):
             return spread(offset + n + k, shift)[at : at + 1, :]
 
-        value = jnp.where(last_row, edges[j : j + 1, :] * line(0), 0.0)
-        value = value - jnp.where(first_row, edges[tiles + j : tiles + j + 1, :] * line(0, -1), 0.0)
-        columns = edges[2 * tiles : 2 * tiles + rows, :]
-        value = value + jnp.where(last_lane, columns[:, j : j + 1] * line(2), 0.0)
+        value = jnp.where(last_row, last_line[j : j + 1, :] * line(0), 0.0)
+        value = value - jnp.where(first_row, above_line[j : j + 1, :] * line(0, -1), 0.0)
+        value = value + jnp.where(last_lane, columns(j) * line(2), 0.0)
         if j:
-            value = value - jnp.where(first_lane, columns[:, j - 1 : j] * line(2, 0, j - 1), 0.0)
+            value = value - jnp.where(first_lane, columns(j - 1) * line(2, 0, j - 1), 0.0)
         return value
 
-    own_edges, next_edges, prev_edges = own_ref[...], next_ref[...], prev_ref[...]
+    own_line, own_above = own_line_ref[...], own_above_ref[...]
+    next_columns, prev_columns = next_columns_ref[...], prev_columns_ref[...]
+    own_edges = (own_line, own_above, lambda j: hori_ref[:, (j + 1) * TILE_W - 1 : (j + 1) * TILE_W])
+    next_edges = (next_line_ref[...], next_above_ref[...], lambda j: next_columns[:, j : j + 1])
+    prev_edges = (prev_line_ref[...], prev_above_ref[...], lambda j: prev_columns[:, j : j + 1])
     for k in range(2):
         for j in range(tiles):
             span = slice(j * TILE_W, (j + 1) * TILE_W)
@@ -435,9 +544,9 @@
                 return spread(n + k, shift)[at : at + 1, :]
 
             field_ref[k, tiles : tiles + rows, span] = line(2, 0) - alpha * image(own_edges, 4, k, j)
-            near = -inside * own_edges[j : j + 1, :] * line(4, 0)
+            near = -inside * own_line[j : j + 1, :] * line(4, 0)
             near = near + jnp.where(line_last, spread(8, 1)[j : j + 1, :] * line(6, 1), 0.0)
-            far = own_edges[tiles + j : tiles + j + 1, :] * line(4, -1)
+            far = own_above[j : j + 1, :] * line(4, -1)
             far = far + jnp.where(line_last, spread(9, -1)[j : j + 1, :] * line(6, -1), 0.0)
             if j:
                 near = near - jnp.where(line_first, spread(8, 1)[j - 1 : j, :] * line(6, 1, j - 1), 0.0)
@@ -462,7 +571,7 @@
             flux_left = turned
             below = field_ref[k, tiles + 1 : tiles + rows + 1, span]
             fall = vert_ref[:, span] * (r - below)
-            edge = own_edges[tiles + j : tiles + j + 1, :] * (field_ref[k, tiles - 1 : tiles, span] - r[0:1, :])
+            edge = own_above[j : j + 1, :] * (field_ref[k, tiles - 1 : tiles, span] - r[0:1, :])
             fall_above = jnp.where(first_row, edge, pltpu.roll(fall, 1, 0))
             applied = flux - before + fall - fall_above
             r_next = spread(12 + k, 0)[j : j + 1, :] - alpha * image(next_edges, 14, k, j)
@@ -478,6 +587,17 @@
     return lax.ppermute(block, axis, route)
 
 
+def from_above(block, distance):
+    groups, sections = lax.axis_size("group"), lax.axis_size(SEC)
+    route = [
+        ((g - 1) * sections + s - distance, g * sections + s)
+        for g in range(1, groups)
+        for s in range(sections)
+        if 0 <= s - distance < sections
+    ]
+    return lax.ppermute(block, ("group",) + SEC, route)
+
+
 def gather(block, axis):
     size = lax.axis_size(axis)
     copies = jnp.broadcast_to(block[None], (size,) + block.shape)
@@ -488,73 +608,74 @@
     groups = lax.axis_size("group")
     sections = lax.axis_size(SEC)
     chips_z = lax.axis_size("z")
-    group = lax.axis_index("group")
-    section = lax.axis_index(SEC)
     patches, flow, corr = fixed_desc.shape[1:]
-    half = patches // 2
     rows, cols = vert.shape[1:]
     tiles = cols // TILE_W
+    length = patches * flow
+    halves = tiles * GROUP_LANES // TILE_W
+
+    anywhere = pl.BlockSpec(memory_space=pl.ANY)
+    hbm = pl.BlockSpec(memory_space=pltpu.HBM)
+    local = pl.BlockSpec(memory_space=pltpu.VMEM)
+    scalars = pl.BlockSpec(memory_space=pltpu.SMEM)
+    packed = jax.ShapeDtypeStruct((length // 2 + rows, corr), fixed_desc.dtype)
+    border = jax.ShapeDtypeStruct((tiles, TILE_W), F32)
+    upright = jax.ShapeDtypeStruct((rows, TILE_W), F32)
+    near, far, line = pl.pallas_call(
+        pack_kernel,
+        out_shape=(packed, packed, border),
+        in_specs=[hbm] * 5,
+        out_specs=(anywhere, anywhere, local),
+        scratch_shapes=[
+            pltpu.VMEM((rows, cols), F32),
+            pltpu.VMEM((rows, cols), F32),
+            pltpu.VMEM(offsets.shape[1:], jnp.int32),
+            pltpu.VMEM((2, rows, corr), fixed_desc.dtype),
+            pltpu.SemaphoreType.DMA((2 * PARTS + 5,)),
+        ],
+        name="pack",
+    )(moving_desc.reshape(length, corr), fixed_desc.reshape(length, corr), vert, hori, offsets)
+    near = from_behind(near, SEC, -1)
+    far = from_behind(far, SEC, 1)
+    above = from_above(line, 0)
+    next_above = from_above(line, -1)
+    prev_above = from_above(line, 1)
+
     vert, hori = vert[0], hori[0]
 
-    moving_near = from_behind(moving_desc[0, :half], SEC, -1)
-    fixed_far = from_behind(fixed_desc[0, half:], SEC, 1)
-    shifts = offsets[0].astype(F32).reshape(patches * 2, offsets.shape[-1])
-    shifts_far = from_behind(shifts[patches:], SEC, 1)
-    above = from_behind(vert[rows - 1 :], "group", 1).reshape(tiles, TILE_W)
-    edge_rows = 2 * tiles + rows
-    edges = pl.pallas_call(
-        edge_kernel, out_shape=jax.ShapeDtypeStruct((edge_rows, TILE_W), F32), name="edges"
-    )(vert, hori, above)
-    edges_next = from_behind(edges, SEC, -1)
-    edges_prev = from_behind(edges, SEC, 1)
-
-    live = jnp.where(jnp.arange(patches) < counts[0, 0], owner[0], -1).astype(F32)
-    owners = jnp.pad(
-        live.reshape(2, half).T, ((0, 0), (COLUMN_OWNER, TILE_W - COLUMN_OWNER - 2))
-    )
+    def borders(*refs):
+        border_kernel(groups, *refs)
+
     table = pl.pallas_call(
-        border_kernel,
-        out_shape=jax.ShapeDtypeStruct((tiles, TILE_W), F32),
-        in_specs=[pl.BlockSpec(memory_space=pltpu.SMEM)] + [pl.BlockSpec(memory_space=pltpu.VMEM)] * 5,
+        borders,
+        out_shape=border,
+        in_specs=[scalars] * 2 + [local] * 4,
         scratch_shapes=[pltpu.VMEM((TILE_W, TILE_W), F32)],
         name="borders",
-    )(jnp.stack([group, jnp.int32(groups - 1)]).astype(jnp.int32), vert, hori, edges, edges_next, owners)
-
-    def match(column, last, fixed, moving, part, known):
-        def features(x):
-            if x.ndim == 4:
-                which = part[0] if x is fixed else part[1]
-                return pl.BlockSpec((pl.Squeezed(), half, flow, corr), lambda i, w=which: (0, w, 0, 0))
-            return pl.BlockSpec((half, flow, corr), lambda i: (0, 0, 0))
-
-        shape = (tiles * GROUP_LANES // TILE_W if last else tiles, TILE_W)
-
-        def kernel(*refs):
-            match_kernel(column, last, *refs)
-
-        return pl.pallas_call(
-            kernel,
-            grid=(1,),
-            out_shape=jax.ShapeDtypeStruct(shape, F32),
-            in_specs=[
-                features(fixed),
-                features(moving),
-                pl.BlockSpec((patches, offsets.shape[-1]), lambda i: (0, 0)),
-                pl.BlockSpec((tiles, TILE_W), lambda i: (0, 0)),
-            ],
-            out_specs=pl.BlockSpec(shape, lambda i: (0, 0)),
-            name="match_far" if last else "match_near",
-        )(fixed, moving, shifts[:patches] if not last else shifts_far, known)
-
-    table = match(COLUMN_NEAR, False, fixed_desc, moving_near, (0, 0), table)
-    mine = match(COLUMN_FAR, True, fixed_far, moving_desc, (0, 1), table)
-
-    seen = gather(mine, "z").reshape(-1, TILE_W)
+    )(owner, counts, vert, hori, line, above)
+    near, far, next_above, prev_above = lax.optimization_barrier((near, far, next_above, prev_above))
+    mine, next_line, next_columns, prev_line, prev_columns = pl.pallas_call(
+        match_kernel,
+        out_shape=(
+            jax.ShapeDtypeStruct((chips_z, halves, TILE_W), F32), border, upright, border, upright,
+        ),
+        in_specs=[local] * 6 + [anywhere] * 2,
+        out_specs=(local,) * 5,
+        scratch_shapes=[
+            pltpu.VMEM(packed.shape, packed.dtype),
+            pltpu.VMEM(packed.shape, packed.dtype),
+            pltpu.VMEM((2, flow, length // 2), F32),
+            pltpu.SemaphoreType.DMA((2 * PARTS + 2,)),
+        ],
+        compiler_params=pltpu.CompilerParams(vmem_limit_bytes=32 << 20),
+        name="match",
+    )(fixed_desc, moving_desc, offsets, table, line, hori, near, far)
+
+    seen = lax.all_to_all(mine, "z", 0, 0, tiled=True).reshape(-1, TILE_W)
     seen = gather(seen, ("group", "y")).reshape(-1, TILE_W)
     seen = lax.all_gather(seen, "core", axis=0, tiled=True)
 
     dims = (groups, sections, rows, tiles, chips_z)
-    halves = tiles * GROUP_LANES // TILE_W
     count = groups * tiles
 
     def both_iterations(*refs):
@@ -564,7 +685,7 @@
     displacement, residual = pl.pallas_call(
         both_iterations,
         out_shape=(field, field),
-        in_specs=[pl.BlockSpec(memory_space=pltpu.SMEM)] + [pl.BlockSpec(memory_space=pltpu.VMEM)] * 6,
+        in_specs=[local] * 11,
         scratch_shapes=[
             pltpu.VMEM((groups * halves, sections, TILE_W), F32),
             pltpu.VMEM((groups, halves * TILE_W, sections), F32),
@@ -574,7 +695,10 @@
         ],
         compiler_params=pltpu.CompilerParams(vmem_limit_bytes=32 << 20),
         name="stack",
-    )(jnp.stack([section, group]).astype(jnp.int32), seen, vert, hori, edges, edges_next, edges_prev)
+    )(
+        seen, vert, hori, line, above,
+        next_line, next_above, next_columns, prev_line, prev_above, prev_columns,
+    )
     return (displacement[None], residual[None])
 
 

time: 87.4 us -> 112 us (1.28)
  Pallas kernels: 12.2 us -> 43.3 us
  blocking collectives: 26.8 us -> 48.1 us
  starting transfers between devices: 29 us -> 16.8 us
  local copies, waits for them, and re-layouts: 9.33 us -> 1.99 us
  waiting for transfers between devices: 6.36 us -> 0.01 us
  other arithmetic: 1.42 us -> 0 us
    pallas_call x5 -> x4, Pallas kernels: 12.2 us -> 43.3 us  [the longest x1 33.6 us: body(): pl.pallas_call(pack_kernel, out_shape=(packed, packed, border), in_specs=...]
    all_to_all x0 -> x1, blocking collectives: none -> 26.1 us  [body(): seen = lax.all_to_all(mine, 'z', 0, 0, tiled=True).reshape(-1, TILE_W)]
    all_to_all x1 -> x0, starting transfers between devices: 10.7 us -> none  [gather(): return lax.all_to_all(copies, axis, 0, 0, tiled=True)]
    all_to_all x1, blocking collectives: 24.5 us -> 16.6 us  [gather(): return lax.all_to_all(copies, axis, 0, 0, tiled=True)]
    ppermute x6 -> x2, starting transfers between devices: 18.3 us -> 10.7 us  [from_behind(): return lax.ppermute(block, axis, route)]
    ppermute x0 -> x3, starting transfers between devices: none -> 6.05 us  [from_above(): return lax.ppermute(block, ('group',) + SEC, route)]
    all_to_all x1 -> x0, waiting for transfers between devices: 4.82 us -> none  [gather(): return lax.all_to_all(copies, axis, 0, 0, tiled=True)]
    all_gather x1, blocking collectives: 2.3 us -> 5.41 us  [body(): seen = lax.all_gather(seen, 'core', axis=0, tiled=True)]
  transfers between devices with their start and end apart: 7 -> 5, of which waited for: 2 -> 0; matrix products, arithmetic and copies ran while one was open for 5% -> 0% of each run, Pallas kernels for 7% -> 2%
where the time goes in v2:
time: 112 us
  blocking collectives  48.1 us (43%)
  Pallas kernels  43.3 us (39%)
  starting transfers between devices  16.8 us (15%)
  local copies, waits for them, and re-layouts  1.99 us (2%)
  between operations  1.44 us (1%)
    pallas_call x1, Pallas kernels, body(): pl.pallas_call(pack_kernel, out_shape=(packed, packed, border), in_specs=...  33.6 us
    all_to_all x1, blocking collectives, body(): seen = lax.all_to_all(mine, 'z', 0, 0, tiled=True).reshape(-1, TILE_W)  26.1 us
    all_to_all x1, blocking collectives, gather(): return lax.all_to_all(copies, axis, 0, 0, tiled=True)  16.6 us
    ppermute x2, starting transfers between devices, from_behind(): return lax.ppermute(block, axis, route)  10.7 us
    ppermute x3, starting transfers between devices, from_above(): return lax.ppermute(block, ('group',) + SEC, route)  6.05 us
    all_gather x1, blocking collectives, body(): seen = lax.all_gather(seen, 'core', axis=0, tiled=True)  5.41 us
    pallas_call x1, Pallas kernels, body(): pl.pallas_call(match_kernel, out_shape=(jax.ShapeDtypeStruct((chips_z, ha...  4.29 us
    pallas_call x1, Pallas kernels, body(): pl.pallas_call(both_iterations, out_shape=(field, field), in_specs=[local...  3.52 us
  transfers between devices with their start and end apart: 5, of which 0 were waited for; matrix products, arithmetic and copies ran while one was open for 0% of the time, Pallas kernels for 2%

profile of v2, /device:TPU:1, one launch (start us, length us, event | category | flops | bytes accessed | tf_op | source)
XLA Modules:
  0.0 111.5 jit_solution(9892727601954759805)
XLA Ops:
  0.6 33.6 %pack.1 = (bf16[528,512]{1,0:T(8,128)(2,1)}, bf16[528,512]{1,0:T(8,128)(2,1)}, f32[8,128]{1,0:T(8,128)}) custom-call(bf16[1024,512]{1,0:T(8,128)(2,1)} %bitcast.9, bf16[1024,512]{1,0:T(8,128)(2,1)} %bitcast.8, f32[1,16,1024]{2,1,0:T(8,128)} %vert_ref.1, f32[1,16,1024]{2,1,0:T(8,128)} %hori_ref.1, s32[1,16,2,64]{3,2,1,0:T(2,128)} %offsets_ref.3), custom_call_target="tpu_custom_call" | custom-call | tf_op jit(solution)/shard_map/pack/pallas_call | solution.py:624
  34.2 8.8 %collective-permute-start.1 = (bf16[528,512]{1,0:T(8,128)(2,1)}, bf16[528,512]{1,0:T(8,128)(2,1)S(1)}, u32[]{:S(2)}, u32[]{:S(2)}) collective-permute-start(bf16[528,512]{1,0:T(8,128)(2,1)} %get-tuple-element.17), channel_id=1, source_target_pairs={{1,0},{2,1},{3,2},{4,3},{5,4},{6,5},{7,6},{8,7},{9,8},{10,9},{11,1... | collective-permute-start | bytes 1622024 | tf_op jit(solution)/shard_map/ppermute | solution.py:587
  43.0 1.9 %collective-permute-start.2 = (bf16[528,512]{1,0:T(8,128)(2,1)}, bf16[528,512]{1,0:T(8,128)(2,1)S(1)}, u32[]{:S(2)}, u32[]{:S(2)}) collective-permute-start(bf16[528,512]{1,0:T(8,128)(2,1)} %get-tuple-element.18), channel_id=1, source_target_pairs={{0,1},{1,2},{2,3},{3,4},{4,5},{5,6},{6,7},{7,8},{8,9},{9,10},{10,1... | collective-permute-start | bytes 1622024 | tf_op jit(solution)/shard_map/ppermute | solution.py:587
  44.9 1.3 %collective-permute-start = (f32[8,128]{1,0:T(8,128)}, f32[8,128]{1,0:T(8,128)S(1)}, u32[]{:S(2)}, u32[]{:S(2)}) collective-permute-start(f32[8,128]{1,0:T(8,128)} %get-tuple-element.16.refs_4_.line_ref.refs_3_), channel_id=1, source_target_pairs={{0,128},{1,129},{2,130},{3,131},{4,132},{5,133},{6,134},{7,135},{8... | collective-permute-start | bytes 12296 | tf_op jit(solution)/shard_map/ppermute | solution.py:598
  46.2 1.3 %collective-permute-start.3 = (f32[8,128]{1,0:T(8,128)}, f32[8,128]{1,0:T(8,128)S(1)}, u32[]{:S(2)}, u32[]{:S(2)}) collective-permute-start(f32[8,128]{1,0:T(8,128)} %get-tuple-element.16.refs_4_.line_ref.refs_3_), channel_id=1, source_target_pairs={{1,128},{2,129},{3,130},{4,131},{5,132},{6,133},{7,134},{8,135},{9... | collective-permute-start | bytes 12296 | tf_op jit(solution)/shard_map/ppermute | solution.py:598
  47.5 3.5 %collective-permute-start.4 = (f32[8,128]{1,0:T(8,128)}, f32[8,128]{1,0:T(8,128)S(1)}, u32[]{:S(2)}, u32[]{:S(2)}) collective-permute-start(f32[8,128]{1,0:T(8,128)} %get-tuple-element.16.refs_4_.line_ref.refs_3_), channel_id=1, source_target_pairs={{0,129},{1,130},{2,131},{3,132},{4,133},{5,134},{6,135},{7,136},{8... | collective-permute-start | bytes 12296 | tf_op jit(solution)/shard_map/ppermute | solution.py:598
  51.7 0.0 collective-permute-done.refs_5_.refs_4_
  51.7 0.0 copy-start.5
  51.7 0.6 copy-done.5
  52.3 1.9 %borders.1.table_ref = f32[8,128]{1,0:T(8,128)} custom-call(s32[1,16]{1,0:T(1,128)} %refs_0_.1, s32[1,1]{1,0:T(1,128)S(6)} %copy.9.refs_1_, f32[16,1024]{1,0:T(8,128)} %bitcast.13, f32[16,1024]{1,0:T(8,128)} %bitcast.10, f32[8,128]{1,0:T(8,128)} %get-tuple-element.16.refs_4_.line_ref.refs_3_, f32[8,128]{1,0:T(8,128)} %copy-done.5), custom_call_target="tpu_custom_call" | custom-call | tf_op jit(solution)/shard_map/borders/pallas_call | solution.py:649
  54.2 0.0 collective-permute-done.3.refs_6_
  54.2 0.0 collective-permute-done.4.refs_9_
  54.2 0.0 collective-permute-done.1.near_ref
  54.2 0.0 collective-permute-done.2.far_ref
  54.2 0.0 copy-done
  54.2 0.0 copy-done.1
  54.2 0.0 copy-start.7
  54.2 0.7 copy-done.7
  54.9 4.3 %match.1 = (f32[16,2,128]{2,1,0:T(2,128)S(1)}, f32[8,128]{1,0:T(8,128)S(1)}, f32[16,128]{1,0:T(8,128)S(1)}, f32[8,128]{1,0:T(8,128)S(1)}, f32[16,128]{1,0:T(8,128)S(1)}) custom-call(bf16[1,16,64,512]{3,2,1,0:T(8,128)(2,1)S(1)} %copy-done, bf16[1,16,64,512]{3,2,1,0:T(8,128)(2,1)S(1)} %copy-done.1, s32[1,16,2,64]{3,2,1,0:T(2,128)S(1)} %copy-done.4, ...), custom_call_target="tpu_custom_call" | custom-call | tf_op jit(solution)/shard_map/match/pallas_call | solution.py:657
  59.2 26.1 %all_to_all.10 = f32[16,2,128]{2,1,0:T(2,128)S(1)} all-to-all(f32[16,2,128]{2,1,0:T(2,128)S(1)} %get-tuple-element.21), channel_id=1, replica_groups=mesh['group'=4,'z'=16,'y'=4,'core'=2] {'z'}, dimensions={0} | all-to-all | bytes 32768 | tf_op jit(solution)/shard_map/all_to_all | solution.py:674
  85.3 16.6 %all_to_all.11 = f32[16,32,128]{2,1,0:T(8,128)S(1)} all-to-all(f32[16,32,128]{2,1,0:T(8,128)S(1)} %broadcast_in_dim.14), channel_id=1, replica_groups=mesh['group'=4,'z'=16,'y'=4,'core'=2] {'group','y'}, dimensions={0} | all-to-all | bytes 524288 | tf_op jit(solution)/shard_map/all_to_all | solution.py:604
  101.9 5.4 %all_gather.3.refs_0_ = f32[1024,128]{1,0:T(8,128)S(1)} all-gather(f32[512,128]{1,0:T(8,128)S(1)} %bitcast.15), channel_id=1, replica_groups=mesh['group'=4,'z'=16,'y'=4,'core'=2] {'core'}, dimensions={0}, use_global_device_ids=true | all-gather | bytes 786432 | tf_op jit(solution)/shard_map/all_gather | solution.py:676
  107.3 0.7 copy-done.6
  108.0 3.5 %stack.1 = (f32[2,16,1024]{2,1,0:T(8,128)}, f32[2,16,1024]{2,1,0:T(8,128)}) custom-call(f32[1024,128]{1,0:T(8,128)S(1)} %all_gather.3.refs_0_, f32[16,1024]{1,0:T(8,128)S(1)} %bitcast.14, f32[16,1024]{1,0:T(8,128)S(1)} %bitcast.12, f32[8,128]{1,0:T(8,128)} %get-tuple-element.16.refs_4_.line_ref.refs_3_, f32[8,128]{1,0:T(8,128)S(1)} %copy-done.6, ...), custom_call_target="tpu_custom_call" | custom-call | tf_op jit(solution)/shard_map/stack/pallas_call | solution.py:685
  (10 shorter events, 0.0 us)
Async XLA Ops:
  0.6 53.6 %copy-start = (bf16[1,16,64,512]{3,2,1,0:T(8,128)(2,1)S(1)}, bf16[1,16,64,512]{3,2,1,0:T(8,128)(2,1)}, u32[]{:S(2)}) copy-start(bf16[1,16,64,512]{3,2,1,0:T(8,128)(2,1)} %fixed_ref.1) | copy-start | bytes 3145732
  0.6 53.6 %copy-start.1 = (bf16[1,16,64,512]{3,2,1,0:T(8,128)(2,1)S(1)}, bf16[1,16,64,512]{3,2,1,0:T(8,128)(2,1)}, u32[]{:S(2)}) copy-start(bf16[1,16,64,512]{3,2,1,0:T(8,128)(2,1)} %moving_ref.1) | copy-start | bytes 3145732
  34.2 19.9 %collective-permute-start.1 = (bf16[528,512]{1,0:T(8,128)(2,1)}, bf16[528,512]{1,0:T(8,128)(2,1)S(1)}, u32[]{:S(2)}, u32[]{:S(2)}) collective-permute-start(bf16[528,512]{1,0:T(8,128)(2,1)} %get-tuple-element.17), channel_id=1, source_target_pairs={{1,0},{2,1},{3,2},{4,3},{5,4},{6,5},{7,6},{8,7},{9,8},{10,9},{11,1... | collective-permute-start | bytes 1622024 | tf_op jit(solution)/shard_map/ppermute | solution.py:587
  43.0 11.2 %collective-permute-start.2 = (bf16[528,512]{1,0:T(8,128)(2,1)}, bf16[528,512]{1,0:T(8,128)(2,1)S(1)}, u32[]{:S(2)}, u32[]{:S(2)}) collective-permute-start(bf16[528,512]{1,0:T(8,128)(2,1)} %get-tuple-element.18), channel_id=1, source_target_pairs={{0,1},{1,2},{2,3},{3,4},{4,5},{5,6},{6,7},{7,8},{8,9},{9,10},{10,1... | collective-permute-start | bytes 1622024 | tf_op jit(solution)/shard_map/ppermute | solution.py:587
  44.9 6.7 %collective-permute-start = (f32[8,128]{1,0:T(8,128)}, f32[8,128]{1,0:T(8,128)S(1)}, u32[]{:S(2)}, u32[]{:S(2)}) collective-permute-start(f32[8,128]{1,0:T(8,128)} %get-tuple-element.16.refs_4_.line_ref.refs_3_), channel_id=1, source_target_pairs={{0,128},{1,129},{2,130},{3,131},{4,132},{5,133},{6,134},{7,135},{8... | collective-permute-start | bytes 12296 | tf_op jit(solution)/shard_map/ppermute | solution.py:598
  46.2 7.9 %collective-permute-start.3 = (f32[8,128]{1,0:T(8,128)}, f32[8,128]{1,0:T(8,128)S(1)}, u32[]{:S(2)}, u32[]{:S(2)}) collective-permute-start(f32[8,128]{1,0:T(8,128)} %get-tuple-element.16.refs_4_.line_ref.refs_3_), channel_id=1, source_target_pairs={{1,128},{2,129},{3,130},{4,131},{5,132},{6,133},{7,134},{8,135},{9... | collective-permute-start | bytes 12296 | tf_op jit(solution)/shard_map/ppermute | solution.py:598
  47.5 6.6 %collective-permute-start.4 = (f32[8,128]{1,0:T(8,128)}, f32[8,128]{1,0:T(8,128)S(1)}, u32[]{:S(2)}, u32[]{:S(2)}) collective-permute-start(f32[8,128]{1,0:T(8,128)} %get-tuple-element.16.refs_4_.line_ref.refs_3_), channel_id=1, source_target_pairs={{0,129},{1,130},{2,131},{3,132},{4,133},{5,134},{6,135},{7,136},{8... | collective-permute-start | bytes 12296 | tf_op jit(solution)/shard_map/ppermute | solution.py:598
  51.7 0.6 copy-start.5
  52.3 1.9 %copy-start.2 = (f32[1,16,1024]{2,1,0:T(8,128)S(1)}, f32[1,16,1024]{2,1,0:T(8,128)}, u32[]{:S(2)}) copy-start(f32[1,16,1024]{2,1,0:T(8,128)} %hori_ref.1) | copy-start | bytes 196612
  52.3 1.9 %copy-start.4 = (s32[1,16,2,64]{3,2,1,0:T(2,128)S(1)}, s32[1,16,2,64]{3,2,1,0:T(2,128)}, u32[]{:S(2)}) copy-start(s32[1,16,2,64]{3,2,1,0:T(2,128)} %offsets_ref.3) | copy-start | bytes 24580
  54.2 0.7 copy-start.7
  101.9 5.4 %copy-start.3 = (f32[1,16,1024]{2,1,0:T(8,128)S(1)}, f32[1,16,1024]{2,1,0:T(8,128)}, u32[]{:S(2)}) copy-start(f32[1,16,1024]{2,1,0:T(8,128)} %vert_ref.1) | copy-start | bytes 196612
  107.3 0.7 copy-start.6

commit v3 on v2

--- a/solution.py
+++ b/solution.py
@@ -47,26 +47,26 @@
 
 
 def pack_kernel(
-    moving_ref, fixed_ref, vert_ref, hori_ref, offsets_ref, near_ref, far_ref, line_ref,
-    vert, hori, offsets, extra, sems,
+    moving_ref, fixed_ref, vert_ref, hori_ref, offsets_ref, near, far, line_ref,
+    vert, hori, offsets, sems,
 ):
     rows, cols = hori.shape
     tiles = cols // TILE_W
     length = moving_ref.shape[0] // 2
     part = length // PARTS
-    copies = []
+    tail = slice(length, length + rows)
+    loads = [
+        pltpu.make_async_copy(vert_ref.at[0], vert, sems.at[0]),
+        pltpu.make_async_copy(hori_ref.at[0], hori, sems.at[1]),
+        pltpu.make_async_copy(offsets_ref.at[0], offsets, sems.at[2]),
+    ]
+    arrive = []
     for n in range(PARTS):
         at = pl.ds(n * part, part)
-        copies.append(pltpu.make_async_copy(moving_ref.at[at], near_ref.at[at], sems.at[2 * n]))
         behind = pl.ds(length + n * part, part)
-        copies.append(pltpu.make_async_copy(fixed_ref.at[behind], far_ref.at[at], sems.at[2 * n + 1]))
-    first = 2 * PARTS
-    loads = [
-        pltpu.make_async_copy(vert_ref.at[0], vert, sems.at[first]),
-        pltpu.make_async_copy(hori_ref.at[0], hori, sems.at[first + 1]),
-        pltpu.make_async_copy(offsets_ref.at[0], offsets, sems.at[first + 2]),
-    ]
-    for copy in copies + loads:
+        arrive.append(pltpu.make_async_copy(moving_ref.at[at], near.at[at], sems.at[3 + 2 * n]))
+        arrive.append(pltpu.make_async_copy(fixed_ref.at[behind], far.at[at], sems.at[4 + 2 * n]))
+    for copy in loads + arrive:
         copy.start()
     for copy in loads:
         copy.wait()
@@ -84,17 +84,11 @@
     blank = jnp.zeros((tiles, TILE_W), F32)
     for n, value in enumerate(three_parts(line_ref[...])):
         span = slice(n * TILE_W, (n + 1) * TILE_W)
-        extra[0, :, span] = jnp.concatenate([value, blank], 0).astype(jnp.bfloat16)
-        extra[1, :, span] = jnp.concatenate([value, blank if n else shifts], 0).astype(jnp.bfloat16)
-    for n in range(2):
-        extra[n, :, 3 * TILE_W :] = columns.astype(jnp.bfloat16)
-    tail = [
-        pltpu.make_async_copy(extra.at[n], ref.at[pl.ds(length, rows)], sems.at[first + 3 + n])
-        for n, ref in enumerate((near_ref, far_ref))
-    ]
-    for copy in tail:
-        copy.start()
-    for copy in copies + tail:
+        near[tail, span] = jnp.concatenate([value, blank], 0).astype(jnp.bfloat16)
+        far[tail, span] = jnp.concatenate([value, blank if n else shifts], 0).astype(jnp.bfloat16)
+    for block in (near, far):
+        block[tail, 3 * TILE_W :] = columns.astype(jnp.bfloat16)
+    for copy in arrive:
         copy.wait()
 
 
@@ -234,48 +228,30 @@
 def match_kernel(
     fixed_ref, moving_ref, offsets_ref, table_ref, line_ref, hori_ref, near_ref, far_ref,
     out_ref, next_line_ref, next_columns_ref, prev_line_ref, prev_columns_ref,
-    near, far, scores_ref, sems,
+    scores_ref,
 ):
     patches, flow, corr = fixed_ref.shape[1:]
     half = patches // 2
     length = half * flow
-    part = length // PARTS
     rows, cols = hori_ref.shape[-2:]
     tiles = cols // TILE_W
     pair = 2 * flow
-    arrivals = [
-        pltpu.make_async_copy(near_ref.at[pl.ds(length, rows)], near.at[pl.ds(length, rows)], sems.at[2 * PARTS]),
-        pltpu.make_async_copy(far_ref.at[pl.ds(length, rows)], far.at[pl.ds(length, rows)], sems.at[2 * PARTS + 1]),
-    ]
-    loads = []
-    for side, (source, target) in enumerate(((near_ref, near), (far_ref, far))):
-        for n in range(PARTS):
-            at = pl.ds(n * part, part)
-            loads.append(pltpu.make_async_copy(source.at[at], target.at[at], sems.at[side * PARTS + n]))
-    for copy in loads + arrivals:
-        copy.start()
-
     lower = iota((flow, pair), 1) < flow
     for side in range(2):
-        for n in range(PARTS):
-            loads[side * PARTS + n].wait()
-            for first in range(n * half // PARTS, (n + 1) * half // PARTS, 2):
-                at = slice(first * flow, (first + 2) * flow)
-                if side == 0:
-                    fixed = fixed_ref[0, first : first + 2].reshape(pair, corr)
-                    moving = near[at, :]
-                else:
-                    fixed = far[at, :]
-                    moving = moving_ref[0, half + first : half + first + 2].reshape(pair, corr)
-                scores = lax.dot_general(
-                    moving, fixed, (((1,), (1,)), ((), ())), preferred_element_type=F32
-                )
-                both = jnp.where(lower, scores[0:flow, :], scores[flow:pair, :])
-                scores_ref[side, :, at] = both
-    for copy in arrivals:
-        copy.wait()
-    next_line, next_columns, _ = unpack(near[length : length + rows, :], tiles)
-    prev_line, prev_columns, shifts = unpack(far[length : length + rows, :], tiles)
+        for first in range(0, half, 2):
+            at = slice(first * flow, (first + 2) * flow)
+            if side == 0:
+                fixed = fixed_ref[0, first : first + 2].reshape(pair, corr)
+                moving = near_ref[at, :]
+            else:
+                fixed = far_ref[at, :]
+                moving = moving_ref[0, half + first : half + first + 2].reshape(pair, corr)
+            scores = lax.dot_general(
+                moving, fixed, (((1,), (1,)), ((), ())), preferred_element_type=F32
+            )
+            scores_ref[side, :, at] = jnp.where(lower, scores[0:flow, :], scores[flow:pair, :])
+    next_line, next_columns, _ = unpack(near_ref[length : length + rows, :], tiles)
+    prev_line, prev_columns, shifts = unpack(far_ref[length : length + rows, :], tiles)
     next_line_ref[...] = next_line
     next_columns_ref[...] = next_columns
     prev_line_ref[...] = prev_line
@@ -581,6 +557,10 @@
             res_ref[k, :, span] = r - beta * applied
 
 
+def in_vmem(x):
+    return pltpu.VMEM(x.shape, x.dtype)
+
+
 def from_behind(block, axis, distance):
     devices = range(lax.axis_size(axis))
     route = [(i - distance, i) for i in devices if i - distance in devices]
@@ -614,27 +594,32 @@
     length = patches * flow
     halves = tiles * GROUP_LANES // TILE_W
 
-    anywhere = pl.BlockSpec(memory_space=pl.ANY)
     hbm = pl.BlockSpec(memory_space=pltpu.HBM)
     local = pl.BlockSpec(memory_space=pltpu.VMEM)
     scalars = pl.BlockSpec(memory_space=pltpu.SMEM)
+    modest = pltpu.CompilerParams(vmem_limit_bytes=16 << 20)
     packed = jax.ShapeDtypeStruct((length // 2 + rows, corr), fixed_desc.dtype)
     border = jax.ShapeDtypeStruct((tiles, TILE_W), F32)
     upright = jax.ShapeDtypeStruct((rows, TILE_W), F32)
     near, far, line = pl.pallas_call(
         pack_kernel,
-        out_shape=(packed, packed, border),
+        out_shape=(in_vmem(packed), in_vmem(packed), in_vmem(border)),
         in_specs=[hbm] * 5,
-        out_specs=(anywhere, anywhere, local),
+        out_specs=(local,) * 3,
         scratch_shapes=[
             pltpu.VMEM((rows, cols), F32),
             pltpu.VMEM((rows, cols), F32),
             pltpu.VMEM(offsets.shape[1:], jnp.int32),
-            pltpu.VMEM((2, rows, corr), fixed_desc.dtype),
-            pltpu.SemaphoreType.DMA((2 * PARTS + 5,)),
+            pltpu.SemaphoreType.DMA((2 * PARTS + 3,)),
         ],
+        compiler_params=modest,
         name="pack",
-    )(moving_desc.reshape(length, corr), fixed_desc.reshape(length, corr), vert, hori, offsets)
+    )(
+        *(
+            pltpu.with_memory_space_constraint(x, pltpu.HBM)
+            for x in (moving_desc.reshape(length, corr), fixed_desc.reshape(length, corr), vert, hori, offsets)
+        )
+    )
     near = from_behind(near, SEC, -1)
     far = from_behind(far, SEC, 1)
     above = from_above(line, 0)
@@ -651,6 +636,7 @@
         out_shape=border,
         in_specs=[scalars] * 2 + [local] * 4,
         scratch_shapes=[pltpu.VMEM((TILE_W, TILE_W), F32)],
+        compiler_params=modest,
         name="borders",
     )(owner, counts, vert, hori, line, above)
     near, far, next_above, prev_above = lax.optimization_barrier((near, far, next_above, prev_above))
@@ -659,15 +645,10 @@
         out_shape=(
             jax.ShapeDtypeStruct((chips_z, halves, TILE_W), F32), border, upright, border, upright,
         ),
-        in_specs=[local] * 6 + [anywhere] * 2,
+        in_specs=[local] * 8,
         out_specs=(local,) * 5,
-        scratch_shapes=[
-            pltpu.VMEM(packed.shape, packed.dtype),
-            pltpu.VMEM(packed.shape, packed.dtype),
-            pltpu.VMEM((2, flow, length // 2), F32),
-            pltpu.SemaphoreType.DMA((2 * PARTS + 2,)),
-        ],
-        compiler_params=pltpu.CompilerParams(vmem_limit_bytes=32 << 20),
+        scratch_shapes=[pltpu.VMEM((2, flow, length // 2), F32)],
+        compiler_params=modest,
         name="match",
     )(fixed_desc, moving_desc, offsets, table, line, hori, near, far)
 
@@ -693,7 +674,7 @@
             pltpu.VMEM((24, count + 2 * tiles, sections), F32),
             pltpu.VMEM((2, rows + 2 * tiles, cols), F32),
         ],
-        compiler_params=pltpu.CompilerParams(vmem_limit_bytes=32 << 20),
+        compiler_params=modest,
         name="stack",
     )(
         seen, vert, hori, line, above,

time: 112 us -> 74 us (0.66)
  Pallas kernels: 43.3 us -> 6.05 us
  local copies, waits for them, and re-layouts: 1.99 us -> 0.67 us
    pallas_call x1, Pallas kernels: 33.6 us -> 1.58 us  [body(): pl.pallas_call(pack_kernel, out_shape=(in_vmem(packed), in_vmem(packed),...]
    pallas_call x1, Pallas kernels: 4.29 us -> 0.78 us  [body(): pl.pallas_call(match_kernel, out_shape=(jax.ShapeDtypeStruct((chips_z, ha...]
    unnamed x16 -> x12, local copies, waits for them, and re-layouts: 1.97 us -> 0.65 us
  transfers between devices with their start and end apart: 5 -> 5, of which waited for: 0 -> 0; matrix products, arithmetic and copies ran while one was open for 0% -> 0% of each run, Pallas kernels for 2% -> 1%
where the time goes in v3:
time: 74 us; the launch traced here: 73.6 us
  blocking collectives  48.7 us (66%)
  starting transfers between devices  16.8 us (23%)
  Pallas kernels  6.05 us (8%)
  between operations  1.46 us (2%)
    all_to_all x1, blocking collectives, body(): seen = lax.all_to_all(mine, 'z', 0, 0, tiled=True).reshape(-1, TILE_W)  26.1 us
    all_to_all x1, blocking collectives, gather(): return lax.all_to_all(copies, axis, 0, 0, tiled=True)  16.4 us
    ppermute x2, starting transfers between devices, from_behind(): return lax.ppermute(block, axis, route)  10.7 us
    all_gather x1, blocking collectives, body(): seen = lax.all_gather(seen, 'core', axis=0, tiled=True)  6.13 us
    ppermute x3, starting transfers between devices, from_above(): return lax.ppermute(block, ('group',) + SEC, route)  6.05 us
    pallas_call x1, Pallas kernels, body(): pl.pallas_call(both_iterations, out_shape=(field, field), in_specs=[local...  2.83 us
    pallas_call x1, Pallas kernels, body(): pl.pallas_call(pack_kernel, out_shape=(in_vmem(packed), in_vmem(packed),...  1.58 us
  transfers between devices with their start and end apart: 5, of which 0 were waited for; matrix products, arithmetic and copies ran while one was open for 0% of the time, Pallas kernels for 1%

profile of v3, /device:TPU:1, one launch (start us, length us, event | category | flops | bytes accessed | tf_op | source)
XLA Modules:
  0.0 73.6 jit_solution(13503551968547566332)
XLA Ops:
  0.7 1.6 %pack.1 = (bf16[528,512]{1,0:T(8,128)(2,1)S(1)}, bf16[528,512]{1,0:T(8,128)(2,1)S(1)}, f32[8,128]{1,0:T(8,128)S(1)}) custom-call(bf16[1024,512]{1,0:T(8,128)(2,1)} %bitcast.9, bf16[1024,512]{1,0:T(8,128)(2,1)} %bitcast.8, f32[1,16,1024]{2,1,0:T(8,128)} %vert_ref.1, f32[1,16,1024]{2,1,0:T(8,128)} %hori_ref.1, s32[1,16,2,64]{3,2,1,0:T(2,128)} %offsets_ref.3), custom_call_target="tpu_custom_call" | custom-call | tf_op jit(solution)/shard_map/pack/pallas_call | solution.py:604
  2.3 8.8 %collective-permute-start.1 = (bf16[528,512]{1,0:T(8,128)(2,1)S(1)}, bf16[528,512]{1,0:T(8,128)(2,1)S(1)}, u32[]{:S(2)}, u32[]{:S(2)}) collective-permute-start(bf16[528,512]{1,0:T(8,128)(2,1)S(1)} %get-tuple-element.17), channel_id=1, source_target_pairs={{1,0},{2,1},{3,2},{4,3},{5,4},{6,5},{7,6},{8,7},{9,8},{10,9},{11,1... | collective-permute-start | bytes 1622024 | tf_op jit(solution)/shard_map/ppermute | solution.py:567
  11.0 1.9 %collective-permute-start.2 = (bf16[528,512]{1,0:T(8,128)(2,1)S(1)}, bf16[528,512]{1,0:T(8,128)(2,1)S(1)}, u32[]{:S(2)}, u32[]{:S(2)}) collective-permute-start(bf16[528,512]{1,0:T(8,128)(2,1)S(1)} %get-tuple-element.18), channel_id=1, source_target_pairs={{0,1},{1,2},{2,3},{3,4},{4,5},{5,6},{6,7},{7,8},{8,9},{9,10},{10,1... | collective-permute-start | bytes 1622024 | tf_op jit(solution)/shard_map/ppermute | solution.py:567
  13.0 1.3 %collective-permute-start = (f32[8,128]{1,0:T(8,128)S(1)}, f32[8,128]{1,0:T(8,128)S(1)}, u32[]{:S(2)}, u32[]{:S(2)}) collective-permute-start(f32[8,128]{1,0:T(8,128)S(1)} %get-tuple-element.16.refs_4_.line_ref.refs_3_), channel_id=1, source_target_pairs={{0,128},{1,129},{2,130},{3,131},{4,132},{5,133},{6,134},{7,135},{8... | collective-permute-start | bytes 12296 | tf_op jit(solution)/shard_map/ppermute | solution.py:578
  14.3 1.3 %collective-permute-start.3 = (f32[8,128]{1,0:T(8,128)S(1)}, f32[8,128]{1,0:T(8,128)S(1)}, u32[]{:S(2)}, u32[]{:S(2)}) collective-permute-start(f32[8,128]{1,0:T(8,128)S(1)} %get-tuple-element.16.refs_4_.line_ref.refs_3_), channel_id=1, source_target_pairs={{1,128},{2,129},{3,130},{4,131},{5,132},{6,133},{7,134},{8,135},{9... | collective-permute-start | bytes 12296 | tf_op jit(solution)/shard_map/ppermute | solution.py:578
  15.6 3.5 %collective-permute-start.4 = (f32[8,128]{1,0:T(8,128)S(1)}, f32[8,128]{1,0:T(8,128)S(1)}, u32[]{:S(2)}, u32[]{:S(2)}) collective-permute-start(f32[8,128]{1,0:T(8,128)S(1)} %get-tuple-element.16.refs_4_.line_ref.refs_3_), channel_id=1, source_target_pairs={{0,129},{1,130},{2,131},{3,132},{4,133},{5,134},{6,135},{7,136},{8... | collective-permute-start | bytes 12296 | tf_op jit(solution)/shard_map/ppermute | solution.py:578
  19.7 0.0 collective-permute-done.refs_5_.refs_4_
  19.7 0.0 copy-start.5
  19.7 0.0 copy-done.2
  19.7 0.0 copy-done.3
  19.7 0.6 copy-done.5
  20.4 0.9 %borders.1.table_ref = f32[8,128]{1,0:T(8,128)S(1)} custom-call(s32[1,16]{1,0:T(1,128)S(1)} %copy-done.5, s32[1,1]{1,0:T(1,128)S(6)} %copy.9.refs_1_, f32[16,1024]{1,0:T(8,128)S(1)} %bitcast.13, f32[16,1024]{1,0:T(8,128)S(1)} %bitcast.10, f32[8,128]{1,0:T(8,128)S(1)} %get-tuple-element.16.refs_4_.line_ref.refs_3_, ...), custom_call_target="tpu_custom_call" | custom-call | tf_op jit(solution)/shard_map/borders/pallas_call | solution.py:634
  21.2 0.0 collective-permute-done.3.refs_6_
  21.2 0.0 collective-permute-done.4.refs_9_
  21.2 0.0 collective-permute-done.1.near_ref
  21.3 0.0 collective-permute-done.2.far_ref
  21.3 0.0 copy-done
  21.3 0.0 copy-done.1
  21.3 0.0 copy-done.4
  21.3 0.8 %match.1 = (f32[16,2,128]{2,1,0:T(2,128)S(1)}, f32[8,128]{1,0:T(8,128)S(1)}, f32[16,128]{1,0:T(8,128)S(1)}, f32[8,128]{1,0:T(8,128)S(1)}, f32[16,128]{1,0:T(8,128)S(1)}) custom-call(bf16[1,16,64,512]{3,2,1,0:T(8,128)(2,1)S(1)} %copy-done, bf16[1,16,64,512]{3,2,1,0:T(8,128)(2,1)S(1)} %copy-done.1, s32[1,16,2,64]{3,2,1,0:T(2,128)S(1)} %copy-done.4, ...), custom_call_target="tpu_custom_call" | custom-call | tf_op jit(solution)/shard_map/match/pallas_call | solution.py:643
  22.1 26.1 %all_to_all.10 = f32[16,2,128]{2,1,0:T(2,128)S(1)} all-to-all(f32[16,2,128]{2,1,0:T(2,128)S(1)} %get-tuple-element.21), channel_id=1, replica_groups=mesh['group'=4,'z'=16,'y'=4,'core'=2] {'z'}, dimensions={0} | all-to-all | bytes 32768 | tf_op jit(solution)/shard_map/all_to_all | solution.py:655
  48.3 16.4 %all_to_all.11 = f32[16,32,128]{2,1,0:T(8,128)S(1)} all-to-all(f32[16,32,128]{2,1,0:T(8,128)S(1)} %broadcast_in_dim.14), channel_id=1, replica_groups=mesh['group'=4,'z'=16,'y'=4,'core'=2] {'group','y'}, dimensions={0} | all-to-all | bytes 524288 | tf_op jit(solution)/shard_map/all_to_all | solution.py:584
  64.7 6.1 %all_gather.3.refs_0_ = f32[1024,128]{1,0:T(8,128)S(1)} all-gather(f32[512,128]{1,0:T(8,128)S(1)} %bitcast.15), channel_id=1, replica_groups=mesh['group'=4,'z'=16,'y'=4,'core'=2] {'core'}, dimensions={0}, use_global_device_ids=true | all-gather | bytes 786432 | tf_op jit(solution)/shard_map/all_gather | solution.py:657
  70.8 2.8 %stack.1 = (f32[2,16,1024]{2,1,0:T(8,128)}, f32[2,16,1024]{2,1,0:T(8,128)}) custom-call(f32[1024,128]{1,0:T(8,128)S(1)} %all_gather.3.refs_0_, f32[16,1024]{1,0:T(8,128)S(1)} %bitcast.14, f32[16,1024]{1,0:T(8,128)S(1)} %bitcast.12, f32[8,128]{1,0:T(8,128)S(1)} %get-tuple-element.16.refs_4_.line_ref.refs_3_, ...), custom_call_target="tpu_custom_call" | custom-call | tf_op jit(solution)/shard_map/stack/pallas_call | solution.py:666
  (6 shorter events, 0.0 us)
Async XLA Ops:
  0.6 19.1 %copy-start.2 = (f32[1,16,1024]{2,1,0:T(8,128)S(1)}, f32[1,16,1024]{2,1,0:T(8,128)}, u32[]{:S(2)}) copy-start(f32[1,16,1024]{2,1,0:T(8,128)} %hori_ref.1) | copy-start | bytes 196612
  0.6 19.1 %copy-start.3 = (f32[1,16,1024]{2,1,0:T(8,128)S(1)}, f32[1,16,1024]{2,1,0:T(8,128)}, u32[]{:S(2)}) copy-start(f32[1,16,1024]{2,1,0:T(8,128)} %vert_ref.1) | copy-start | bytes 196612
  0.7 20.6 %copy-start = (bf16[1,16,64,512]{3,2,1,0:T(8,128)(2,1)S(1)}, bf16[1,16,64,512]{3,2,1,0:T(8,128)(2,1)}, u32[]{:S(2)}) copy-start(bf16[1,16,64,512]{3,2,1,0:T(8,128)(2,1)} %fixed_ref.1) | copy-start | bytes 3145732
  0.7 20.6 %copy-start.1 = (bf16[1,16,64,512]{3,2,1,0:T(8,128)(2,1)S(1)}, bf16[1,16,64,512]{3,2,1,0:T(8,128)(2,1)}, u32[]{:S(2)}) copy-start(bf16[1,16,64,512]{3,2,1,0:T(8,128)(2,1)} %moving_ref.1) | copy-start | bytes 3145732
  2.3 19.0 %collective-permute-start.1 = (bf16[528,512]{1,0:T(8,128)(2,1)S(1)}, bf16[528,512]{1,0:T(8,128)(2,1)S(1)}, u32[]{:S(2)}, u32[]{:S(2)}) collective-permute-start(bf16[528,512]{1,0:T(8,128)(2,1)S(1)} %get-tuple-element.17), channel_id=1, source_target_pairs={{1,0},{2,1},{3,2},{4,3},{5,4},{6,5},{7,6},{8,7},{9,8},{10,9},{11,1... | collective-permute-start | bytes 1622024 | tf_op jit(solution)/shard_map/ppermute | solution.py:567
  11.0 10.2 %collective-permute-start.2 = (bf16[528,512]{1,0:T(8,128)(2,1)S(1)}, bf16[528,512]{1,0:T(8,128)(2,1)S(1)}, u32[]{:S(2)}, u32[]{:S(2)}) collective-permute-start(bf16[528,512]{1,0:T(8,128)(2,1)S(1)} %get-tuple-element.18), channel_id=1, source_target_pairs={{0,1},{1,2},{2,3},{3,4},{4,5},{5,6},{6,7},{7,8},{8,9},{9,10},{10,1... | collective-permute-start | bytes 1622024 | tf_op jit(solution)/shard_map/ppermute | solution.py:567
  13.0 6.7 %collective-permute-start = (f32[8,128]{1,0:T(8,128)S(1)}, f32[8,128]{1,0:T(8,128)S(1)}, u32[]{:S(2)}, u32[]{:S(2)}) collective-permute-start(f32[8,128]{1,0:T(8,128)S(1)} %get-tuple-element.16.refs_4_.line_ref.refs_3_), channel_id=1, source_target_pairs={{0,128},{1,129},{2,130},{3,131},{4,132},{5,133},{6,134},{7,135},{8... | collective-permute-start | bytes 12296 | tf_op jit(solution)/shard_map/ppermute | solution.py:578
  14.3 7.0 %collective-permute-start.3 = (f32[8,128]{1,0:T(8,128)S(1)}, f32[8,128]{1,0:T(8,128)S(1)}, u32[]{:S(2)}, u32[]{:S(2)}) collective-permute-start(f32[8,128]{1,0:T(8,128)S(1)} %get-tuple-element.16.refs_4_.line_ref.refs_3_), channel_id=1, source_target_pairs={{1,128},{2,129},{3,130},{4,131},{5,132},{6,133},{7,134},{8,135},{9... | collective-permute-start | bytes 12296 | tf_op jit(solution)/shard_map/ppermute | solution.py:578
  15.6 5.7 %collective-permute-start.4 = (f32[8,128]{1,0:T(8,128)S(1)}, f32[8,128]{1,0:T(8,128)S(1)}, u32[]{:S(2)}, u32[]{:S(2)}) collective-permute-start(f32[8,128]{1,0:T(8,128)S(1)} %get-tuple-element.16.refs_4_.line_ref.refs_3_), channel_id=1, source_target_pairs={{0,129},{1,130},{2,131},{3,132},{4,133},{5,134},{6,135},{7,136},{8... | collective-permute-start | bytes 12296 | tf_op jit(solution)/shard_map/ppermute | solution.py:578
  19.7 0.7 copy-start.5
  20.4 1.0 %copy-start.4 = (s32[1,16,2,64]{3,2,1,0:T(2,128)S(1)}, s32[1,16,2,64]{3,2,1,0:T(2,128)}, u32[]{:S(2)}) copy-start(s32[1,16,2,64]{3,2,1,0:T(2,128)} %offsets_ref.3) | copy-start | bytes 24580

commit v4 on v3

--- a/solution.py
+++ b/solution.py
@@ -20,8 +20,9 @@
 COLUMN_OWNER = 17
 COLUMN_NEAR = 19
 COLUMN_FAR = 21
+COLUMN_HELP = 23
 GROUP_LANES = 32
-PARTS = 4
+PARTS = 2
 
 
 def iota(shape, axis):
@@ -47,27 +48,41 @@
 
 
 def pack_kernel(
-    moving_ref, fixed_ref, vert_ref, hori_ref, offsets_ref, near, far, line_ref,
+    moving_ref, fixed_ref, vert_ref, hori_ref, offsets_ref, across_ref, beside_ref, line_ref,
     vert, hori, offsets, sems,
 ):
     rows, cols = hori.shape
     tiles = cols // TILE_W
     length = moving_ref.shape[0] // 2
     part = length // PARTS
-    tail = slice(length, length + rows)
     loads = [
         pltpu.make_async_copy(vert_ref.at[0], vert, sems.at[0]),
         pltpu.make_async_copy(hori_ref.at[0], hori, sems.at[1]),
         pltpu.make_async_copy(offsets_ref.at[0], offsets, sems.at[2]),
     ]
-    arrive = []
-    for n in range(PARTS):
-        at = pl.ds(n * part, part)
-        behind = pl.ds(length + n * part, part)
-        arrive.append(pltpu.make_async_copy(moving_ref.at[at], near.at[at], sems.at[3 + 2 * n]))
-        arrive.append(pltpu.make_async_copy(fixed_ref.at[behind], far.at[at], sems.at[4 + 2 * n]))
-    for copy in loads + arrive:
+    for copy in loads:
         copy.start()
+
+    def features(back, ahead):
+        copies = []
+        for n in range(PARTS):
+            at, behind = pl.ds(n * part, part), pl.ds(length + n * part, part)
+            copies.append(pltpu.make_async_copy(moving_ref.at[at], back.at[at], sems.at[3 + 2 * n]))
+            copies.append(pltpu.make_async_copy(fixed_ref.at[behind], ahead.at[at], sems.at[4 + 2 * n]))
+        return copies
+
+    first = lax.axis_index("core") == 0
+
+    @pl.when(first)
+    def _():
+        for copy in features(across_ref, beside_ref):
+            copy.start()
+
+    @pl.when(jnp.logical_not(first))
+    def _():
+        for copy in features(beside_ref, across_ref):
+            copy.start()
+
     for copy in loads:
         copy.wait()
     lane = iota((rows, TILE_W), 1)
@@ -82,13 +97,12 @@
     half = offsets.shape[0] // 2
     shifts = jnp.concatenate([offsets[half:, 0, :], offsets[half:, 1, :]], 1).astype(F32)
     blank = jnp.zeros((tiles, TILE_W), F32)
-    for n, value in enumerate(three_parts(line_ref[...])):
-        span = slice(n * TILE_W, (n + 1) * TILE_W)
-        near[tail, span] = jnp.concatenate([value, blank], 0).astype(jnp.bfloat16)
-        far[tail, span] = jnp.concatenate([value, blank if n else shifts], 0).astype(jnp.bfloat16)
-    for block in (near, far):
-        block[tail, 3 * TILE_W :] = columns.astype(jnp.bfloat16)
-    for copy in arrive:
+    for ref in (across_ref, beside_ref):
+        for n, value in enumerate(three_parts(line_ref[...])):
+            block = jnp.concatenate([value, blank if n else shifts], 0)
+            ref[length:, n * TILE_W : (n + 1) * TILE_W] = block.astype(jnp.bfloat16)
+        ref[length:, 3 * TILE_W :] = columns.astype(jnp.bfloat16)
+    for copy in features(across_ref, beside_ref):
         copy.wait()
 
 
@@ -101,34 +115,28 @@
     return line, columns, parts[0][tiles:]
 
 
-def border_kernel(groups, owner_ref, counts_ref, vert_ref, hori_ref, line_ref, above_ref, out_ref, stack):
+def border_kernel(groups, owner_ref, counts_ref, vert_ref, hori_ref, line_ref, out_ref, firsts_ref, right_ref, stack):
     rows, cols = hori_ref.shape
     tiles = cols // TILE_W
     last_group = lax.axis_index("group") == groups - 1
     bottom = jnp.where(last_group, 1.0, 4.0).astype(F32)
 
     v_last = line_ref[...]
-    v_above = above_ref[...]
     for j in range(tiles):
         span = slice(j * TILE_W, (j + 1) * TILE_W)
         stack[j : j + 1, :] = vert_ref[rows - 2 : rows - 1, span]
-        stack[tiles + j : tiles + j + 1, :] = vert_ref[0:1, span]
-        stack[2 * tiles + j : 2 * tiles + j + 1, :] = hori_ref[rows - 1 : rows, span]
-        stack[3 * tiles + j : 3 * tiles + j + 1, :] = hori_ref[0:1, span]
-    v_second, v_first = stack[0:tiles, :], stack[tiles : 2 * tiles, :]
-    h_last, h_first = stack[2 * tiles : 3 * tiles, :], stack[3 * tiles : 4 * tiles, :]
+        stack[tiles + j : tiles + j + 1, :] = hori_ref[rows - 1 : rows, span]
+        firsts_ref[j : j + 1, :] = vert_ref[0:1, span]
+        firsts_ref[tiles + j : tiles + j + 1, :] = hori_ref[0:1, span]
+    v_second, h_last = stack[0:tiles, :], stack[tiles : 2 * tiles, :]
     lane = iota((tiles, TILE_W), 1)
     inside = lane < TILE_W - 1
     square = v_last * v_last
     step_last = v_last - pltpu.roll(v_last, TILE_W - 1, 1)
-    step_above = v_above - pltpu.roll(v_above, TILE_W - 1, 1)
     dh = lane_sum(
         bottom * square * v_last
         + v_second * square
         + jnp.where(inside, h_last * step_last * step_last, 0.0)
-    )
-    dt = lane_sum(
-        v_first * v_above * v_above + jnp.where(inside, h_first * step_above * step_above, 0.0)
     )
     sub = iota((tiles, TILE_W), 0)
     table = jnp.zeros((tiles, TILE_W), F32)
@@ -140,7 +148,6 @@
         (COLUMN_KH, lane_sum(v_last)),
         (COLUMN_K2H, lane_sum(square)),
         (COLUMN_DH, dh),
-        (COLUMN_DT, dt),
     ):
         table = jnp.where(lane == column, value, table)
 
@@ -161,14 +168,6 @@
             at = j * TILE_W + column
             value = jnp.where(tall == j, ref[:, at : at + 1], value)
         picked[name] = value
-    wide = iota((tiles, TILE_W), 0)
-    diagonal = iota((tiles, TILE_W), 1) == wide
-
-    def above_at(column):
-        return row_sum(jnp.where(diagonal, v_above[:, column : column + 1], 0.0))
-
-    a0, a1 = above_at(0), above_at(1)
-    a126, a127 = above_at(TILE_W - 2), above_at(TILE_W - 1)
     right = picked["h127"]
     left = pltpu.roll(right, 1, 1)
     row = iota((rows, TILE_W), 0)
@@ -201,11 +200,10 @@
         at(h0, end) * (at(v0, end) - at(v1, end)) * at(left, end)
         + at(v0, pre) * at(v0, end) * (at(left, end) - at(left, pre))
     )
-    xtr = -(
-        at(h126, 0) * (a127 - a126) * at(right, 0)
-        + at(v127, 0) * a127 * (at(right, 0) - at(right, 1))
-    )
-    xtl = at(h0, 0) * (a0 - a1) * at(left, 0) + at(v0, 0) * a0 * (at(left, 0) - at(left, 1))
+    along_last, along_first = at(h126, 0) * at(right, 0), at(h0, 0) * at(left, 0)
+    fall_last = at(v127, 0) * (at(right, 0) - at(right, 1))
+    fall_first = at(v0, 0) * (at(left, 0) - at(left, 1))
+    right_ref[...] = right
     stack[...] = jnp.zeros_like(stack)
     for column, value in (
         (COLUMN_KV, row_sum(right)),
@@ -217,94 +215,124 @@
         (COLUMN_DV, dv),
         (COLUMN_XBR, xbr),
         (COLUMN_XBL, xbl),
-        (COLUMN_XTR, xtr),
-        (COLUMN_XTL, xtl),
+        (COLUMN_HELP, -along_last - fall_last),
+        (COLUMN_HELP + 1, along_last),
+        (COLUMN_HELP + 2, along_first + fall_first),
+        (COLUMN_HELP + 3, -along_first),
     ):
         stack[column : column + 1, :] = value
     turned = jnp.transpose(stack[...])[0:tiles, :]
-    out_ref[...] = jnp.where(lane <= COLUMN_XTL, turned, table)
+    upright = (lane <= COLUMN_XTL) | (lane >= COLUMN_HELP)
+    out_ref[...] = jnp.where(upright, turned, table)
 
 
 def match_kernel(
-    fixed_ref, moving_ref, offsets_ref, table_ref, line_ref, hori_ref, near_ref, far_ref,
-    out_ref, next_line_ref, next_columns_ref, prev_line_ref, prev_columns_ref,
-    scores_ref,
+    fixed_ref, moving_ref, offsets_ref, table_ref, firsts_ref, right_ref, line_ref, above_ref, across_ref, beside_ref,
+    out_ref, lines_ref, next_columns_ref, prev_columns_ref, scores_ref, shifts_ref,
 ):
     patches, flow, corr = fixed_ref.shape[1:]
     half = patches // 2
-    length = half * flow
-    rows, cols = hori_ref.shape[-2:]
-    tiles = cols // TILE_W
+    rows = right_ref.shape[0]
+    tiles = line_ref.shape[0]
     pair = 2 * flow
     lower = iota((flow, pair), 1) < flow
-    for side in range(2):
-        for first in range(0, half, 2):
-            at = slice(first * flow, (first + 2) * flow)
-            if side == 0:
-                fixed = fixed_ref[0, first : first + 2].reshape(pair, corr)
-                moving = near_ref[at, :]
+
+    def receive(near_ref, far_ref):
+        for first in range(0, patches, 2):
+            own = slice(first, first + 2)
+            if first < half:
+                fixed = fixed_ref[0, own].reshape(pair, corr)
+                moving = near_ref[first * flow : (first + 2) * flow, :]
             else:
-                fixed = far_ref[at, :]
-                moving = moving_ref[0, half + first : half + first + 2].reshape(pair, corr)
-            scores = lax.dot_general(
-                moving, fixed, (((1,), (1,)), ((), ())), preferred_element_type=F32
+                fixed = far_ref[(first - half) * flow : (first + 2 - half) * flow, :]
+                moving = moving_ref[0, own].reshape(pair, corr)
+            scores = lax.dot_general(moving, fixed, (((1,), (1,)), ((), ())), preferred_element_type=F32)
+            scores_ref[:, first * flow : (first + 2) * flow] = jnp.where(
+                lower, scores[0:flow, :], scores[flow:pair, :]
             )
-            scores_ref[side, :, at] = jnp.where(lower, scores[0:flow, :], scores[flow:pair, :])
-    next_line, next_columns, _ = unpack(near_ref[length : length + rows, :], tiles)
-    prev_line, prev_columns, shifts = unpack(far_ref[length : length + rows, :], tiles)
-    next_line_ref[...] = next_line
-    next_columns_ref[...] = next_columns
-    prev_line_ref[...] = prev_line
-    prev_columns_ref[...] = prev_columns
+        next_line, next_columns, _ = unpack(near_ref[half * flow :, :], tiles)
+        prev_line, prev_columns, shifts = unpack(far_ref[half * flow :, :], tiles)
+        lines_ref[0:tiles, :] = next_line
+        lines_ref[tiles:, :] = prev_line
+        next_columns_ref[...] = next_columns
+        prev_columns_ref[...] = prev_columns
+        shifts_ref[...] = shifts
+
+    first_core = lax.axis_index("core") == 0
+
+    @pl.when(first_core)
+    def _():
+        receive(beside_ref, across_ref)
+
+    @pl.when(jnp.logical_not(first_core))
+    def _():
+        receive(across_ref, beside_ref)
+
+    next_line, next_columns, shifts = lines_ref[0:tiles, :], next_columns_ref[...], shifts_ref[...]
+    scores = scores_ref[...]
+    top = jnp.max(scores, axis=0, keepdims=True)
+    likely = jnp.exp((scores - top) * (1.0 / math.sqrt(corr)))
+    offsets = []
+    for k in range(2):
+        offsets.append(offsets_ref[0, 0:half, k, :].astype(F32))
+        offsets.append(shifts[:, k * flow : (k + 1) * flow])
+    sums = lax.dot_general(
+        jnp.concatenate(offsets, 0),
+        likely,
+        (((1,), (0,)), ((), ())),
+        precision=lax.Precision.HIGHEST,
+        preferred_element_type=F32,
+    )
+    weight = row_sum(likely) * flow
+    mine = lax.rem(iota(sums.shape, 0), patches) == lax.div(iota(sums.shape, 1), flow)
+    ratio = lane_sum(jnp.where(mine, sums, 0.0) / weight)
 
     table = table_ref[...]
     lane = iota(table.shape, 1)
-    own_shifts = [offsets_ref[0, 0:half, k, :].astype(F32) for k in range(2)]
-    far_shifts = [shifts[:, 0:flow], shifts[:, flow:pair]]
-    scale = 1.0 / math.sqrt(corr)
-    slot = lax.rem(iota((2 * half, length), 0), half)
-    mine = slot == lax.div(iota((2 * half, length), 1), flow)
-    for side, offsets in enumerate((own_shifts, far_shifts)):
-        both = scores_ref[side]
-        top = jnp.max(both, axis=0, keepdims=True)
-        likely = jnp.exp((both - top) * scale)
-        sums = lax.dot_general(
-            jnp.concatenate(offsets, 0),
-            likely,
-            (((1,), (0,)), ((), ())),
-            precision=lax.Precision.HIGHEST,
-            preferred_element_type=F32,
-        )
-        weight = row_sum(likely)
-        ratio = lane_sum(jnp.where(mine, sums, 0.0) / (weight * flow))
-        for k in range(2):
-            column = (COLUMN_FAR if side else COLUMN_NEAR) + k
-            table = jnp.where(lane == column, ratio[k * half : (k + 1) * half], table)
-
-    table = jnp.where(lane == COLUMN_KXH, lane_sum(line_ref[...] * next_line), table)
+
+    def helper(n):
+        return table[:, COLUMN_HELP + n : COLUMN_HELP + n + 1]
+
+    line, above = line_ref[...], above_ref[...]
+    step = above - pltpu.roll(above, TILE_W - 1, 1)
+    top_energy = firsts_ref[0:tiles, :] * above * above + jnp.where(
+        lane < TILE_W - 1, firsts_ref[tiles:, :] * step * step, 0.0
+    )
     diagonal = iota(table.shape, 0) == lane
-    columns = jnp.zeros((rows, TILE_W), F32)
-    tall = iota((rows, TILE_W), 1)
-    for j in range(tiles):
-        end = (j + 1) * TILE_W - 1
-        columns = jnp.where(tall == j, hori_ref[:, end : end + 1], columns)
-    across = row_sum(columns * next_columns)
-    table = jnp.where(lane == COLUMN_KXV, lane_sum(jnp.where(diagonal, across, 0.0)), table)
-
-    table = jnp.where(lane < GROUP_LANES, table, 0.0)
+    across = row_sum(right_ref[...] * next_columns)
+    columns = [
+        (COLUMN_XTR, above[:, TILE_W - 1 :] * helper(0) + above[:, TILE_W - 2 : TILE_W - 1] * helper(1)),
+        (COLUMN_XTL, above[:, 0:1] * helper(2) + above[:, 1:2] * helper(3)),
+        (COLUMN_DT, lane_sum(top_energy)),
+        (COLUMN_KXH, lane_sum(line * next_line)),
+        (COLUMN_KXV, lane_sum(jnp.where(diagonal, across, 0.0))),
+    ]
+    for k in range(2):
+        columns.append((COLUMN_NEAR + k, ratio[2 * k * half : (2 * k + 1) * half]))
+        columns.append((COLUMN_FAR + k, ratio[(2 * k + 1) * half : (2 * k + 2) * half]))
+    for column, value in columns:
+        table = jnp.where(lane == column, value, table)
+
+    table = jnp.where(lane < COLUMN_HELP, table, 0.0)
     per_row = TILE_W // GROUP_LANES
     for part in range(tiles // per_row):
-        line = jnp.zeros((1, TILE_W), F32)
+        packed = jnp.zeros((1, TILE_W), F32)
         for j in range(per_row):
             source = table[part * per_row + j : part * per_row + j + 1, :]
-            line = line + (pltpu.roll(source, j * GROUP_LANES, 1) if j else source)
+            packed = packed + (pltpu.roll(source, j * GROUP_LANES, 1) if j else source)
         for n in range(out_ref.shape[0]):
-            out_ref[n, part : part + 1, :] = line
+            out_ref[n, part : part + 1, :] = packed
+
+
+def copies_kernel(seen_ref, out_ref):
+    seen = seen_ref[...]
+    for n in range(out_ref.shape[0]):
+        out_ref[n] = seen
 
 
 def stack_kernel(
     dims, seen_ref, vert_ref, hori_ref, own_line_ref, own_above_ref,
-    next_line_ref, next_above_ref, next_columns_ref, prev_line_ref, prev_above_ref, prev_columns_ref,
+    lines_ref, aboves_ref, next_columns_ref, prev_columns_ref,
     disp_ref, res_ref, rows_ref, turn_ref, sums_ref, out_ref, field_ref,
 ):
     groups, sections, rows, tiles, chips_z = dims
@@ -510,8 +538,8 @@
     own_line, own_above = own_line_ref[...], own_above_ref[...]
     next_columns, prev_columns = next_columns_ref[...], prev_columns_ref[...]
     own_edges = (own_line, own_above, lambda j: hori_ref[:, (j + 1) * TILE_W - 1 : (j + 1) * TILE_W])
-    next_edges = (next_line_ref[...], next_above_ref[...], lambda j: next_columns[:, j : j + 1])
-    prev_edges = (prev_line_ref[...], prev_above_ref[...], lambda j: prev_columns[:, j : j + 1])
+    next_edges = (lines_ref[0:tiles, :], aboves_ref[0:tiles, :], lambda j: next_columns[:, j : j + 1])
+    prev_edges = (lines_ref[tiles:, :], aboves_ref[tiles:, :], lambda j: prev_columns[:, j : j + 1])
     for k in range(2):
         for j in range(tiles):
             span = slice(j * TILE_W, (j + 1) * TILE_W)
@@ -567,21 +595,11 @@
     return lax.ppermute(block, axis, route)
 
 
-def from_above(block, distance):
-    groups, sections = lax.axis_size("group"), lax.axis_size(SEC)
-    route = [
-        ((g - 1) * sections + s - distance, g * sections + s)
-        for g in range(1, groups)
-        for s in range(sections)
-        if 0 <= s - distance < sections
-    ]
-    return lax.ppermute(block, ("group",) + SEC, route)
-
-
-def gather(block, axis):
-    size = lax.axis_size(axis)
-    copies = jnp.broadcast_to(block[None], (size,) + block.shape)
-    return lax.all_to_all(copies, axis, 0, 0, tiled=True)
+def swap(block, first):
+    route = []
+    for s in range(first, lax.axis_size(SEC) - 1, 2):
+        route += [(s, s + 1), (s + 1, s)]
+    return lax.ppermute(block, SEC, route)
 
 
 def body(fixed_desc, moving_desc, offsets, owner, counts, vert, hori):
@@ -598,12 +616,13 @@
     local = pl.BlockSpec(memory_space=pltpu.VMEM)
     scalars = pl.BlockSpec(memory_space=pltpu.SMEM)
     modest = pltpu.CompilerParams(vmem_limit_bytes=16 << 20)
-    packed = jax.ShapeDtypeStruct((length // 2 + rows, corr), fixed_desc.dtype)
     border = jax.ShapeDtypeStruct((tiles, TILE_W), F32)
     upright = jax.ShapeDtypeStruct((rows, TILE_W), F32)
-    near, far, line = pl.pallas_call(
+    lines_shape = jax.ShapeDtypeStruct((2 * tiles, TILE_W), F32)
+    packed = pltpu.VMEM((length // 2 + rows, corr), fixed_desc.dtype)
+    across, beside, line = pl.pallas_call(
         pack_kernel,
-        out_shape=(in_vmem(packed), in_vmem(packed), in_vmem(border)),
+        out_shape=(packed, packed, in_vmem(border)),
         in_specs=[hbm] * 5,
         out_specs=(local,) * 3,
         scratch_shapes=[
@@ -620,40 +639,50 @@
             for x in (moving_desc.reshape(length, corr), fixed_desc.reshape(length, corr), vert, hori, offsets)
         )
     )
-    near = from_behind(near, SEC, -1)
-    far = from_behind(far, SEC, 1)
-    above = from_above(line, 0)
-    next_above = from_above(line, -1)
-    prev_above = from_above(line, 1)
+    across = swap(across, 1)
+    beside = swap(beside, 0)
+    above = from_behind(line, "group", 1)
 
     vert, hori = vert[0], hori[0]
 
     def borders(*refs):
         border_kernel(groups, *refs)
 
-    table = pl.pallas_call(
+    table, firsts, right = pl.pallas_call(
         borders,
-        out_shape=border,
-        in_specs=[scalars] * 2 + [local] * 4,
+        out_shape=(in_vmem(border), in_vmem(lines_shape), in_vmem(upright)),
+        in_specs=[scalars] * 2 + [local] * 3,
+        out_specs=(local,) * 3,
         scratch_shapes=[pltpu.VMEM((TILE_W, TILE_W), F32)],
         compiler_params=modest,
         name="borders",
-    )(owner, counts, vert, hori, line, above)
-    near, far, next_above, prev_above = lax.optimization_barrier((near, far, next_above, prev_above))
-    mine, next_line, next_columns, prev_line, prev_columns = pl.pallas_call(
+    )(owner, counts, vert, hori, line)
+    mine, lines, next_columns, prev_columns = pl.pallas_call(
         match_kernel,
         out_shape=(
-            jax.ShapeDtypeStruct((chips_z, halves, TILE_W), F32), border, upright, border, upright,
+            pltpu.VMEM((chips_z, halves, TILE_W), F32),
+            in_vmem(lines_shape), in_vmem(upright), in_vmem(upright),
         ),
-        in_specs=[local] * 8,
-        out_specs=(local,) * 5,
-        scratch_shapes=[pltpu.VMEM((2, flow, length // 2), F32)],
+        in_specs=[local] * 10,
+        out_specs=(local,) * 4,
+        scratch_shapes=[pltpu.VMEM((flow, length), F32), pltpu.VMEM((tiles, TILE_W), F32)],
         compiler_params=modest,
         name="match",
-    )(fixed_desc, moving_desc, offsets, table, line, hori, near, far)
+    )(fixed_desc, moving_desc, offsets, table, firsts, right, line, above, across, beside)
 
     seen = lax.all_to_all(mine, "z", 0, 0, tiled=True).reshape(-1, TILE_W)
-    seen = gather(seen, ("group", "y")).reshape(-1, TILE_W)
+    lines, seen = lax.optimization_barrier((lines, seen))
+    aboves = from_behind(lines, "group", 1)
+    peers = groups * lax.axis_size("y")
+    copies = pl.pallas_call(
+        copies_kernel,
+        out_shape=pltpu.VMEM((peers,) + seen.shape, F32),
+        in_specs=[local],
+        out_specs=local,
+        compiler_params=modest,
+        name="copies",
+    )(seen)
+    seen = lax.all_to_all(copies, ("group", "y"), 0, 0, tiled=True).reshape(-1, TILE_W)
     seen = lax.all_gather(seen, "core", axis=0, tiled=True)
 
     dims = (groups, sections, rows, tiles, chips_z)
@@ -666,7 +695,7 @@
     displacement, residual = pl.pallas_call(
         both_iterations,
         out_shape=(field, field),
-        in_specs=[local] * 11,
+        in_specs=[local] * 9,
         scratch_shapes=[
             pltpu.VMEM((groups * halves, sections, TILE_W), F32),
             pltpu.VMEM((groups, halves * TILE_W, sections), F32),
@@ -676,10 +705,7 @@
         ],
         compiler_params=modest,
         name="stack",
-    )(
-        seen, vert, hori, line, above,
-        next_line, next_above, next_columns, prev_line, prev_above, prev_columns,
-    )
+    )(seen, vert, hori, line, above, lines, aboves, next_columns, prev_columns)
     return (displacement[None], residual[None])
 
 

time: 74 us -> 64.8 us (0.88)
  blocking collectives: 48.7 us -> 30.3 us
  starting transfers between devices: 16.8 us -> 21 us
  waiting for transfers between devices: 0.04 us -> 4.19 us
  Pallas kernels: 6.05 us -> 6.85 us
    all_to_all x1 -> x0, blocking collectives: 16.4 us -> none  [gather(): return lax.all_to_all(copies, axis, 0, 0, tiled=True)]
    all_to_all x0 -> x1, starting transfers between devices: none -> 6.97 us  [body(): lax.all_to_all(copies, ('group', 'y'), 0, 0, tiled=True).reshape(-1, TILE_W)]
    ppermute x2, starting transfers between devices: 10.7 us -> 4.55 us  [from_behind(): return lax.ppermute(block, axis, route)]
    all_to_all x0 -> x1, waiting for transfers between devices: none -> 4.16 us  [body(): lax.all_to_all(copies, ('group', 'y'), 0, 0, tiled=True).reshape(-1, TILE_W)]
    ppermute x3 -> x2, starting transfers between devices: 6.05 us -> 9.48 us  [swap(): return lax.ppermute(block, SEC, route)]
    all_gather x1, blocking collectives: 6.13 us -> 4.09 us  [body(): seen = lax.all_gather(seen, 'core', axis=0, tiled=True)]
    pallas_call x3 -> x4, Pallas kernels: 3.22 us -> 4.02 us  [the longest x1 1.48 us: body(): pl.pallas_call(pack_kernel, out_shape=(packed, packed, in_vmem(border)),...]
  transfers between devices with their start and end apart: 5 -> 5, of which waited for: 0 -> 1; matrix products, arithmetic and copies ran while one was open for 0% -> 0% of each run, Pallas kernels for 1% -> 1%
where the time goes in v4:
time: 64.8 us; the launch traced here: 64.4 us
  blocking collectives  30.3 us (47%)
  starting transfers between devices  21 us (32%)
  Pallas kernels  6.85 us (11%)
  waiting for transfers between devices  4.19 us (6%)
  between operations  1.42 us (2%)
  local copies, waits for them, and re-layouts  0.65 us (1%)
    all_to_all x1, blocking collectives, body(): seen = lax.all_to_all(mine, 'z', 0, 0, tiled=True).reshape(-1, TILE_W)  26.2 us
    ppermute x2, starting transfers between devices, swap(): return lax.ppermute(block, SEC, route)  9.48 us
    all_to_all x1, starting transfers between devices, body(): lax.all_to_all(copies, ('group', 'y'), 0, 0, tiled=True).reshape(-1, TILE_W)  6.97 us
    ppermute x2, starting transfers between devices, from_behind(): return lax.ppermute(block, axis, route)  4.55 us
    all_to_all x1, waiting for transfers between devices, body(): lax.all_to_all(copies, ('group', 'y'), 0, 0, tiled=True).reshape(-1, TILE_W)  4.16 us
    all_gather x1, blocking collectives, body(): seen = lax.all_gather(seen, 'core', axis=0, tiled=True)  4.09 us
    pallas_call x1, Pallas kernels, body(): pl.pallas_call(both_iterations, out_shape=(field, field), in_specs=[local...  2.83 us
    pallas_call x1, Pallas kernels, body(): pl.pallas_call(pack_kernel, out_shape=(packed, packed, in_vmem(border)),...  1.48 us
  transfers between devices with their start and end apart: 5, of which 1 were waited for; matrix products, arithmetic and copies ran while one was open for 0% of the time, Pallas kernels for 1%

profile of v4, /device:TPU:1, one launch (start us, length us, event | category | flops | bytes accessed | tf_op | source)
XLA Modules:
  0.0 64.4 jit_solution(13919232281109032588)
XLA Ops:
  0.7 1.5 %pack.1 = (bf16[528,512]{1,0:T(8,128)(2,1)S(1)}, bf16[528,512]{1,0:T(8,128)(2,1)S(1)}, f32[8,128]{1,0:T(8,128)S(1)}) custom-call(bf16[1024,512]{1,0:T(8,128)(2,1)} %bitcast.9, bf16[1024,512]{1,0:T(8,128)(2,1)} %bitcast.8, f32[1,16,1024]{2,1,0:T(8,128)} %vert_ref.1, f32[1,16,1024]{2,1,0:T(8,128)} %hori_ref.1, s32[1,16,2,64]{3,2,1,0:T(2,128)} %offsets_ref.3), custom_call_target="tpu_custom_call" | custom-call | tf_op jit(solution)/shard_map/pack/pallas_call | solution.py:623
  2.2 4.6 %collective-permute-start.1 = (bf16[528,512]{1,0:T(8,128)(2,1)S(1)}, bf16[528,512]{1,0:T(8,128)(2,1)S(1)}, u32[]{:S(2)}, u32[]{:S(2)}) collective-permute-start(bf16[528,512]{1,0:T(8,128)(2,1)S(1)} %get-tuple-element.20), channel_id=1, source_target_pairs={{1,2},{2,1},{3,4},{4,3},{5,6},{6,5},{7,8},{8,7},{9,10},{10,9},{11,... | collective-permute-start | bytes 1622024 | tf_op jit(solution)/shard_map/ppermute | solution.py:602
  6.8 4.9 %collective-permute-start.2 = (bf16[528,512]{1,0:T(8,128)(2,1)S(1)}, bf16[528,512]{1,0:T(8,128)(2,1)S(1)}, u32[]{:S(2)}, u32[]{:S(2)}) collective-permute-start(bf16[528,512]{1,0:T(8,128)(2,1)S(1)} %get-tuple-element.21), channel_id=1, source_target_pairs={{0,1},{1,0},{2,3},{3,2},{4,5},{5,4},{6,7},{7,6},{8,9},{9,8},{10,11... | collective-permute-start | bytes 1622024 | tf_op jit(solution)/shard_map/ppermute | solution.py:602
  11.7 1.3 %collective-permute-start = (f32[8,128]{1,0:T(8,128)S(1)}, f32[8,128]{1,0:T(8,128)S(1)}, u32[]{:S(2)}, u32[]{:S(2)}) collective-permute-start(f32[8,128]{1,0:T(8,128)S(1)} %get-tuple-element.16.refs_4_.line_ref.refs_3_), channel_id=1, source_target_pairs={{0,128},{128,256},{256,384},{1,129},{129,257},{257,385},{2,130},{1... | collective-permute-start | bytes 12296 | tf_op jit(solution)/shard_map/ppermute | solution.py:595
  13.6 0.0 copy-start.5
  13.6 0.0 copy-done.2
  13.6 0.0 copy-done.3
  13.6 0.6 copy-done.5
  14.3 0.9 %borders.1 = (f32[8,128]{1,0:T(8,128)S(1)}, f32[16,128]{1,0:T(8,128)S(1)}, f32[16,128]{1,0:T(8,128)S(1)}) custom-call(s32[1,16]{1,0:T(1,128)S(1)} %copy-done.5, s32[1,1]{1,0:T(1,128)S(6)} %copy.9.refs_1_, f32[16,1024]{1,0:T(8,128)S(1)} %bitcast.10, f32[16,1024]{1,0:T(8,128)S(1)} %bitcast.12, f32[8,128]{1,0:T(8,128)S(1)} %get-tuple-element.16.refs_4_.line_ref.refs_3_), custom_call_target="tpu_custom_call" | custom-call | tf_op jit(solution)/shard_map/borders/pallas_call | solution.py:651
  15.1 0.0 collective-permute-done.above_ref.refs_4_
  15.1 0.0 collective-permute-done.1.across_ref
  15.2 0.0 collective-permute-done.2.beside_ref
  15.2 0.0 copy-done
  15.2 0.0 copy-done.1
  15.2 0.0 copy-done.4
  15.2 0.9 %match.1 = (f32[16,2,128]{2,1,0:T(2,128)S(1)}, f32[16,128]{1,0:T(8,128)S(1)}, f32[16,128]{1,0:T(8,128)S(1)}, f32[16,128]{1,0:T(8,128)S(1)}) custom-call(bf16[1,16,64,512]{3,2,1,0:T(8,128)(2,1)S(1)} %copy-done, bf16[1,16,64,512]{3,2,1,0:T(8,128)(2,1)S(1)} %copy-done.1, s32[1,16,2,64]{3,2,1,0:T(2,128)S(1)} %copy-done.4, ...), custom_call_target="tpu_custom_call" | custom-call | tf_op jit(solution)/shard_map/match/pallas_call | solution.py:660
  16.1 26.2 %all_to_all.10 = f32[16,2,128]{2,1,0:T(2,128)S(1)} all-to-all(f32[16,2,128]{2,1,0:T(2,128)S(1)} %get-tuple-element.23), channel_id=1, replica_groups=mesh['group'=4,'z'=16,'y'=4,'core'=2] {'z'}, dimensions={0} | all-to-all | bytes 32768 | tf_op jit(solution)/shard_map/all_to_all | solution.py:673
  42.4 0.7 %copies.1 = f32[16,32,128]{2,1,0:T(8,128)} custom-call(f32[32,128]{1,0:T(8,128)S(1)} %bitcast.14), custom_call_target="tpu_custom_call" | custom-call | tf_op jit(solution)/shard_map/copies/pallas_call | solution.py:677
  43.1 7.0 %all-to-all-start.1 = ((f32[16,32,128]{2,1,0:T(8,128)}), f32[16,32,128]{2,1,0:T(8,128)S(1)}, u32[]{:S(2)}, u32[]{:S(2)}) async-start(f32[16,32,128]{2,1,0:T(8,128)} %copies.1), calls=%async_computation.1 | async-start | bytes 524288 | tf_op jit(solution)/shard_map/all_to_all | solution.py:685
  50.1 3.3 %collective-permute-start.3 = (f32[16,128]{1,0:T(8,128)S(1)}, f32[16,128]{1,0:T(8,128)S(1)}, u32[]{:S(2)}, u32[]{:S(2)}) collective-permute-start(f32[16,128]{1,0:T(8,128)S(1)} %get-tuple-element.25.refs_5_), channel_id=1, source_target_pairs={{0,128},{128,256},{256,384},{1,129},{129,257},{257,385},{2,130},{1... | collective-permute-start | bytes 24584 | tf_op jit(solution)/shard_map/ppermute | solution.py:595
  53.3 4.2 %all-to-all-done.1 = f32[16,32,128]{2,1,0:T(8,128)S(1)} async-done(((f32[16,32,128]{2,1,0:T(8,128)}), f32[16,32,128]{2,1,0:T(8,128)S(1)}, u32[]{:S(2)}, u32[]{:S(2)}) %all-to-all-start.1) | async-done | bytes 262176 | tf_op jit(solution)/shard_map/all_to_all | solution.py:685
  57.5 4.1 %all_gather.3.refs_0_ = f32[1024,128]{1,0:T(8,128)S(1)} all-gather(f32[512,128]{1,0:T(8,128)S(1)} %bitcast.15), channel_id=1, replica_groups=mesh['group'=4,'z'=16,'y'=4,'core'=2] {'core'}, dimensions={0}, use_global_device_ids=true | all-gather | bytes 786432 | tf_op jit(solution)/shard_map/all_gather | solution.py:686
  61.6 0.0 collective-permute-done.3.refs_6_
  61.6 2.8 %stack.1 = (f32[2,16,1024]{2,1,0:T(8,128)}, f32[2,16,1024]{2,1,0:T(8,128)}) custom-call(f32[1024,128]{1,0:T(8,128)S(1)} %all_gather.3.refs_0_, f32[16,1024]{1,0:T(8,128)S(1)} %bitcast.11, f32[16,1024]{1,0:T(8,128)S(1)} %bitcast.13, f32[8,128]{1,0:T(8,128)S(1)} %get-tuple-element.16.refs_4_.line_ref.refs_3_, ...), custom_call_target="tpu_custom_call" | custom-call | tf_op jit(solution)/shard_map/stack/pallas_call | solution.py:695
  (5 shorter events, 0.0 us)
Async XLA Ops:
  0.6 13.0 %copy-start.2 = (f32[1,16,1024]{2,1,0:T(8,128)S(1)}, f32[1,16,1024]{2,1,0:T(8,128)}, u32[]{:S(2)}) copy-start(f32[1,16,1024]{2,1,0:T(8,128)} %vert_ref.1) | copy-start | bytes 196612
  0.6 13.0 %copy-start.3 = (f32[1,16,1024]{2,1,0:T(8,128)S(1)}, f32[1,16,1024]{2,1,0:T(8,128)}, u32[]{:S(2)}) copy-start(f32[1,16,1024]{2,1,0:T(8,128)} %hori_ref.1) | copy-start | bytes 196612
  0.7 14.5 %copy-start = (bf16[1,16,64,512]{3,2,1,0:T(8,128)(2,1)S(1)}, bf16[1,16,64,512]{3,2,1,0:T(8,128)(2,1)}, u32[]{:S(2)}) copy-start(bf16[1,16,64,512]{3,2,1,0:T(8,128)(2,1)} %fixed_ref.1) | copy-start | bytes 3145732
  0.7 14.5 %copy-start.1 = (bf16[1,16,64,512]{3,2,1,0:T(8,128)(2,1)S(1)}, bf16[1,16,64,512]{3,2,1,0:T(8,128)(2,1)}, u32[]{:S(2)}) copy-start(bf16[1,16,64,512]{3,2,1,0:T(8,128)(2,1)} %moving_ref.1) | copy-start | bytes 3145732
  2.2 13.0 %collective-permute-start.1 = (bf16[528,512]{1,0:T(8,128)(2,1)S(1)}, bf16[528,512]{1,0:T(8,128)(2,1)S(1)}, u32[]{:S(2)}, u32[]{:S(2)}) collective-permute-start(bf16[528,512]{1,0:T(8,128)(2,1)S(1)} %get-tuple-element.20), channel_id=1, source_target_pairs={{1,2},{2,1},{3,4},{4,3},{5,6},{6,5},{7,8},{8,7},{9,10},{10,9},{11,... | collective-permute-start | bytes 1622024 | tf_op jit(solution)/shard_map/ppermute | solution.py:602
  6.8 8.4 %collective-permute-start.2 = (bf16[528,512]{1,0:T(8,128)(2,1)S(1)}, bf16[528,512]{1,0:T(8,128)(2,1)S(1)}, u32[]{:S(2)}, u32[]{:S(2)}) collective-permute-start(bf16[528,512]{1,0:T(8,128)(2,1)S(1)} %get-tuple-element.21), channel_id=1, source_target_pairs={{0,1},{1,0},{2,3},{3,2},{4,5},{5,4},{6,7},{7,6},{8,9},{9,8},{10,11... | collective-permute-start | bytes 1622024 | tf_op jit(solution)/shard_map/ppermute | solution.py:602
  11.7 3.5 %collective-permute-start = (f32[8,128]{1,0:T(8,128)S(1)}, f32[8,128]{1,0:T(8,128)S(1)}, u32[]{:S(2)}, u32[]{:S(2)}) collective-permute-start(f32[8,128]{1,0:T(8,128)S(1)} %get-tuple-element.16.refs_4_.line_ref.refs_3_), channel_id=1, source_target_pairs={{0,128},{128,256},{256,384},{1,129},{129,257},{257,385},{2,130},{1... | collective-permute-start | bytes 12296 | tf_op jit(solution)/shard_map/ppermute | solution.py:595
  13.6 0.7 %copy-start.5 = (s32[1,16]{1,0:T(1,128)S(1)}, s32[1,16]{1,0:T(1,128)}, u32[]{:S(2)}) copy-start(s32[1,16]{1,0:T(1,128)} %refs_0_.1) | copy-start | bytes 196
  14.3 0.9 %copy-start.4 = (s32[1,16,2,64]{3,2,1,0:T(2,128)S(1)}, s32[1,16,2,64]{3,2,1,0:T(2,128)}, u32[]{:S(2)}) copy-start(s32[1,16,2,64]{3,2,1,0:T(2,128)} %offsets_ref.3) | copy-start | bytes 24580
  43.1 14.4 %all-to-all-start.1 = ((f32[16,32,128]{2,1,0:T(8,128)}), f32[16,32,128]{2,1,0:T(8,128)S(1)}, u32[]{:S(2)}, u32[]{:S(2)}) async-start(f32[16,32,128]{2,1,0:T(8,128)} %copies.1), calls=%async_computation.1 | async-start | bytes 524288 | tf_op jit(solution)/shard_map/all_to_all | solution.py:685
  50.1 11.5 %collective-permute-start.3 = (f32[16,128]{1,0:T(8,128)S(1)}, f32[16,128]{1,0:T(8,128)S(1)}, u32[]{:S(2)}, u32[]{:S(2)}) collective-permute-start(f32[16,128]{1,0:T(8,128)S(1)} %get-tuple-element.25.refs_5_), channel_id=1, source_target_pairs={{0,128},{128,256},{256,384},{1,129},{129,257},{257,385},{2,130},{1... | collective-permute-start | bytes 24584 | tf_op jit(solution)/shard_map/ppermute | solution.py:595

commit v5 on v4

--- a/solution.py
+++ b/solution.py
@@ -21,7 +21,9 @@
 COLUMN_NEAR = 19
 COLUMN_FAR = 21
 COLUMN_HELP = 23
-GROUP_LANES = 32
+GROUP_LANES = 24
+FIRST_GROUP = 2
+FIRST_CHIP = (0, 3)
 PARTS = 2
 
 
@@ -314,20 +316,33 @@
         table = jnp.where(lane == column, value, table)
 
     table = jnp.where(lane < COLUMN_HELP, table, 0.0)
-    per_row = TILE_W // GROUP_LANES
-    for part in range(tiles // per_row):
-        packed = jnp.zeros((1, TILE_W), F32)
-        for j in range(per_row):
-            source = table[part * per_row + j : part * per_row + j + 1, :]
-            packed = packed + (pltpu.roll(source, j * GROUP_LANES, 1) if j else source)
+    pieces = [jnp.zeros((1, TILE_W), F32) for _ in range(out_ref.shape[1])]
+    place = iota((1, TILE_W), 1)
+    for j in range(tiles):
+        part, start = divmod(j * GROUP_LANES, TILE_W)
+        source = table[j : j + 1, :]
+        source = pltpu.roll(source, start, 1) if start else source
+        if start + GROUP_LANES > TILE_W:
+            pieces[part] = pieces[part] + jnp.where(place >= start, source, 0.0)
+            pieces[part + 1] = pieces[part + 1] + jnp.where(place < start, source, 0.0)
+        else:
+            pieces[part] = pieces[part] + source
+    for part, piece in enumerate(pieces):
         for n in range(out_ref.shape[0]):
-            out_ref[n, part : part + 1, :] = packed
+            out_ref[n, part : part + 1, :] = piece
 
 
 def copies_kernel(seen_ref, out_ref):
-    seen = seen_ref[...]
+    chips = seen_ref.shape[0] // 2
+    half = chips // 2
+    first = [seen_ref[pl.ds(n * chips, half, stride=2), :] for n in (1, 0)]
+    low = seen_ref[pl.ds(1 + chips, half, stride=2), :]
+    high = seen_ref[pl.ds(1, half, stride=2), :]
+    second = low + pltpu.roll(high, TILE_W // 2, 1)
     for n in range(out_ref.shape[0]):
-        out_ref[n] = seen
+        out_ref[n, 0:half, :] = first[0]
+        out_ref[n, half:chips, :] = first[1]
+        out_ref[n, chips:, :] = second
 
 
 def stack_kernel(
@@ -337,22 +352,34 @@
 ):
     groups, sections, rows, tiles, chips_z = dims
     per_chip = sections // chips_z
-    halves = tiles * GROUP_LANES // TILE_W
     count = groups * tiles
     nodes = float(rows * TILE_W)
     me, group = lax.axis_index(SEC), lax.axis_index("group")
 
+    shared = chips_z // 2
+    half_lanes = TILE_W // 2
     for core in range(CORES):
         for g in range(groups):
             for y in range(per_chip // CORES):
-                base = ((core * groups + g) * (per_chip // CORES) + y) * chips_z * halves
-                for h in range(halves):
-                    rows_ref[g * halves + h, pl.ds(y * CORES + core, chips_z, stride=per_chip), :] = seen_ref[
-                        pl.ds(base + h, chips_z, stride=halves), :
-                    ]
+                place = core * groups * CHIPS_Y + plane_place(groups, core, g, y)
+                base = place * (chips_z + shared)
+                chip = y * CORES + core
+                rows_ref[g, pl.ds(chip, chips_z, stride=per_chip), :] = seen_ref[base : base + chips_z, :]
+                rows_ref[
+                    groups + g // 2, pl.ds((g % 2) * (sections // 2) + chip, shared, stride=per_chip), :
+                ] = seen_ref[base + chips_z : base + chips_z + shared, :]
+    left_half = iota((half_lanes, sections), 1) < sections // 2
     for g in range(groups):
-        for h in range(halves):
-            turn_ref[g, h * TILE_W : (h + 1) * TILE_W, :] = jnp.transpose(rows_ref[g * halves + h])
+        turn_ref[g, 0:TILE_W, :] = jnp.transpose(rows_ref[g])
+    for pair in range(groups // 2):
+        turned = jnp.transpose(rows_ref[groups + pair])
+        low_half, high_half = turned[0:half_lanes, :], turned[half_lanes:, :]
+        turn_ref[2 * pair, TILE_W:, :] = jnp.where(
+            left_half, low_half, pltpu.roll(high_half, sections // 2, 1)
+        )
+        turn_ref[2 * pair + 1, TILE_W:, :] = jnp.where(
+            left_half, pltpu.roll(low_half, sections // 2, 1), high_half
+        )
 
     def block(g, column):
         return turn_ref[g, pl.ds(column, tiles, stride=GROUP_LANES), :]
@@ -595,6 +622,23 @@
     return lax.ppermute(block, axis, route)
 
 
+def plane_place(groups, core, g, y):
+    return (g - FIRST_GROUP) % groups * CHIPS_Y + (y - FIRST_CHIP[core]) % CHIPS_Y
+
+
+def planes(groups, chips_z):
+    lists = []
+    for z in range(chips_z):
+        for core in range(CORES):
+            members = [None] * (groups * CHIPS_Y)
+            for g in range(groups):
+                for y in range(CHIPS_Y):
+                    device = ((g * chips_z + z) * CHIPS_Y + y) * CORES + core
+                    members[plane_place(groups, core, g, y)] = device
+            lists.append(members)
+    return lists
+
+
 def swap(block, first):
     route = []
     for s in range(first, lax.axis_size(SEC) - 1, 2):
@@ -610,7 +654,7 @@
     rows, cols = vert.shape[1:]
     tiles = cols // TILE_W
     length = patches * flow
-    halves = tiles * GROUP_LANES // TILE_W
+    halves = -(-tiles * GROUP_LANES // TILE_W)
 
     hbm = pl.BlockSpec(memory_space=pltpu.HBM)
     local = pl.BlockSpec(memory_space=pltpu.VMEM)
@@ -670,19 +714,23 @@
         name="match",
     )(fixed_desc, moving_desc, offsets, table, firsts, right, line, above, across, beside)
 
-    seen = lax.all_to_all(mine, "z", 0, 0, tiled=True).reshape(-1, TILE_W)
+    turned = [(z + chips_z // 2) % chips_z for z in range(chips_z)]
+    seen = lax.all_to_all(mine, "z", 0, 0, tiled=True, axis_index_groups=[turned]).reshape(-1, TILE_W)
     lines, seen = lax.optimization_barrier((lines, seen))
     aboves = from_behind(lines, "group", 1)
     peers = groups * lax.axis_size("y")
+    block_rows = chips_z + chips_z // 2
     copies = pl.pallas_call(
         copies_kernel,
-        out_shape=pltpu.VMEM((peers,) + seen.shape, F32),
+        out_shape=jax.ShapeDtypeStruct((peers, block_rows, TILE_W), F32),
         in_specs=[local],
         out_specs=local,
         compiler_params=modest,
         name="copies",
     )(seen)
-    seen = lax.all_to_all(copies, ("group", "y"), 0, 0, tiled=True).reshape(-1, TILE_W)
+    seen = lax.all_to_all(
+        copies, ("group",) + SEC, 0, 0, tiled=True, axis_index_groups=planes(groups, chips_z)
+    ).reshape(-1, TILE_W)
     seen = lax.all_gather(seen, "core", axis=0, tiled=True)
 
     dims = (groups, sections, rows, tiles, chips_z)
@@ -697,8 +745,8 @@
         out_shape=(field, field),
         in_specs=[local] * 9,
         scratch_shapes=[
-            pltpu.VMEM((groups * halves, sections, TILE_W), F32),
-            pltpu.VMEM((groups, halves * TILE_W, sections), F32),
+            pltpu.VMEM((groups + groups // 2, sections, TILE_W), F32),
+            pltpu.VMEM((groups, tiles * GROUP_LANES, sections), F32),
             pltpu.VMEM((3, count, sections), F32),
             pltpu.VMEM((24, count + 2 * tiles, sections), F32),
             pltpu.VMEM((2, rows + 2 * tiles, cols), F32),

time: 64.8 us -> 56.5 us (0.87)
  blocking collectives: 30.3 us -> 24.8 us
  waiting for transfers between devices: 4.19 us -> 1.8 us
    all_to_all x1, blocking collectives: 26.2 us -> 20.7 us  [body(): lax.all_to_all(mine, 'z', 0, 0, tiled=True, axis_index_groups=[turned])]
    all_to_all x1, waiting for transfers between devices: 4.16 us -> 1.77 us  [body(): lax.all_to_all(copies, ('group',) + SEC, 0, 0, tiled=True, axis_index_gro...]
    ppermute x2, starting transfers between devices: 4.55 us -> 2.89 us  [from_behind(): return lax.ppermute(block, axis, route)]
    all_to_all x1, starting transfers between devices: 6.97 us -> 8.18 us  [body(): lax.all_to_all(copies, ('group',) + SEC, 0, 0, tiled=True, axis_index_gro...]
  transfers between devices with their start and end apart: 5 -> 5, of which waited for: 1 -> 1; matrix products, arithmetic and copies ran while one was open for 0% -> 0% of each run, Pallas kernels for 1% -> 2%
where the time goes in v5:
time: 56.5 us; the launch traced here: 56.1 us
  blocking collectives  24.8 us (44%)
  starting transfers between devices  20.5 us (36%)
  Pallas kernels  6.88 us (12%)
  waiting for transfers between devices  1.8 us (3%)
  between operations  1.42 us (3%)
  local copies, waits for them, and re-layouts  0.65 us (1%)
    all_to_all x1, blocking collectives, body(): lax.all_to_all(mine, 'z', 0, 0, tiled=True, axis_index_groups=[turned])  20.7 us
    ppermute x2, starting transfers between devices, swap(): return lax.ppermute(block, SEC, route)  9.48 us
    all_to_all x1, starting transfers between devices, body(): lax.all_to_all(copies, ('group',) + SEC, 0, 0, tiled=True, axis_index_gro...  8.18 us
    all_gather x1, blocking collectives, body(): seen = lax.all_gather(seen, 'core', axis=0, tiled=True)  4.1 us
    ppermute x2, starting transfers between devices, from_behind(): return lax.ppermute(block, axis, route)  2.89 us
    pallas_call x1, Pallas kernels, body(): pl.pallas_call(both_iterations, out_shape=(field, field), in_specs=[local...  2.83 us
    all_to_all x1, waiting for transfers between devices, body(): lax.all_to_all(copies, ('group',) + SEC, 0, 0, tiled=True, axis_index_gro...  1.77 us
    pallas_call x1, Pallas kernels, body(): pl.pallas_call(pack_kernel, out_shape=(packed, packed, in_vmem(border)),...  1.48 us
  transfers between devices with their start and end apart: 5, of which 1 were waited for; matrix products, arithmetic and copies ran while one was open for 0% of the time, Pallas kernels for 2%

profile of v5, /device:TPU:1, one launch (start us, length us, event | category | flops | bytes accessed | tf_op | source)
XLA Modules:
  0.0 56.1 jit_solution(6653483908666299199)
XLA Ops:
  0.7 1.5 %pack.1 = (bf16[528,512]{1,0:T(8,128)(2,1)S(1)}, bf16[528,512]{1,0:T(8,128)(2,1)S(1)}, f32[8,128]{1,0:T(8,128)S(1)}) custom-call(bf16[1024,512]{1,0:T(8,128)(2,1)} %bitcast.9, bf16[1024,512]{1,0:T(8,128)(2,1)} %bitcast.8, f32[1,16,1024]{2,1,0:T(8,128)} %vert_ref.1, f32[1,16,1024]{2,1,0:T(8,128)} %hori_ref.1, s32[1,16,2,64]{3,2,1,0:T(2,128)} %offsets_ref.3), custom_call_target="tpu_custom_call" | custom-call | tf_op jit(solution)/shard_map/pack/pallas_call | solution.py:667
  2.2 4.6 %collective-permute-start.1 = (bf16[528,512]{1,0:T(8,128)(2,1)S(1)}, bf16[528,512]{1,0:T(8,128)(2,1)S(1)}, u32[]{:S(2)}, u32[]{:S(2)}) collective-permute-start(bf16[528,512]{1,0:T(8,128)(2,1)S(1)} %get-tuple-element.20), channel_id=1, source_target_pairs={{1,2},{2,1},{3,4},{4,3},{5,6},{6,5},{7,8},{8,7},{9,10},{10,9},{11,... | collective-permute-start | bytes 1622024 | tf_op jit(solution)/shard_map/ppermute | solution.py:646
  6.8 4.9 %collective-permute-start.2 = (bf16[528,512]{1,0:T(8,128)(2,1)S(1)}, bf16[528,512]{1,0:T(8,128)(2,1)S(1)}, u32[]{:S(2)}, u32[]{:S(2)}) collective-permute-start(bf16[528,512]{1,0:T(8,128)(2,1)S(1)} %get-tuple-element.21), channel_id=1, source_target_pairs={{0,1},{1,0},{2,3},{3,2},{4,5},{5,4},{6,7},{7,6},{8,9},{9,8},{10,11... | collective-permute-start | bytes 1622024 | tf_op jit(solution)/shard_map/ppermute | solution.py:646
  11.7 1.3 %collective-permute-start = (f32[8,128]{1,0:T(8,128)S(1)}, f32[8,128]{1,0:T(8,128)S(1)}, u32[]{:S(2)}, u32[]{:S(2)}) collective-permute-start(f32[8,128]{1,0:T(8,128)S(1)} %get-tuple-element.16.refs_4_.line_ref.refs_3_), channel_id=1, source_target_pairs={{0,128},{128,256},{256,384},{1,129},{129,257},{257,385},{2,130},{1... | collective-permute-start | bytes 12296 | tf_op jit(solution)/shard_map/ppermute | solution.py:622
  13.6 0.0 copy-start.5
  13.6 0.0 copy-done.2
  13.6 0.0 copy-done.3
  13.6 0.6 %copy-done.5 = s32[1,16]{1,0:T(1,128)S(1)} copy-done((s32[1,16]{1,0:T(1,128)S(1)}, s32[1,16]{1,0:T(1,128)}, u32[]{:S(2)}) %copy-start.5) | copy-done | bytes 88
  14.3 0.9 %borders.1 = (f32[8,128]{1,0:T(8,128)S(1)}, f32[16,128]{1,0:T(8,128)S(1)}, f32[16,128]{1,0:T(8,128)S(1)}) custom-call(s32[1,16]{1,0:T(1,128)S(1)} %copy-done.5, s32[1,1]{1,0:T(1,128)S(6)} %copy.9.refs_1_, f32[16,1024]{1,0:T(8,128)S(1)} %bitcast.10, f32[16,1024]{1,0:T(8,128)S(1)} %bitcast.12, f32[8,128]{1,0:T(8,128)S(1)} %get-tuple-element.16.refs_4_.line_ref.refs_3_), custom_call_target="tpu_custom_call" | custom-call | tf_op jit(solution)/shard_map/borders/pallas_call | solution.py:695
  15.1 0.0 collective-permute-done.above_ref.refs_4_
  15.1 0.0 collective-permute-done.1.across_ref
  15.2 0.0 collective-permute-done.2.beside_ref
  15.2 0.0 copy-done
  15.2 0.0 copy-done.1
  15.2 0.0 copy-done.4
  15.2 0.9 %match.1 = (f32[16,2,128]{2,1,0:T(2,128)S(1)}, f32[16,128]{1,0:T(8,128)S(1)}, f32[16,128]{1,0:T(8,128)S(1)}, f32[16,128]{1,0:T(8,128)S(1)}) custom-call(bf16[1,16,64,512]{3,2,1,0:T(8,128)(2,1)S(1)} %copy-done, bf16[1,16,64,512]{3,2,1,0:T(8,128)(2,1)S(1)} %copy-done.1, s32[1,16,2,64]{3,2,1,0:T(2,128)S(1)} %copy-done.4, ...), custom_call_target="tpu_custom_call" | custom-call | tf_op jit(solution)/shard_map/match/pallas_call | solution.py:704
  16.1 20.7 %all_to_all.10 = f32[16,2,128]{2,1,0:T(2,128)S(1)} all-to-all(f32[16,2,128]{2,1,0:T(2,128)S(1)} %get-tuple-element.23), channel_id=1, replica_groups={{64,72,80,88,96,104,112,120,0,8,16,24,32,40,48,56},{65,73,81,89,97,105,..., dimensions={0} | all-to-all | bytes 32768 | tf_op jit(solution)/shard_map/all_to_all | solution.py:718
  36.8 0.8 %copies.1 = f32[16,24,128]{2,1,0:T(8,128)} custom-call(f32[32,128]{1,0:T(8,128)S(1)} %bitcast.14), custom_call_target="tpu_custom_call" | custom-call | tf_op jit(solution)/shard_map/copies/pallas_call | solution.py:723
  37.6 8.2 %all-to-all-start.1 = ((f32[16,24,128]{2,1,0:T(8,128)}), f32[16,24,128]{2,1,0:T(8,128)S(1)}, u32[]{:S(2)}, u32[]{:S(2)}) async-start(f32[16,24,128]{2,1,0:T(8,128)} %copies.1), calls=%async_computation.1 | async-start | bytes 393216 | tf_op jit(solution)/shard_map/all_to_all | solution.py:731
  45.8 1.6 %collective-permute-start.3 = (f32[16,128]{1,0:T(8,128)S(1)}, f32[16,128]{1,0:T(8,128)S(1)}, u32[]{:S(2)}, u32[]{:S(2)}) collective-permute-start(f32[16,128]{1,0:T(8,128)S(1)} %get-tuple-element.25.refs_5_), channel_id=1, source_target_pairs={{0,128},{128,256},{256,384},{1,129},{129,257},{257,385},{2,130},{1... | collective-permute-start | bytes 24584 | tf_op jit(solution)/shard_map/ppermute | solution.py:622
  47.4 1.8 %all-to-all-done.1 = f32[16,24,128]{2,1,0:T(8,128)S(1)} async-done(((f32[16,24,128]{2,1,0:T(8,128)}), f32[16,24,128]{2,1,0:T(8,128)S(1)}, u32[]{:S(2)}, u32[]{:S(2)}) %all-to-all-start.1) | async-done | bytes 196640 | tf_op jit(solution)/shard_map/all_to_all | solution.py:731
  49.2 4.1 %all_gather.3.refs_0_ = f32[768,128]{1,0:T(8,128)S(1)} all-gather(f32[384,128]{1,0:T(8,128)S(1)} %bitcast.15), channel_id=1, replica_groups=mesh['group'=4,'z'=16,'y'=4,'core'=2] {'core'}, dimensions={0}, use_global_device_ids=true | all-gather | bytes 589824 | tf_op jit(solution)/shard_map/all_gather | solution.py:734
  53.3 0.0 collective-permute-done.3.refs_6_
  53.3 2.8 %stack.1 = (f32[2,16,1024]{2,1,0:T(8,128)}, f32[2,16,1024]{2,1,0:T(8,128)}) custom-call(f32[768,128]{1,0:T(8,128)S(1)} %all_gather.3.refs_0_, f32[16,1024]{1,0:T(8,128)S(1)} %bitcast.11, f32[16,1024]{1,0:T(8,128)S(1)} %bitcast.13, f32[8,128]{1,0:T(8,128)S(1)} %get-tuple-element.16.refs_4_.line_ref.refs_3_, ...), custom_call_target="tpu_custom_call" | custom-call | tf_op jit(solution)/shard_map/stack/pallas_call | solution.py:743
  (5 shorter events, 0.0 us)
Async XLA Ops:
  0.6 13.0 %copy-start.2 = (f32[1,16,1024]{2,1,0:T(8,128)S(1)}, f32[1,16,1024]{2,1,0:T(8,128)}, u32[]{:S(2)}) copy-start(f32[1,16,1024]{2,1,0:T(8,128)} %vert_ref.1) | copy-start | bytes 196612
  0.6 13.0 %copy-start.3 = (f32[1,16,1024]{2,1,0:T(8,128)S(1)}, f32[1,16,1024]{2,1,0:T(8,128)}, u32[]{:S(2)}) copy-start(f32[1,16,1024]{2,1,0:T(8,128)} %hori_ref.1) | copy-start | bytes 196612
  0.7 14.5 %copy-start = (bf16[1,16,64,512]{3,2,1,0:T(8,128)(2,1)S(1)}, bf16[1,16,64,512]{3,2,1,0:T(8,128)(2,1)}, u32[]{:S(2)}) copy-start(bf16[1,16,64,512]{3,2,1,0:T(8,128)(2,1)} %fixed_ref.1) | copy-start | bytes 3145732
  0.7 14.5 %copy-start.1 = (bf16[1,16,64,512]{3,2,1,0:T(8,128)(2,1)S(1)}, bf16[1,16,64,512]{3,2,1,0:T(8,128)(2,1)}, u32[]{:S(2)}) copy-start(bf16[1,16,64,512]{3,2,1,0:T(8,128)(2,1)} %moving_ref.1) | copy-start | bytes 3145732
  2.2 13.0 %collective-permute-start.1 = (bf16[528,512]{1,0:T(8,128)(2,1)S(1)}, bf16[528,512]{1,0:T(8,128)(2,1)S(1)}, u32[]{:S(2)}, u32[]{:S(2)}) collective-permute-start(bf16[528,512]{1,0:T(8,128)(2,1)S(1)} %get-tuple-element.20), channel_id=1, source_target_pairs={{1,2},{2,1},{3,4},{4,3},{5,6},{6,5},{7,8},{8,7},{9,10},{10,9},{11,... | collective-permute-start | bytes 1622024 | tf_op jit(solution)/shard_map/ppermute | solution.py:646
  6.8 8.4 %collective-permute-start.2 = (bf16[528,512]{1,0:T(8,128)(2,1)S(1)}, bf16[528,512]{1,0:T(8,128)(2,1)S(1)}, u32[]{:S(2)}, u32[]{:S(2)}) collective-permute-start(bf16[528,512]{1,0:T(8,128)(2,1)S(1)} %get-tuple-element.21), channel_id=1, source_target_pairs={{0,1},{1,0},{2,3},{3,2},{4,5},{5,4},{6,7},{7,6},{8,9},{9,8},{10,11... | collective-permute-start | bytes 1622024 | tf_op jit(solution)/shard_map/ppermute | solution.py:646
  11.7 3.5 %collective-permute-start = (f32[8,128]{1,0:T(8,128)S(1)}, f32[8,128]{1,0:T(8,128)S(1)}, u32[]{:S(2)}, u32[]{:S(2)}) collective-permute-start(f32[8,128]{1,0:T(8,128)S(1)} %get-tuple-element.16.refs_4_.line_ref.refs_3_), channel_id=1, source_target_pairs={{0,128},{128,256},{256,384},{1,129},{129,257},{257,385},{2,130},{1... | collective-permute-start | bytes 12296 | tf_op jit(solution)/shard_map/ppermute | solution.py:622
  13.6 0.7 %copy-start.5 = (s32[1,16]{1,0:T(1,128)S(1)}, s32[1,16]{1,0:T(1,128)}, u32[]{:S(2)}) copy-start(s32[1,16]{1,0:T(1,128)} %refs_0_.1) | copy-start | bytes 196
  14.3 0.9 %copy-start.4 = (s32[1,16,2,64]{3,2,1,0:T(2,128)S(1)}, s32[1,16,2,64]{3,2,1,0:T(2,128)}, u32[]{:S(2)}) copy-start(s32[1,16,2,64]{3,2,1,0:T(2,128)} %offsets_ref.3) | copy-start | bytes 24580
  37.6 11.5 %all-to-all-start.1 = ((f32[16,24,128]{2,1,0:T(8,128)}), f32[16,24,128]{2,1,0:T(8,128)S(1)}, u32[]{:S(2)}, u32[]{:S(2)}) async-start(f32[16,24,128]{2,1,0:T(8,128)} %copies.1), calls=%async_computation.1 | async-start | bytes 393216 | tf_op jit(solution)/shard_map/all_to_all | solution.py:731
  45.8 7.5 %collective-permute-start.3 = (f32[16,128]{1,0:T(8,128)S(1)}, f32[16,128]{1,0:T(8,128)S(1)}, u32[]{:S(2)}, u32[]{:S(2)}) collective-permute-start(f32[16,128]{1,0:T(8,128)S(1)} %get-tuple-element.25.refs_5_), channel_id=1, source_target_pairs={{0,128},{128,256},{256,384},{1,129},{129,257},{257,385},{2,130},{1... | collective-permute-start | bytes 24584 | tf_op jit(solution)/shard_map/ppermute | solution.py:622

commit v6 on v5

--- a/solution.py
+++ b/solution.py
@@ -22,8 +22,11 @@
 COLUMN_FAR = 21
 COLUMN_HELP = 23
 GROUP_LANES = 24
+FIRST_Z = 8
 FIRST_GROUP = 2
-FIRST_CHIP = (0, 3)
+FIRST_CHIP = (2, 2)
+ORIGIN = (0, 0)
+ORIGIN_PLACE = 15
 PARTS = 2
 
 
@@ -278,11 +281,12 @@
     for k in range(2):
         offsets.append(offsets_ref[0, 0:half, k, :].astype(F32))
         offsets.append(shifts[:, k * flow : (k + 1) * flow])
+    shifted = jnp.concatenate(offsets, 0).astype(jnp.bfloat16)
+    parts = [part.astype(jnp.bfloat16) for part in three_parts(likely)]
     sums = lax.dot_general(
-        jnp.concatenate(offsets, 0),
-        likely,
+        jnp.concatenate([shifted] * 3, 1),
+        jnp.concatenate(parts, 0),
         (((1,), (0,)), ((), ())),
-        precision=lax.Precision.HIGHEST,
         preferred_element_type=F32,
     )
     weight = row_sum(likely) * flow
@@ -332,16 +336,18 @@
             out_ref[n, part : part + 1, :] = piece
 
 
-def copies_kernel(seen_ref, out_ref):
+def copies_kernel(seen_ref, out_ref, block):
     chips = seen_ref.shape[0] // 2
-    half = chips // 2
-    first = [seen_ref[pl.ds(n * chips, half, stride=2), :] for n in (1, 0)]
-    low = seen_ref[pl.ds(1 + chips, half, stride=2), :]
-    high = seen_ref[pl.ds(1, half, stride=2), :]
-    second = low + pltpu.roll(high, TILE_W // 2, 1)
+    shared = chips // 2
+    lead = chips - FIRST_Z
+    block[0:FIRST_Z, :] = seen_ref[pl.ds(2 * lead, FIRST_Z, stride=2), :]
+    block[FIRST_Z:chips, :] = seen_ref[pl.ds(0, lead, stride=2), :]
+    block[chips : chips + FIRST_Z, :] = seen_ref[pl.ds(2 * lead + 1, FIRST_Z, stride=2), :]
+    block[chips + FIRST_Z :, :] = seen_ref[pl.ds(1, lead, stride=2), :]
+    first = block[0:chips, :]
+    second = block[chips : chips + shared, :] + pltpu.roll(block[chips + shared :, :], TILE_W // 2, 1)
     for n in range(out_ref.shape[0]):
-        out_ref[n, 0:half, :] = first[0]
-        out_ref[n, half:chips, :] = first[1]
+        out_ref[n, 0:chips, :] = first
         out_ref[n, chips:, :] = second
 
 
@@ -361,7 +367,7 @@
     for core in range(CORES):
         for g in range(groups):
             for y in range(per_chip // CORES):
-                place = core * groups * CHIPS_Y + plane_place(groups, core, g, y)
+                place = (CORES - 1 - core) * groups * CHIPS_Y + plane_order(groups, core).index((g, y))
                 base = place * (chips_z + shared)
                 chip = y * CORES + core
                 rows_ref[g, pl.ds(chip, chips_z, stride=per_chip), :] = seen_ref[base : base + chips_z, :]
@@ -469,13 +475,22 @@
     energy = energy + nodes * weight * (gap[0] * gap[0] + gap[1] * gap[1])
     alpha = norm / total(energy)
 
+    index = jnp.maximum(owner, 0.0).astype(jnp.int32)
+    inside_index = lax.rem(index, tiles)
+    row_index = lax.div(index, tiles)
+    look = []
     for k in range(2):
-        sums_ref[k] = alpha * gap[k]
-    look = [jnp.zeros_like(owner), jnp.zeros_like(owner)]
-    for t in range(count):
-        mine = owner == float(t)
-        for k in range(2):
-            look[k] = jnp.where(mine, sums_ref[k, t : t + 1, :], look[k])
+        shift = alpha * gap[k]
+        rows_of = []
+        for p in range(0, owner.shape[0], tiles):
+            value = jnp.zeros((tiles, sections), F32)
+            for g in range(groups):
+                picked = jnp.take_along_axis(
+                    shift[g * tiles : (g + 1) * tiles], inside_index[p : p + tiles], axis=0
+                )
+                value = jnp.where(row_index[p : p + tiles] == g, picked, value)
+            rows_of.append(value)
+        look.append(jnp.concatenate(rows_of, 0))
     weight, *pull = tile_sums([look[k] - targets[k] for k in range(2)])
     weight_low = low(weight)
     const = [
@@ -622,21 +637,23 @@
     return lax.ppermute(block, axis, route)
 
 
-def plane_place(groups, core, g, y):
-    return (g - FIRST_GROUP) % groups * CHIPS_Y + (y - FIRST_CHIP[core]) % CHIPS_Y
+def plane_order(groups, core):
+    order = [
+        ((FIRST_GROUP + g) % groups, (FIRST_CHIP[core] + y) % CHIPS_Y)
+        for g in range(groups)
+        for y in range(CHIPS_Y)
+    ]
+    order.remove(ORIGIN)
+    order.insert(ORIGIN_PLACE, ORIGIN)
+    return order
 
 
 def planes(groups, chips_z):
-    lists = []
-    for z in range(chips_z):
-        for core in range(CORES):
-            members = [None] * (groups * CHIPS_Y)
-            for g in range(groups):
-                for y in range(CHIPS_Y):
-                    device = ((g * chips_z + z) * CHIPS_Y + y) * CORES + core
-                    members[plane_place(groups, core, g, y)] = device
-            lists.append(members)
-    return lists
+    return [
+        [((g * chips_z + z) * CHIPS_Y + y) * CORES + core for g, y in plane_order(groups, core)]
+        for z in range(chips_z)
+        for core in range(CORES)
+    ]
 
 
 def swap(block, first):
@@ -714,7 +731,7 @@
         name="match",
     )(fixed_desc, moving_desc, offsets, table, firsts, right, line, above, across, beside)
 
-    turned = [(z + chips_z // 2) % chips_z for z in range(chips_z)]
+    turned = [(z + FIRST_Z) % chips_z for z in range(chips_z)]
     seen = lax.all_to_all(mine, "z", 0, 0, tiled=True, axis_index_groups=[turned]).reshape(-1, TILE_W)
     lines, seen = lax.optimization_barrier((lines, seen))
     aboves = from_behind(lines, "group", 1)
@@ -725,13 +742,15 @@
         out_shape=jax.ShapeDtypeStruct((peers, block_rows, TILE_W), F32),
         in_specs=[local],
         out_specs=local,
+        scratch_shapes=[pltpu.VMEM((2 * chips_z, TILE_W), F32)],
         compiler_params=modest,
         name="copies",
     )(seen)
     seen = lax.all_to_all(
         copies, ("group",) + SEC, 0, 0, tiled=True, axis_index_groups=planes(groups, chips_z)
     ).reshape(-1, TILE_W)
-    seen = lax.all_gather(seen, "core", axis=0, tiled=True)
+    cores = list(reversed(range(CORES)))
+    seen = lax.all_gather(seen, "core", axis=0, tiled=True, axis_index_groups=[cores])
 
     dims = (groups, sections, rows, tiles, chips_z)
     count = groups * tiles

time: 56.5 us -> 55.4 us (0.981)
  waiting for transfers between devices: 1.8 us -> 0.92 us
    all_to_all x1, waiting for transfers between devices: 1.77 us -> 0.89 us  [body(): lax.all_to_all(copies, ('group',) + SEC, 0, 0, tiled=True, axis_index_gro...]
where the time goes in v6:
time: 55.4 us; the launch traced here: 55.1 us
  blocking collectives  25.1 us (45%)
  starting transfers between devices  20.3 us (37%)
  Pallas kernels  6.74 us (12%)
  between operations  1.42 us (3%)
  waiting for transfers between devices  0.92 us (2%)
  local copies, waits for them, and re-layouts  0.65 us (1%)
    all_to_all x1, blocking collectives, body(): lax.all_to_all(mine, 'z', 0, 0, tiled=True, axis_index_groups=[turned])  20.7 us
    ppermute x2, starting transfers between devices, swap(): return lax.ppermute(block, SEC, route)  9.48 us
    all_to_all x1, starting transfers between devices, body(): lax.all_to_all(copies, ('group',) + SEC, 0, 0, tiled=True, axis_index_gro...  7.92 us
    all_gather x1, blocking collectives, body(): lax.all_gather(seen, 'core', axis=0, tiled=True, axis_index_groups=[cores])  4.37 us
    ppermute x2, starting transfers between devices, from_behind(): return lax.ppermute(block, axis, route)  2.86 us
    pallas_call x1, Pallas kernels, body(): pl.pallas_call(both_iterations, out_shape=(field, field), in_specs=[local...  2.72 us
    pallas_call x1, Pallas kernels, body(): pl.pallas_call(pack_kernel, out_shape=(packed, packed, in_vmem(border)),...  1.48 us
  transfers between devices with their start and end apart: 5, of which 1 were waited for; matrix products, arithmetic and copies ran while one was open for 0% of the time, Pallas kernels for 2%

profile of v6, /device:TPU:1, one launch (start us, length us, event | category | flops | bytes accessed | tf_op | source)
XLA Modules:
  0.0 55.1 jit_solution(15877353586808314073)
XLA Ops:
  0.6 0.0 copy-start.2
  0.6 0.0 copy-start.3
  0.7 0.0 copy-start
  0.7 0.0 copy-start.1
  0.7 1.5 %pack.1 = (bf16[528,512]{1,0:T(8,128)(2,1)S(1)}, bf16[528,512]{1,0:T(8,128)(2,1)S(1)}, f32[8,128]{1,0:T(8,128)S(1)}) custom-call(bf16[1024,512]{1,0:T(8,128)(2,1)} %bitcast.9, bf16[1024,512]{1,0:T(8,128)(2,1)} %bitcast.8, f32[1,16,1024]{2,1,0:T(8,128)} %vert_ref.1, f32[1,16,1024]{2,1,0:T(8,128)} %hori_ref.1, s32[1,16,2,64]{3,2,1,0:T(2,128)} %offsets_ref.3), custom_call_target="tpu_custom_call" | custom-call | tf_op jit(solution)/shard_map/pack/pallas_call | solution.py:684
  2.2 4.6 %collective-permute-start.1 = (bf16[528,512]{1,0:T(8,128)(2,1)S(1)}, bf16[528,512]{1,0:T(8,128)(2,1)S(1)}, u32[]{:S(2)}, u32[]{:S(2)}) collective-permute-start(bf16[528,512]{1,0:T(8,128)(2,1)S(1)} %get-tuple-element.20), channel_id=1, source_target_pairs={{1,2},{2,1},{3,4},{4,3},{5,6},{6,5},{7,8},{8,7},{9,10},{10,9},{11,... | collective-permute-start | bytes 1622024 | tf_op jit(solution)/shard_map/ppermute | solution.py:663
  6.8 4.9 %collective-permute-start.2 = (bf16[528,512]{1,0:T(8,128)(2,1)S(1)}, bf16[528,512]{1,0:T(8,128)(2,1)S(1)}, u32[]{:S(2)}, u32[]{:S(2)}) collective-permute-start(bf16[528,512]{1,0:T(8,128)(2,1)S(1)} %get-tuple-element.21), channel_id=1, source_target_pairs={{0,1},{1,0},{2,3},{3,2},{4,5},{5,4},{6,7},{7,6},{8,9},{9,8},{10,11... | collective-permute-start | bytes 1622024 | tf_op jit(solution)/shard_map/ppermute | solution.py:663
  11.7 1.3 %collective-permute-start = (f32[8,128]{1,0:T(8,128)S(1)}, f32[8,128]{1,0:T(8,128)S(1)}, u32[]{:S(2)}, u32[]{:S(2)}) collective-permute-start(f32[8,128]{1,0:T(8,128)S(1)} %get-tuple-element.16.refs_4_.line_ref.refs_3_), channel_id=1, source_target_pairs={{0,128},{128,256},{256,384},{1,129},{129,257},{257,385},{2,130},{1... | collective-permute-start | bytes 12296 | tf_op jit(solution)/shard_map/ppermute | solution.py:637
  13.6 0.0 copy-start.5
  13.6 0.0 copy-done.2
  13.6 0.6 %copy-done.5 = s32[1,16]{1,0:T(1,128)S(1)} copy-done((s32[1,16]{1,0:T(1,128)S(1)}, s32[1,16]{1,0:T(1,128)}, u32[]{:S(2)}) %copy-start.5) | copy-done | bytes 88
  14.3 0.9 %borders.1 = (f32[8,128]{1,0:T(8,128)S(1)}, f32[16,128]{1,0:T(8,128)S(1)}, f32[16,128]{1,0:T(8,128)S(1)}) custom-call(s32[1,16]{1,0:T(1,128)S(1)} %copy-done.5, s32[1,1]{1,0:T(1,128)S(6)} %copy.9.refs_1_, f32[16,1024]{1,0:T(8,128)S(1)} %bitcast.10, f32[16,1024]{1,0:T(8,128)S(1)} %bitcast.12, f32[8,128]{1,0:T(8,128)S(1)} %get-tuple-element.16.refs_4_.line_ref.refs_3_), custom_call_target="tpu_custom_call" | custom-call | tf_op jit(solution)/shard_map/borders/pallas_call | solution.py:712
  15.1 0.0 collective-permute-done.above_ref.refs_4_
  15.1 0.0 collective-permute-done.1.across_ref
  15.2 0.0 collective-permute-done.2.beside_ref
  15.2 0.9 %match.1 = (f32[16,2,128]{2,1,0:T(2,128)S(1)}, f32[16,128]{1,0:T(8,128)S(1)}, f32[16,128]{1,0:T(8,128)S(1)}, f32[16,128]{1,0:T(8,128)S(1)}) custom-call(bf16[1,16,64,512]{3,2,1,0:T(8,128)(2,1)S(1)} %copy-done, bf16[1,16,64,512]{3,2,1,0:T(8,128)(2,1)S(1)} %copy-done.1, s32[1,16,2,64]{3,2,1,0:T(2,128)S(1)} %copy-done.4, ...), custom_call_target="tpu_custom_call" | custom-call | tf_op jit(solution)/shard_map/match/pallas_call | solution.py:721
  16.1 20.7 %all_to_all.10 = f32[16,2,128]{2,1,0:T(2,128)S(1)} all-to-all(f32[16,2,128]{2,1,0:T(2,128)S(1)} %get-tuple-element.23), channel_id=1, replica_groups={{64,72,80,88,96,104,112,120,0,8,16,24,32,40,48,56},{65,73,81,89,97,105,..., dimensions={0} | all-to-all | bytes 32768 | tf_op jit(solution)/shard_map/all_to_all | solution.py:735
  36.8 0.8 %copies.1 = f32[16,24,128]{2,1,0:T(8,128)} custom-call(f32[32,128]{1,0:T(8,128)S(1)} %bitcast.14), custom_call_target="tpu_custom_call" | custom-call | tf_op jit(solution)/shard_map/copies/pallas_call | solution.py:740
  37.6 7.9 %all-to-all-start.1 = ((f32[16,24,128]{2,1,0:T(8,128)}), f32[16,24,128]{2,1,0:T(8,128)S(1)}, u32[]{:S(2)}, u32[]{:S(2)}) async-start(f32[16,24,128]{2,1,0:T(8,128)} %copies.1), calls=%async_computation.1 | async-start | bytes 393216 | tf_op jit(solution)/shard_map/all_to_all | solution.py:749
  45.5 1.6 %collective-permute-start.3 = (f32[16,128]{1,0:T(8,128)S(1)}, f32[16,128]{1,0:T(8,128)S(1)}, u32[]{:S(2)}, u32[]{:S(2)}) collective-permute-start(f32[16,128]{1,0:T(8,128)S(1)} %get-tuple-element.25.refs_5_), channel_id=1, source_target_pairs={{0,128},{128,256},{256,384},{1,129},{129,257},{257,385},{2,130},{1... | collective-permute-start | bytes 24584 | tf_op jit(solution)/shard_map/ppermute | solution.py:637
  47.1 0.9 %all-to-all-done.1 = f32[16,24,128]{2,1,0:T(8,128)S(1)} async-done(((f32[16,24,128]{2,1,0:T(8,128)}), f32[16,24,128]{2,1,0:T(8,128)S(1)}, u32[]{:S(2)}, u32[]{:S(2)}) %all-to-all-start.1) | async-done | bytes 196640 | tf_op jit(solution)/shard_map/all_to_all | solution.py:749
  48.0 4.4 %all_gather.3.refs_0_ = f32[768,128]{1,0:T(8,128)S(1)} all-gather(f32[384,128]{1,0:T(8,128)S(1)} %bitcast.15), channel_id=1, replica_groups={{1,0},{3,2},{5,4},{7,6},{9,8},{11,10},{13,12},{15,14},{17,16},{19,18},{..., dimensions={0}, use_global_device_ids=true | all-gather | bytes 589824 | tf_op jit(solution)/shard_map/all_gather | solution.py:753
  52.3 0.0 collective-permute-done.3.refs_6_
  52.3 2.7 %stack.1 = (f32[2,16,1024]{2,1,0:T(8,128)}, f32[2,16,1024]{2,1,0:T(8,128)}) custom-call(f32[768,128]{1,0:T(8,128)S(1)} %all_gather.3.refs_0_, f32[16,1024]{1,0:T(8,128)S(1)} %bitcast.11, f32[16,1024]{1,0:T(8,128)S(1)} %bitcast.13, f32[8,128]{1,0:T(8,128)S(1)} %get-tuple-element.16.refs_4_.line_ref.refs_3_, ...), custom_call_target="tpu_custom_call" | custom-call | tf_op jit(solution)/shard_map/stack/pallas_call | solution.py:762
  (5 shorter events, 0.0 us)
Async XLA Ops:
  0.6 13.0 %copy-start.2 = (f32[1,16,1024]{2,1,0:T(8,128)S(1)}, f32[1,16,1024]{2,1,0:T(8,128)}, u32[]{:S(2)}) copy-start(f32[1,16,1024]{2,1,0:T(8,128)} %vert_ref.1) | copy-start | bytes 196612
  0.6 13.0 %copy-start.3 = (f32[1,16,1024]{2,1,0:T(8,128)S(1)}, f32[1,16,1024]{2,1,0:T(8,128)}, u32[]{:S(2)}) copy-start(f32[1,16,1024]{2,1,0:T(8,128)} %hori_ref.1) | copy-start | bytes 196612
  0.7 14.5 %copy-start = (bf16[1,16,64,512]{3,2,1,0:T(8,128)(2,1)S(1)}, bf16[1,16,64,512]{3,2,1,0:T(8,128)(2,1)}, u32[]{:S(2)}) copy-start(bf16[1,16,64,512]{3,2,1,0:T(8,128)(2,1)} %fixed_ref.1) | copy-start | bytes 3145732
  0.7 14.5 %copy-start.1 = (bf16[1,16,64,512]{3,2,1,0:T(8,128)(2,1)S(1)}, bf16[1,16,64,512]{3,2,1,0:T(8,128)(2,1)}, u32[]{:S(2)}) copy-start(bf16[1,16,64,512]{3,2,1,0:T(8,128)(2,1)} %moving_ref.1) | copy-start | bytes 3145732
  2.2 13.0 %collective-permute-start.1 = (bf16[528,512]{1,0:T(8,128)(2,1)S(1)}, bf16[528,512]{1,0:T(8,128)(2,1)S(1)}, u32[]{:S(2)}, u32[]{:S(2)}) collective-permute-start(bf16[528,512]{1,0:T(8,128)(2,1)S(1)} %get-tuple-element.20), channel_id=1, source_target_pairs={{1,2},{2,1},{3,4},{4,3},{5,6},{6,5},{7,8},{8,7},{9,10},{10,9},{11,... | collective-permute-start | bytes 1622024 | tf_op jit(solution)/shard_map/ppermute | solution.py:663
  6.8 8.4 %collective-permute-start.2 = (bf16[528,512]{1,0:T(8,128)(2,1)S(1)}, bf16[528,512]{1,0:T(8,128)(2,1)S(1)}, u32[]{:S(2)}, u32[]{:S(2)}) collective-permute-start(bf16[528,512]{1,0:T(8,128)(2,1)S(1)} %get-tuple-element.21), channel_id=1, source_target_pairs={{0,1},{1,0},{2,3},{3,2},{4,5},{5,4},{6,7},{7,6},{8,9},{9,8},{10,11... | collective-permute-start | bytes 1622024 | tf_op jit(solution)/shard_map/ppermute | solution.py:663
  11.7 3.5 %collective-permute-start = (f32[8,128]{1,0:T(8,128)S(1)}, f32[8,128]{1,0:T(8,128)S(1)}, u32[]{:S(2)}, u32[]{:S(2)}) collective-permute-start(f32[8,128]{1,0:T(8,128)S(1)} %get-tuple-element.16.refs_4_.line_ref.refs_3_), channel_id=1, source_target_pairs={{0,128},{128,256},{256,384},{1,129},{129,257},{257,385},{2,130},{1... | collective-permute-start | bytes 12296 | tf_op jit(solution)/shard_map/ppermute | solution.py:637
  13.6 0.7 %copy-start.5 = (s32[1,16]{1,0:T(1,128)S(1)}, s32[1,16]{1,0:T(1,128)}, u32[]{:S(2)}) copy-start(s32[1,16]{1,0:T(1,128)} %refs_0_.1) | copy-start | bytes 196
  14.3 0.9 %copy-start.4 = (s32[1,16,2,64]{3,2,1,0:T(2,128)S(1)}, s32[1,16,2,64]{3,2,1,0:T(2,128)}, u32[]{:S(2)}) copy-start(s32[1,16,2,64]{3,2,1,0:T(2,128)} %offsets_ref.3) | copy-start | bytes 24580
  37.6 10.4 %all-to-all-start.1 = ((f32[16,24,128]{2,1,0:T(8,128)}), f32[16,24,128]{2,1,0:T(8,128)S(1)}, u32[]{:S(2)}, u32[]{:S(2)}) async-start(f32[16,24,128]{2,1,0:T(8,128)} %copies.1), calls=%async_computation.1 | async-start | bytes 393216 | tf_op jit(solution)/shard_map/all_to_all | solution.py:749
  45.5 6.8 %collective-permute-start.3 = (f32[16,128]{1,0:T(8,128)S(1)}, f32[16,128]{1,0:T(8,128)S(1)}, u32[]{:S(2)}, u32[]{:S(2)}) collective-permute-start(f32[16,128]{1,0:T(8,128)S(1)} %get-tuple-element.25.refs_5_), channel_id=1, source_target_pairs={{0,128},{128,256},{256,384},{1,129},{129,257},{257,385},{2,130},{1... | collective-permute-start | bytes 24584 | tf_op jit(solution)/shard_map/ppermute | solution.py:637

commit v7 on v6

--- a/solution.py
+++ b/solution.py
@@ -28,6 +28,7 @@
 ORIGIN = (0, 0)
 ORIGIN_PLACE = 15
 PARTS = 2
+OWN_PARTS = 4
 
 
 def iota(shape, axis):
@@ -120,7 +121,19 @@
     return line, columns, parts[0][tiles:]
 
 
-def border_kernel(groups, owner_ref, counts_ref, vert_ref, hori_ref, line_ref, out_ref, firsts_ref, right_ref, stack):
+def border_kernel(
+    groups, owner_ref, counts_ref, vert_ref, hori_ref, line_ref, fixed_ref, moving_ref,
+    out_ref, firsts_ref, right_ref, own_fixed_ref, own_moving_ref, stack, sems,
+):
+    length = own_fixed_ref.shape[0]
+    part = length // OWN_PARTS
+    own = []
+    for n in range(OWN_PARTS):
+        at, behind = pl.ds(n * part, part), pl.ds(length + n * part, part)
+        own.append(pltpu.make_async_copy(fixed_ref.at[at], own_fixed_ref.at[at], sems.at[2 * n]))
+        own.append(pltpu.make_async_copy(moving_ref.at[behind], own_moving_ref.at[at], sems.at[2 * n + 1]))
+    for copy in own:
+        copy.start()
     rows, cols = hori_ref.shape
     tiles = cols // TILE_W
     last_group = lax.axis_index("group") == groups - 1
@@ -229,13 +242,16 @@
     turned = jnp.transpose(stack[...])[0:tiles, :]
     upright = (lane <= COLUMN_XTL) | (lane >= COLUMN_HELP)
     out_ref[...] = jnp.where(upright, turned, table)
+    for copy in own:
+        copy.wait()
 
 
 def match_kernel(
     fixed_ref, moving_ref, offsets_ref, table_ref, firsts_ref, right_ref, line_ref, above_ref, across_ref, beside_ref,
     out_ref, lines_ref, next_columns_ref, prev_columns_ref, scores_ref, shifts_ref,
 ):
-    patches, flow, corr = fixed_ref.shape[1:]
+    patches, _, flow = offsets_ref.shape[1:]
+    corr = fixed_ref.shape[1]
     half = patches // 2
     rows = right_ref.shape[0]
     tiles = line_ref.shape[0]
@@ -244,13 +260,11 @@
 
     def receive(near_ref, far_ref):
         for first in range(0, patches, 2):
-            own = slice(first, first + 2)
+            start = first % half * flow
             if first < half:
-                fixed = fixed_ref[0, own].reshape(pair, corr)
-                moving = near_ref[first * flow : (first + 2) * flow, :]
+                fixed, moving = fixed_ref[start : start + pair, :], near_ref[start : start + pair, :]
             else:
-                fixed = far_ref[(first - half) * flow : (first + 2 - half) * flow, :]
-                moving = moving_ref[0, own].reshape(pair, corr)
+                fixed, moving = far_ref[start : start + pair, :], moving_ref[start : start + pair, :]
             scores = lax.dot_general(moving, fixed, (((1,), (1,)), ((), ())), preferred_element_type=F32)
             scores_ref[:, first * flow : (first + 2) * flow] = jnp.where(
                 lower, scores[0:flow, :], scores[flow:pair, :]
@@ -709,15 +723,19 @@
     def borders(*refs):
         border_kernel(groups, *refs)
 
-    table, firsts, right = pl.pallas_call(
+    half_features = pltpu.VMEM((length // 2, corr), fixed_desc.dtype)
+    table, firsts, right, own_fixed, own_moving = pl.pallas_call(
         borders,
-        out_shape=(in_vmem(border), in_vmem(lines_shape), in_vmem(upright)),
-        in_specs=[scalars] * 2 + [local] * 3,
-        out_specs=(local,) * 3,
-        scratch_shapes=[pltpu.VMEM((TILE_W, TILE_W), F32)],
+        out_shape=(in_vmem(border), in_vmem(lines_shape), in_vmem(upright), half_features, half_features),
+        in_specs=[scalars] * 2 + [local] * 3 + [hbm] * 2,
+        out_specs=(local,) * 5,
+        scratch_shapes=[pltpu.VMEM((TILE_W, TILE_W), F32), pltpu.SemaphoreType.DMA((2 * OWN_PARTS,))],
         compiler_params=modest,
         name="borders",
-    )(owner, counts, vert, hori, line)
+    )(
+        owner, counts, vert, hori, line,
+        *(pltpu.with_memory_space_constraint(x.reshape(length, corr), pltpu.HBM) for x in (fixed_desc, moving_desc)),
+    )
     mine, lines, next_columns, prev_columns = pl.pallas_call(
         match_kernel,
         out_shape=(
@@ -729,7 +747,7 @@
         scratch_shapes=[pltpu.VMEM((flow, length), F32), pltpu.VMEM((tiles, TILE_W), F32)],
         compiler_params=modest,
         name="match",
-    )(fixed_desc, moving_desc, offsets, table, firsts, right, line, above, across, beside)
+    )(own_fixed, own_moving, offsets, table, firsts, right, line, above, across, beside)
 
     turned = [(z + FIRST_Z) % chips_z for z in range(chips_z)]
     seen = lax.all_to_all(mine, "z", 0, 0, tiled=True, axis_index_groups=[turned]).reshape(-1, TILE_W)

time: 55.4 us -> 55.3 us (level)
  starting transfers between devices: 20.3 us -> 19.2 us
  Pallas kernels: 6.74 us -> 7.72 us
    all_to_all x1, starting transfers between devices: 7.92 us -> 6.83 us  [body(): lax.all_to_all(copies, ('group',) + SEC, 0, 0, tiled=True, axis_index_gro...]
    pallas_call x1, Pallas kernels: 0.89 us -> 1.97 us  [body(): pl.pallas_call(borders, out_shape=(in_vmem(border), in_vmem(lines_shape),...]
  transfers between devices with their start and end apart: 5 -> 5, of which waited for: 1 -> 1; matrix products, arithmetic and copies ran while one was open for 0% -> 0% of each run, Pallas kernels for 2% -> 4%
where the time goes in v7:
time: 55.3 us; the launch traced here: 54.9 us
  blocking collectives  25.1 us (45%)
  starting transfers between devices  19.2 us (35%)
  Pallas kernels  7.72 us (14%)
  between operations  1.41 us (3%)
  waiting for transfers between devices  0.9 us (2%)
  local copies, waits for them, and re-layouts  0.64 us (1%)
    all_to_all x1, blocking collectives, body(): lax.all_to_all(mine, 'z', 0, 0, tiled=True, axis_index_groups=[turned])  20.7 us
    ppermute x2, starting transfers between devices, swap(): return lax.ppermute(block, SEC, route)  9.48 us
    all_to_all x1, starting transfers between devices, body(): lax.all_to_all(copies, ('group',) + SEC, 0, 0, tiled=True, axis_index_gro...  6.83 us
    all_gather x1, blocking collectives, body(): lax.all_gather(seen, 'core', axis=0, tiled=True, axis_index_groups=[cores])  4.4 us
    ppermute x2, starting transfers between devices, from_behind(): return lax.ppermute(block, axis, route)  2.86 us
    pallas_call x1, Pallas kernels, body(): pl.pallas_call(both_iterations, out_shape=(field, field), in_specs=[local...  2.72 us
    pallas_call x1, Pallas kernels, body(): pl.pallas_call(borders, out_shape=(in_vmem(border), in_vmem(lines_shape),...  1.97 us
    pallas_call x1, Pallas kernels, body(): pl.pallas_call(pack_kernel, out_shape=(packed, packed, in_vmem(border)),...  1.38 us
  transfers between devices with their start and end apart: 5, of which 1 were waited for; matrix products, arithmetic and copies ran while one was open for 0% of the time, Pallas kernels for 4%

profile of v7, /device:TPU:1, one launch (start us, length us, event | category | flops | bytes accessed | tf_op | source)
XLA Modules:
  0.0 54.9 jit_solution(2984422604564175529)
XLA Ops:
  0.6 0.0 copy-start
  0.6 0.0 copy-start.1
  0.6 1.4 %pack.1 = (bf16[528,512]{1,0:T(8,128)(2,1)S(1)}, bf16[528,512]{1,0:T(8,128)(2,1)S(1)}, f32[8,128]{1,0:T(8,128)S(1)}) custom-call(bf16[1024,512]{1,0:T(8,128)(2,1)} %bitcast.13, bf16[1024,512]{1,0:T(8,128)(2,1)} %bitcast.15, f32[1,16,1024]{2,1,0:T(8,128)} %vert_ref.1, f32[1,16,1024]{2,1,0:T(8,128)} %hori_ref.1, s32[1,16,2,64]{3,2,1,0:T(2,128)} %offsets_ref.3), custom_call_target="tpu_custom_call" | custom-call | tf_op jit(solution)/shard_map/pack/pallas_call | solution.py:698
  2.0 4.6 %collective-permute-start.1 = (bf16[528,512]{1,0:T(8,128)(2,1)S(1)}, bf16[528,512]{1,0:T(8,128)(2,1)S(1)}, u32[]{:S(2)}, u32[]{:S(2)}) collective-permute-start(bf16[528,512]{1,0:T(8,128)(2,1)S(1)} %get-tuple-element.24), channel_id=1, source_target_pairs={{1,2},{2,1},{3,4},{4,3},{5,6},{6,5},{7,8},{8,7},{9,10},{10,9},{11,... | collective-permute-start | bytes 1622024 | tf_op jit(solution)/shard_map/ppermute | solution.py:677
  6.6 4.9 %collective-permute-start.2 = (bf16[528,512]{1,0:T(8,128)(2,1)S(1)}, bf16[528,512]{1,0:T(8,128)(2,1)S(1)}, u32[]{:S(2)}, u32[]{:S(2)}) collective-permute-start(bf16[528,512]{1,0:T(8,128)(2,1)S(1)} %get-tuple-element.25), channel_id=1, source_target_pairs={{0,1},{1,0},{2,3},{3,2},{4,5},{5,4},{6,7},{7,6},{8,9},{9,8},{10,11... | collective-permute-start | bytes 1622024 | tf_op jit(solution)/shard_map/ppermute | solution.py:677
  11.5 1.3 %collective-permute-start = (f32[8,128]{1,0:T(8,128)S(1)}, f32[8,128]{1,0:T(8,128)S(1)}, u32[]{:S(2)}, u32[]{:S(2)}) collective-permute-start(f32[8,128]{1,0:T(8,128)S(1)} %get-tuple-element.18.refs_4_.line_ref.refs_3_), channel_id=1, source_target_pairs={{0,128},{128,256},{256,384},{1,129},{129,257},{257,385},{2,130},{1... | collective-permute-start | bytes 12296 | tf_op jit(solution)/shard_map/ppermute | solution.py:651
  13.5 0.0 copy-start.3
  13.5 0.0 copy-done
  13.5 0.0 copy-done.1
  13.5 0.6 %copy-done.3 = s32[1,16]{1,0:T(1,128)S(1)} copy-done((s32[1,16]{1,0:T(1,128)S(1)}, s32[1,16]{1,0:T(1,128)}, u32[]{:S(2)}) %copy-start.3) | copy-done | bytes 88
  14.1 2.0 %borders.1 = (f32[8,128]{1,0:T(8,128)S(1)}, f32[16,128]{1,0:T(8,128)S(1)}, f32[16,128]{1,0:T(8,128)S(1)}, bf16[512,512]{1,0:T(8,128)(2,1)S(1)}, bf16[512,512]{1,0:T(8,128)(2,1)S(1)}) custom-call(s32[1,16]{1,0:T(1,128)S(1)} %copy-done.3, s32[1,1]{1,0:T(1,128)S(6)} %copy.9.refs_1_, f32[16,1024]{1,0:T(8,128)S(1)} %bitcast.8, f32[16,1024]{1,0:T(8,128)S(1)} %bitcast.10, ...), custom_call_target="tpu_custom_call" | custom-call | tf_op jit(solution)/shard_map/borders/pallas_call | solution.py:727
  16.1 0.0 collective-permute-done.above_ref.refs_4_
  16.1 0.0 collective-permute-done.1.across_ref
  16.1 0.0 collective-permute-done.2.beside_ref
  16.1 0.0 copy-done.2
  16.2 0.9 %match.1 = (f32[16,2,128]{2,1,0:T(2,128)S(1)}, f32[16,128]{1,0:T(8,128)S(1)}, f32[16,128]{1,0:T(8,128)S(1)}, f32[16,128]{1,0:T(8,128)S(1)}) custom-call(bf16[512,512]{1,0:T(8,128)(2,1)S(1)} %get-tuple-element.19.fixed_ref, bf16[512,512]{1,0:T(8,128)(2,1)S(1)} %get-tuple-element.20.moving_ref, s32[1,16,2,64]{3,2,1,0:T(2,128)S(1)} %copy-done.2, ...), custom_call_target="tpu_custom_call" | custom-call | tf_op jit(solution)/shard_map/match/pallas_call | solution.py:739
  17.1 20.7 %all_to_all.10 = f32[16,2,128]{2,1,0:T(2,128)S(1)} all-to-all(f32[16,2,128]{2,1,0:T(2,128)S(1)} %get-tuple-element.27), channel_id=1, replica_groups={{64,72,80,88,96,104,112,120,0,8,16,24,32,40,48,56},{65,73,81,89,97,105,..., dimensions={0} | all-to-all | bytes 32768 | tf_op jit(solution)/shard_map/all_to_all | solution.py:753
  37.8 0.8 %copies.1 = f32[16,24,128]{2,1,0:T(8,128)} custom-call(f32[32,128]{1,0:T(8,128)S(1)} %bitcast.12), custom_call_target="tpu_custom_call" | custom-call | tf_op jit(solution)/shard_map/copies/pallas_call | solution.py:758
  38.5 6.8 %all-to-all-start.1 = ((f32[16,24,128]{2,1,0:T(8,128)}), f32[16,24,128]{2,1,0:T(8,128)S(1)}, u32[]{:S(2)}, u32[]{:S(2)}) async-start(f32[16,24,128]{2,1,0:T(8,128)} %copies.1), calls=%async_computation.1 | async-start | bytes 393216 | tf_op jit(solution)/shard_map/all_to_all | solution.py:767
  45.4 1.6 %collective-permute-start.3 = (f32[16,128]{1,0:T(8,128)S(1)}, f32[16,128]{1,0:T(8,128)S(1)}, u32[]{:S(2)}, u32[]{:S(2)}) collective-permute-start(f32[16,128]{1,0:T(8,128)S(1)} %get-tuple-element.29.refs_5_), channel_id=1, source_target_pairs={{0,128},{128,256},{256,384},{1,129},{129,257},{257,385},{2,130},{1... | collective-permute-start | bytes 24584 | tf_op jit(solution)/shard_map/ppermute | solution.py:651
  46.9 0.9 %all-to-all-done.1 = f32[16,24,128]{2,1,0:T(8,128)S(1)} async-done(((f32[16,24,128]{2,1,0:T(8,128)}), f32[16,24,128]{2,1,0:T(8,128)S(1)}, u32[]{:S(2)}, u32[]{:S(2)}) %all-to-all-start.1) | async-done | bytes 196640 | tf_op jit(solution)/shard_map/all_to_all | solution.py:767
  47.8 4.4 %all_gather.3.refs_0_ = f32[768,128]{1,0:T(8,128)S(1)} all-gather(f32[384,128]{1,0:T(8,128)S(1)} %bitcast.17), channel_id=1, replica_groups={{1,0},{3,2},{5,4},{7,6},{9,8},{11,10},{13,12},{15,14},{17,16},{19,18},{..., dimensions={0}, use_global_device_ids=true | all-gather | bytes 589824 | tf_op jit(solution)/shard_map/all_gather | solution.py:771
  52.2 0.0 collective-permute-done.3.refs_6_
  52.2 2.7 %stack.1 = (f32[2,16,1024]{2,1,0:T(8,128)}, f32[2,16,1024]{2,1,0:T(8,128)}) custom-call(f32[768,128]{1,0:T(8,128)S(1)} %all_gather.3.refs_0_, f32[16,1024]{1,0:T(8,128)S(1)} %bitcast.9, f32[16,1024]{1,0:T(8,128)S(1)} %bitcast.11, f32[8,128]{1,0:T(8,128)S(1)} %get-tuple-element.18.refs_4_.line_ref.refs_3_, ...), custom_call_target="tpu_custom_call" | custom-call | tf_op jit(solution)/shard_map/stack/pallas_call | solution.py:780
  (1 shorter events, 0.0 us)
Async XLA Ops:
  0.6 12.9 %copy-start = (f32[1,16,1024]{2,1,0:T(8,128)S(1)}, f32[1,16,1024]{2,1,0:T(8,128)}, u32[]{:S(2)}) copy-start(f32[1,16,1024]{2,1,0:T(8,128)} %vert_ref.1) | copy-start | bytes 196612
  0.6 12.9 %copy-start.1 = (f32[1,16,1024]{2,1,0:T(8,128)S(1)}, f32[1,16,1024]{2,1,0:T(8,128)}, u32[]{:S(2)}) copy-start(f32[1,16,1024]{2,1,0:T(8,128)} %hori_ref.1) | copy-start | bytes 196612
  2.0 14.1 %collective-permute-start.1 = (bf16[528,512]{1,0:T(8,128)(2,1)S(1)}, bf16[528,512]{1,0:T(8,128)(2,1)S(1)}, u32[]{:S(2)}, u32[]{:S(2)}) collective-permute-start(bf16[528,512]{1,0:T(8,128)(2,1)S(1)} %get-tuple-element.24), channel_id=1, source_target_pairs={{1,2},{2,1},{3,4},{4,3},{5,6},{6,5},{7,8},{8,7},{9,10},{10,9},{11,... | collective-permute-start | bytes 1622024 | tf_op jit(solution)/shard_map/ppermute | solution.py:677
  6.6 9.5 %collective-permute-start.2 = (bf16[528,512]{1,0:T(8,128)(2,1)S(1)}, bf16[528,512]{1,0:T(8,128)(2,1)S(1)}, u32[]{:S(2)}, u32[]{:S(2)}) collective-permute-start(bf16[528,512]{1,0:T(8,128)(2,1)S(1)} %get-tuple-element.25), channel_id=1, source_target_pairs={{0,1},{1,0},{2,3},{3,2},{4,5},{5,4},{6,7},{7,6},{8,9},{9,8},{10,11... | collective-permute-start | bytes 1622024 | tf_op jit(solution)/shard_map/ppermute | solution.py:677
  11.5 4.6 %collective-permute-start = (f32[8,128]{1,0:T(8,128)S(1)}, f32[8,128]{1,0:T(8,128)S(1)}, u32[]{:S(2)}, u32[]{:S(2)}) collective-permute-start(f32[8,128]{1,0:T(8,128)S(1)} %get-tuple-element.18.refs_4_.line_ref.refs_3_), channel_id=1, source_target_pairs={{0,128},{128,256},{256,384},{1,129},{129,257},{257,385},{2,130},{1... | collective-permute-start | bytes 12296 | tf_op jit(solution)/shard_map/ppermute | solution.py:651
  13.5 0.7 %copy-start.3 = (s32[1,16]{1,0:T(1,128)S(1)}, s32[1,16]{1,0:T(1,128)}, u32[]{:S(2)}) copy-start(s32[1,16]{1,0:T(1,128)} %refs_0_.1) | copy-start | bytes 196
  14.1 2.0 %copy-start.2 = (s32[1,16,2,64]{3,2,1,0:T(2,128)S(1)}, s32[1,16,2,64]{3,2,1,0:T(2,128)}, u32[]{:S(2)}) copy-start(s32[1,16,2,64]{3,2,1,0:T(2,128)} %offsets_ref.3) | copy-start | bytes 24580
  38.5 9.3 %all-to-all-start.1 = ((f32[16,24,128]{2,1,0:T(8,128)}), f32[16,24,128]{2,1,0:T(8,128)S(1)}, u32[]{:S(2)}, u32[]{:S(2)}) async-start(f32[16,24,128]{2,1,0:T(8,128)} %copies.1), calls=%async_computation.1 | async-start | bytes 393216 | tf_op jit(solution)/shard_map/all_to_all | solution.py:767
  45.4 6.9 %collective-permute-start.3 = (f32[16,128]{1,0:T(8,128)S(1)}, f32[16,128]{1,0:T(8,128)S(1)}, u32[]{:S(2)}, u32[]{:S(2)}) collective-permute-start(f32[16,128]{1,0:T(8,128)S(1)} %get-tuple-element.29.refs_5_), channel_id=1, source_target_pairs={{0,128},{128,256},{256,384},{1,129},{129,257},{257,385},{2,130},{1... | collective-permute-start | bytes 24584 | tf_op jit(solution)/shard_map/ppermute | solution.py:651

commit v8 on v6

--- a/solution.py
+++ b/solution.py
@@ -22,7 +22,7 @@
 COLUMN_FAR = 21
 COLUMN_HELP = 23
 GROUP_LANES = 24
-FIRST_Z = 8
+FIRST_Z = 9
 FIRST_GROUP = 2
 FIRST_CHIP = (2, 2)
 ORIGIN = (0, 0)

time: 55.4 us -> 55.4 us (level)
  no operation moved by 1% of the time
where the time goes in v8:
time: 55.4 us; the launch traced here: 55 us
  blocking collectives  25.1 us (45%)
  starting transfers between devices  20.2 us (36%)
  Pallas kernels  6.74 us (12%)
  between operations  1.42 us (3%)
  waiting for transfers between devices  0.92 us (2%)
  local copies, waits for them, and re-layouts  0.65 us (1%)
    all_to_all x1, blocking collectives, body(): lax.all_to_all(mine, 'z', 0, 0, tiled=True, axis_index_groups=[turned])  20.6 us
    ppermute x2, starting transfers between devices, swap(): return lax.ppermute(block, SEC, route)  9.48 us
    all_to_all x1, starting transfers between devices, body(): lax.all_to_all(copies, ('group',) + SEC, 0, 0, tiled=True, axis_index_gro...  7.85 us
    all_gather x1, blocking collectives, body(): lax.all_gather(seen, 'core', axis=0, tiled=True, axis_index_groups=[cores])  4.55 us
    ppermute x2, starting transfers between devices, from_behind(): return lax.ppermute(block, axis, route)  2.86 us
    pallas_call x1, Pallas kernels, body(): pl.pallas_call(both_iterations, out_shape=(field, field), in_specs=[local...  2.72 us
    pallas_call x1, Pallas kernels, body(): pl.pallas_call(pack_kernel, out_shape=(packed, packed, in_vmem(border)),...  1.48 us
  transfers between devices with their start and end apart: 5, of which 1 were waited for; matrix products, arithmetic and copies ran while one was open for 0% of the time, Pallas kernels for 2%

profile of v8, /device:TPU:1, one launch (start us, length us, event | category | flops | bytes accessed | tf_op | source)
XLA Modules:
  0.0 55.0 jit_solution(4146298287064318918)
XLA Ops:
  0.7 1.5 %pack.1 = (bf16[528,512]{1,0:T(8,128)(2,1)S(1)}, bf16[528,512]{1,0:T(8,128)(2,1)S(1)}, f32[8,128]{1,0:T(8,128)S(1)}) custom-call(bf16[1024,512]{1,0:T(8,128)(2,1)} %bitcast.9, bf16[1024,512]{1,0:T(8,128)(2,1)} %bitcast.8, f32[1,16,1024]{2,1,0:T(8,128)} %vert_ref.1, f32[1,16,1024]{2,1,0:T(8,128)} %hori_ref.1, s32[1,16,2,64]{3,2,1,0:T(2,128)} %offsets_ref.3), custom_call_target="tpu_custom_call" | custom-call | tf_op jit(solution)/shard_map/pack/pallas_call | solution.py:684
  2.2 4.6 %collective-permute-start.1 = (bf16[528,512]{1,0:T(8,128)(2,1)S(1)}, bf16[528,512]{1,0:T(8,128)(2,1)S(1)}, u32[]{:S(2)}, u32[]{:S(2)}) collective-permute-start(bf16[528,512]{1,0:T(8,128)(2,1)S(1)} %get-tuple-element.20), channel_id=1, source_target_pairs={{1,2},{2,1},{3,4},{4,3},{5,6},{6,5},{7,8},{8,7},{9,10},{10,9},{11,... | collective-permute-start | bytes 1622024 | tf_op jit(solution)/shard_map/ppermute | solution.py:663
  6.8 4.9 %collective-permute-start.2 = (bf16[528,512]{1,0:T(8,128)(2,1)S(1)}, bf16[528,512]{1,0:T(8,128)(2,1)S(1)}, u32[]{:S(2)}, u32[]{:S(2)}) collective-permute-start(bf16[528,512]{1,0:T(8,128)(2,1)S(1)} %get-tuple-element.21), channel_id=1, source_target_pairs={{0,1},{1,0},{2,3},{3,2},{4,5},{5,4},{6,7},{7,6},{8,9},{9,8},{10,11... | collective-permute-start | bytes 1622024 | tf_op jit(solution)/shard_map/ppermute | solution.py:663
  11.7 1.3 %collective-permute-start = (f32[8,128]{1,0:T(8,128)S(1)}, f32[8,128]{1,0:T(8,128)S(1)}, u32[]{:S(2)}, u32[]{:S(2)}) collective-permute-start(f32[8,128]{1,0:T(8,128)S(1)} %get-tuple-element.16.refs_4_.line_ref.refs_3_), channel_id=1, source_target_pairs={{0,128},{128,256},{256,384},{1,129},{129,257},{257,385},{2,130},{1... | collective-permute-start | bytes 12296 | tf_op jit(solution)/shard_map/ppermute | solution.py:637
  13.6 0.0 copy-start.5
  13.6 0.0 copy-done.2
  13.6 0.0 copy-done.3
  13.6 0.6 %copy-done.5 = s32[1,16]{1,0:T(1,128)S(1)} copy-done((s32[1,16]{1,0:T(1,128)S(1)}, s32[1,16]{1,0:T(1,128)}, u32[]{:S(2)}) %copy-start.5) | copy-done | bytes 88
  14.3 0.9 %borders.1 = (f32[8,128]{1,0:T(8,128)S(1)}, f32[16,128]{1,0:T(8,128)S(1)}, f32[16,128]{1,0:T(8,128)S(1)}) custom-call(s32[1,16]{1,0:T(1,128)S(1)} %copy-done.5, s32[1,1]{1,0:T(1,128)S(6)} %copy.9.refs_1_, f32[16,1024]{1,0:T(8,128)S(1)} %bitcast.10, f32[16,1024]{1,0:T(8,128)S(1)} %bitcast.12, f32[8,128]{1,0:T(8,128)S(1)} %get-tuple-element.16.refs_4_.line_ref.refs_3_), custom_call_target="tpu_custom_call" | custom-call | tf_op jit(solution)/shard_map/borders/pallas_call | solution.py:712
  15.1 0.0 collective-permute-done.above_ref.refs_4_
  15.1 0.0 collective-permute-done.1.across_ref
  15.2 0.0 collective-permute-done.2.beside_ref
  15.2 0.0 copy-done
  15.2 0.0 copy-done.1
  15.2 0.0 copy-done.4
  15.2 0.9 %match.1 = (f32[16,2,128]{2,1,0:T(2,128)S(1)}, f32[16,128]{1,0:T(8,128)S(1)}, f32[16,128]{1,0:T(8,128)S(1)}, f32[16,128]{1,0:T(8,128)S(1)}) custom-call(bf16[1,16,64,512]{3,2,1,0:T(8,128)(2,1)S(1)} %copy-done, bf16[1,16,64,512]{3,2,1,0:T(8,128)(2,1)S(1)} %copy-done.1, s32[1,16,2,64]{3,2,1,0:T(2,128)S(1)} %copy-done.4, ...), custom_call_target="tpu_custom_call" | custom-call | tf_op jit(solution)/shard_map/match/pallas_call | solution.py:721
  16.1 20.6 %all_to_all.10 = f32[16,2,128]{2,1,0:T(2,128)S(1)} all-to-all(f32[16,2,128]{2,1,0:T(2,128)S(1)} %get-tuple-element.23), channel_id=1, replica_groups={{72,80,88,96,104,112,120,0,8,16,24,32,40,48,56,64},{73,81,89,97,105,113..., dimensions={0} | all-to-all | bytes 32768 | tf_op jit(solution)/shard_map/all_to_all | solution.py:735
  36.7 0.8 %copies.1 = f32[16,24,128]{2,1,0:T(8,128)} custom-call(f32[32,128]{1,0:T(8,128)S(1)} %bitcast.14), custom_call_target="tpu_custom_call" | custom-call | tf_op jit(solution)/shard_map/copies/pallas_call | solution.py:740
  37.4 7.9 %all-to-all-start.1 = ((f32[16,24,128]{2,1,0:T(8,128)}), f32[16,24,128]{2,1,0:T(8,128)S(1)}, u32[]{:S(2)}, u32[]{:S(2)}) async-start(f32[16,24,128]{2,1,0:T(8,128)} %copies.1), calls=%async_computation.1 | async-start | bytes 393216 | tf_op jit(solution)/shard_map/all_to_all | solution.py:749
  45.3 1.6 %collective-permute-start.3 = (f32[16,128]{1,0:T(8,128)S(1)}, f32[16,128]{1,0:T(8,128)S(1)}, u32[]{:S(2)}, u32[]{:S(2)}) collective-permute-start(f32[16,128]{1,0:T(8,128)S(1)} %get-tuple-element.25.refs_5_), channel_id=1, source_target_pairs={{0,128},{128,256},{256,384},{1,129},{129,257},{257,385},{2,130},{1... | collective-permute-start | bytes 24584 | tf_op jit(solution)/shard_map/ppermute | solution.py:637
  46.9 0.9 %all-to-all-done.1 = f32[16,24,128]{2,1,0:T(8,128)S(1)} async-done(((f32[16,24,128]{2,1,0:T(8,128)}), f32[16,24,128]{2,1,0:T(8,128)S(1)}, u32[]{:S(2)}, u32[]{:S(2)}) %all-to-all-start.1) | async-done | bytes 196640 | tf_op jit(solution)/shard_map/all_to_all | solution.py:749
  47.8 4.5 %all_gather.3.refs_0_ = f32[768,128]{1,0:T(8,128)S(1)} all-gather(f32[384,128]{1,0:T(8,128)S(1)} %bitcast.15), channel_id=1, replica_groups={{1,0},{3,2},{5,4},{7,6},{9,8},{11,10},{13,12},{15,14},{17,16},{19,18},{..., dimensions={0}, use_global_device_ids=true | all-gather | bytes 589824 | tf_op jit(solution)/shard_map/all_gather | solution.py:753
  52.3 0.0 collective-permute-done.3.refs_6_
  52.3 2.7 %stack.1 = (f32[2,16,1024]{2,1,0:T(8,128)}, f32[2,16,1024]{2,1,0:T(8,128)}) custom-call(f32[768,128]{1,0:T(8,128)S(1)} %all_gather.3.refs_0_, f32[16,1024]{1,0:T(8,128)S(1)} %bitcast.11, f32[16,1024]{1,0:T(8,128)S(1)} %bitcast.13, f32[8,128]{1,0:T(8,128)S(1)} %get-tuple-element.16.refs_4_.line_ref.refs_3_, ...), custom_call_target="tpu_custom_call" | custom-call | tf_op jit(solution)/shard_map/stack/pallas_call | solution.py:762
  (5 shorter events, 0.0 us)
Async XLA Ops:
  0.6 13.0 %copy-start.2 = (f32[1,16,1024]{2,1,0:T(8,128)S(1)}, f32[1,16,1024]{2,1,0:T(8,128)}, u32[]{:S(2)}) copy-start(f32[1,16,1024]{2,1,0:T(8,128)} %vert_ref.1) | copy-start | bytes 196612
  0.6 13.0 %copy-start.3 = (f32[1,16,1024]{2,1,0:T(8,128)S(1)}, f32[1,16,1024]{2,1,0:T(8,128)}, u32[]{:S(2)}) copy-start(f32[1,16,1024]{2,1,0:T(8,128)} %hori_ref.1) | copy-start | bytes 196612
  0.7 14.5 %copy-start = (bf16[1,16,64,512]{3,2,1,0:T(8,128)(2,1)S(1)}, bf16[1,16,64,512]{3,2,1,0:T(8,128)(2,1)}, u32[]{:S(2)}) copy-start(bf16[1,16,64,512]{3,2,1,0:T(8,128)(2,1)} %fixed_ref.1) | copy-start | bytes 3145732
  0.7 14.5 %copy-start.1 = (bf16[1,16,64,512]{3,2,1,0:T(8,128)(2,1)S(1)}, bf16[1,16,64,512]{3,2,1,0:T(8,128)(2,1)}, u32[]{:S(2)}) copy-start(bf16[1,16,64,512]{3,2,1,0:T(8,128)(2,1)} %moving_ref.1) | copy-start | bytes 3145732
  2.2 13.0 %collective-permute-start.1 = (bf16[528,512]{1,0:T(8,128)(2,1)S(1)}, bf16[528,512]{1,0:T(8,128)(2,1)S(1)}, u32[]{:S(2)}, u32[]{:S(2)}) collective-permute-start(bf16[528,512]{1,0:T(8,128)(2,1)S(1)} %get-tuple-element.20), channel_id=1, source_target_pairs={{1,2},{2,1},{3,4},{4,3},{5,6},{6,5},{7,8},{8,7},{9,10},{10,9},{11,... | collective-permute-start | bytes 1622024 | tf_op jit(solution)/shard_map/ppermute | solution.py:663
  6.8 8.4 %collective-permute-start.2 = (bf16[528,512]{1,0:T(8,128)(2,1)S(1)}, bf16[528,512]{1,0:T(8,128)(2,1)S(1)}, u32[]{:S(2)}, u32[]{:S(2)}) collective-permute-start(bf16[528,512]{1,0:T(8,128)(2,1)S(1)} %get-tuple-element.21), channel_id=1, source_target_pairs={{0,1},{1,0},{2,3},{3,2},{4,5},{5,4},{6,7},{7,6},{8,9},{9,8},{10,11... | collective-permute-start | bytes 1622024 | tf_op jit(solution)/shard_map/ppermute | solution.py:663
  11.7 3.5 %collective-permute-start = (f32[8,128]{1,0:T(8,128)S(1)}, f32[8,128]{1,0:T(8,128)S(1)}, u32[]{:S(2)}, u32[]{:S(2)}) collective-permute-start(f32[8,128]{1,0:T(8,128)S(1)} %get-tuple-element.16.refs_4_.line_ref.refs_3_), channel_id=1, source_target_pairs={{0,128},{128,256},{256,384},{1,129},{129,257},{257,385},{2,130},{1... | collective-permute-start | bytes 12296 | tf_op jit(solution)/shard_map/ppermute | solution.py:637
  13.6 0.7 %copy-start.5 = (s32[1,16]{1,0:T(1,128)S(1)}, s32[1,16]{1,0:T(1,128)}, u32[]{:S(2)}) copy-start(s32[1,16]{1,0:T(1,128)} %refs_0_.1) | copy-start | bytes 196
  14.3 0.9 %copy-start.4 = (s32[1,16,2,64]{3,2,1,0:T(2,128)S(1)}, s32[1,16,2,64]{3,2,1,0:T(2,128)}, u32[]{:S(2)}) copy-start(s32[1,16,2,64]{3,2,1,0:T(2,128)} %offsets_ref.3) | copy-start | bytes 24580
  37.4 10.3 %all-to-all-start.1 = ((f32[16,24,128]{2,1,0:T(8,128)}), f32[16,24,128]{2,1,0:T(8,128)S(1)}, u32[]{:S(2)}, u32[]{:S(2)}) async-start(f32[16,24,128]{2,1,0:T(8,128)} %copies.1), calls=%async_computation.1 | async-start | bytes 393216 | tf_op jit(solution)/shard_map/all_to_all | solution.py:749
  45.3 7.0 %collective-permute-start.3 = (f32[16,128]{1,0:T(8,128)S(1)}, f32[16,128]{1,0:T(8,128)S(1)}, u32[]{:S(2)}, u32[]{:S(2)}) collective-permute-start(f32[16,128]{1,0:T(8,128)S(1)} %get-tuple-element.25.refs_5_), channel_id=1, source_target_pairs={{0,128},{128,256},{256,384},{1,129},{129,257},{257,385},{2,130},{1... | collective-permute-start | bytes 24584 | tf_op jit(solution)/shard_map/ppermute | solution.py:637

commit v9 on v6

--- a/solution.py
+++ b/solution.py
@@ -27,7 +27,7 @@
 FIRST_CHIP = (2, 2)
 ORIGIN = (0, 0)
 ORIGIN_PLACE = 15
-PARTS = 2
+PARTS = 1
 
 
 def iota(shape, axis):

time: 55.4 us -> 55.4 us (level)
  no operation moved by 1% of the time
where the time goes in v9:
time: 55.4 us; the launch traced here: 55 us
  blocking collectives  25.1 us (45%)
  starting transfers between devices  20.3 us (37%)
  Pallas kernels  6.74 us (12%)
  between operations  1.42 us (3%)
  waiting for transfers between devices  0.92 us (2%)
  local copies, waits for them, and re-layouts  0.65 us (1%)
    all_to_all x1, blocking collectives, body(): lax.all_to_all(mine, 'z', 0, 0, tiled=True, axis_index_groups=[turned])  20.7 us
    ppermute x2, starting transfers between devices, swap(): return lax.ppermute(block, SEC, route)  9.48 us
    all_to_all x1, starting transfers between devices, body(): lax.all_to_all(copies, ('group',) + SEC, 0, 0, tiled=True, axis_index_gro...  7.92 us
    all_gather x1, blocking collectives, body(): lax.all_gather(seen, 'core', axis=0, tiled=True, axis_index_groups=[cores])  4.35 us
    ppermute x2, starting transfers between devices, from_behind(): return lax.ppermute(block, axis, route)  2.86 us
    pallas_call x1, Pallas kernels, body(): pl.pallas_call(both_iterations, out_shape=(field, field), in_specs=[local...  2.72 us
    pallas_call x1, Pallas kernels, body(): pl.pallas_call(pack_kernel, out_shape=(packed, packed, in_vmem(border)),...  1.47 us
  transfers between devices with their start and end apart: 5, of which 1 were waited for; matrix products, arithmetic and copies ran while one was open for 0% of the time, Pallas kernels for 2%

profile of v9, /device:TPU:1, one launch (start us, length us, event | category | flops | bytes accessed | tf_op | source)
XLA Modules:
  0.0 55.0 jit_solution(13834999500622072877)
XLA Ops:
  0.7 1.5 %pack.1 = (bf16[528,512]{1,0:T(8,128)(2,1)S(1)}, bf16[528,512]{1,0:T(8,128)(2,1)S(1)}, f32[8,128]{1,0:T(8,128)S(1)}) custom-call(bf16[1024,512]{1,0:T(8,128)(2,1)} %bitcast.9, bf16[1024,512]{1,0:T(8,128)(2,1)} %bitcast.8, f32[1,16,1024]{2,1,0:T(8,128)} %vert_ref.1, f32[1,16,1024]{2,1,0:T(8,128)} %hori_ref.1, s32[1,16,2,64]{3,2,1,0:T(2,128)} %offsets_ref.3), custom_call_target="tpu_custom_call" | custom-call | tf_op jit(solution)/shard_map/pack/pallas_call | solution.py:684
  2.2 4.6 %collective-permute-start.1 = (bf16[528,512]{1,0:T(8,128)(2,1)S(1)}, bf16[528,512]{1,0:T(8,128)(2,1)S(1)}, u32[]{:S(2)}, u32[]{:S(2)}) collective-permute-start(bf16[528,512]{1,0:T(8,128)(2,1)S(1)} %get-tuple-element.20), channel_id=1, source_target_pairs={{1,2},{2,1},{3,4},{4,3},{5,6},{6,5},{7,8},{8,7},{9,10},{10,9},{11,... | collective-permute-start | bytes 1622024 | tf_op jit(solution)/shard_map/ppermute | solution.py:663
  6.8 4.9 %collective-permute-start.2 = (bf16[528,512]{1,0:T(8,128)(2,1)S(1)}, bf16[528,512]{1,0:T(8,128)(2,1)S(1)}, u32[]{:S(2)}, u32[]{:S(2)}) collective-permute-start(bf16[528,512]{1,0:T(8,128)(2,1)S(1)} %get-tuple-element.21), channel_id=1, source_target_pairs={{0,1},{1,0},{2,3},{3,2},{4,5},{5,4},{6,7},{7,6},{8,9},{9,8},{10,11... | collective-permute-start | bytes 1622024 | tf_op jit(solution)/shard_map/ppermute | solution.py:663
  11.6 1.3 %collective-permute-start = (f32[8,128]{1,0:T(8,128)S(1)}, f32[8,128]{1,0:T(8,128)S(1)}, u32[]{:S(2)}, u32[]{:S(2)}) collective-permute-start(f32[8,128]{1,0:T(8,128)S(1)} %get-tuple-element.16.refs_4_.line_ref.refs_3_), channel_id=1, source_target_pairs={{0,128},{128,256},{256,384},{1,129},{129,257},{257,385},{2,130},{1... | collective-permute-start | bytes 12296 | tf_op jit(solution)/shard_map/ppermute | solution.py:637
  13.6 0.0 copy-start.5
  13.6 0.0 copy-done.2
  13.6 0.0 copy-done.3
  13.6 0.6 %copy-done.5 = s32[1,16]{1,0:T(1,128)S(1)} copy-done((s32[1,16]{1,0:T(1,128)S(1)}, s32[1,16]{1,0:T(1,128)}, u32[]{:S(2)}) %copy-start.5) | copy-done | bytes 88
  14.3 0.9 %borders.1 = (f32[8,128]{1,0:T(8,128)S(1)}, f32[16,128]{1,0:T(8,128)S(1)}, f32[16,128]{1,0:T(8,128)S(1)}) custom-call(s32[1,16]{1,0:T(1,128)S(1)} %copy-done.5, s32[1,1]{1,0:T(1,128)S(6)} %copy.9.refs_1_, f32[16,1024]{1,0:T(8,128)S(1)} %bitcast.10, f32[16,1024]{1,0:T(8,128)S(1)} %bitcast.12, f32[8,128]{1,0:T(8,128)S(1)} %get-tuple-element.16.refs_4_.line_ref.refs_3_), custom_call_target="tpu_custom_call" | custom-call | tf_op jit(solution)/shard_map/borders/pallas_call | solution.py:712
  15.1 0.0 collective-permute-done.above_ref.refs_4_
  15.1 0.0 collective-permute-done.1.across_ref
  15.1 0.0 collective-permute-done.2.beside_ref
  15.2 0.0 copy-done
  15.2 0.0 copy-done.1
  15.2 0.0 copy-done.4
  15.2 0.9 %match.1 = (f32[16,2,128]{2,1,0:T(2,128)S(1)}, f32[16,128]{1,0:T(8,128)S(1)}, f32[16,128]{1,0:T(8,128)S(1)}, f32[16,128]{1,0:T(8,128)S(1)}) custom-call(bf16[1,16,64,512]{3,2,1,0:T(8,128)(2,1)S(1)} %copy-done, bf16[1,16,64,512]{3,2,1,0:T(8,128)(2,1)S(1)} %copy-done.1, s32[1,16,2,64]{3,2,1,0:T(2,128)S(1)} %copy-done.4, ...), custom_call_target="tpu_custom_call" | custom-call | tf_op jit(solution)/shard_map/match/pallas_call | solution.py:721
  16.1 20.7 %all_to_all.10 = f32[16,2,128]{2,1,0:T(2,128)S(1)} all-to-all(f32[16,2,128]{2,1,0:T(2,128)S(1)} %get-tuple-element.23), channel_id=1, replica_groups={{64,72,80,88,96,104,112,120,0,8,16,24,32,40,48,56},{65,73,81,89,97,105,..., dimensions={0} | all-to-all | bytes 32768 | tf_op jit(solution)/shard_map/all_to_all | solution.py:735
  36.8 0.8 %copies.1 = f32[16,24,128]{2,1,0:T(8,128)} custom-call(f32[32,128]{1,0:T(8,128)S(1)} %bitcast.14), custom_call_target="tpu_custom_call" | custom-call | tf_op jit(solution)/shard_map/copies/pallas_call | solution.py:740
  37.6 7.9 %all-to-all-start.1 = ((f32[16,24,128]{2,1,0:T(8,128)}), f32[16,24,128]{2,1,0:T(8,128)S(1)}, u32[]{:S(2)}, u32[]{:S(2)}) async-start(f32[16,24,128]{2,1,0:T(8,128)} %copies.1), calls=%async_computation.1 | async-start | bytes 393216 | tf_op jit(solution)/shard_map/all_to_all | solution.py:749
  45.5 1.6 %collective-permute-start.3 = (f32[16,128]{1,0:T(8,128)S(1)}, f32[16,128]{1,0:T(8,128)S(1)}, u32[]{:S(2)}, u32[]{:S(2)}) collective-permute-start(f32[16,128]{1,0:T(8,128)S(1)} %get-tuple-element.25.refs_5_), channel_id=1, source_target_pairs={{0,128},{128,256},{256,384},{1,129},{129,257},{257,385},{2,130},{1... | collective-permute-start | bytes 24584 | tf_op jit(solution)/shard_map/ppermute | solution.py:637
  47.1 0.9 %all-to-all-done.1 = f32[16,24,128]{2,1,0:T(8,128)S(1)} async-done(((f32[16,24,128]{2,1,0:T(8,128)}), f32[16,24,128]{2,1,0:T(8,128)S(1)}, u32[]{:S(2)}, u32[]{:S(2)}) %all-to-all-start.1) | async-done | bytes 196640 | tf_op jit(solution)/shard_map/all_to_all | solution.py:749
  48.0 4.4 %all_gather.3.refs_0_ = f32[768,128]{1,0:T(8,128)S(1)} all-gather(f32[384,128]{1,0:T(8,128)S(1)} %bitcast.15), channel_id=1, replica_groups={{1,0},{3,2},{5,4},{7,6},{9,8},{11,10},{13,12},{15,14},{17,16},{19,18},{..., dimensions={0}, use_global_device_ids=true | all-gather | bytes 589824 | tf_op jit(solution)/shard_map/all_gather | solution.py:753
  52.3 0.0 collective-permute-done.3.refs_6_
  52.3 2.7 %stack.1 = (f32[2,16,1024]{2,1,0:T(8,128)}, f32[2,16,1024]{2,1,0:T(8,128)}) custom-call(f32[768,128]{1,0:T(8,128)S(1)} %all_gather.3.refs_0_, f32[16,1024]{1,0:T(8,128)S(1)} %bitcast.11, f32[16,1024]{1,0:T(8,128)S(1)} %bitcast.13, f32[8,128]{1,0:T(8,128)S(1)} %get-tuple-element.16.refs_4_.line_ref.refs_3_, ...), custom_call_target="tpu_custom_call" | custom-call | tf_op jit(solution)/shard_map/stack/pallas_call | solution.py:762
  (5 shorter events, 0.0 us)
Async XLA Ops:
  0.6 13.0 %copy-start.2 = (f32[1,16,1024]{2,1,0:T(8,128)S(1)}, f32[1,16,1024]{2,1,0:T(8,128)}, u32[]{:S(2)}) copy-start(f32[1,16,1024]{2,1,0:T(8,128)} %vert_ref.1) | copy-start | bytes 196612
  0.6 13.0 %copy-start.3 = (f32[1,16,1024]{2,1,0:T(8,128)S(1)}, f32[1,16,1024]{2,1,0:T(8,128)}, u32[]{:S(2)}) copy-start(f32[1,16,1024]{2,1,0:T(8,128)} %hori_ref.1) | copy-start | bytes 196612
  0.7 14.5 %copy-start = (bf16[1,16,64,512]{3,2,1,0:T(8,128)(2,1)S(1)}, bf16[1,16,64,512]{3,2,1,0:T(8,128)(2,1)}, u32[]{:S(2)}) copy-start(bf16[1,16,64,512]{3,2,1,0:T(8,128)(2,1)} %fixed_ref.1) | copy-start | bytes 3145732
  0.7 14.5 %copy-start.1 = (bf16[1,16,64,512]{3,2,1,0:T(8,128)(2,1)S(1)}, bf16[1,16,64,512]{3,2,1,0:T(8,128)(2,1)}, u32[]{:S(2)}) copy-start(bf16[1,16,64,512]{3,2,1,0:T(8,128)(2,1)} %moving_ref.1) | copy-start | bytes 3145732
  2.2 13.0 %collective-permute-start.1 = (bf16[528,512]{1,0:T(8,128)(2,1)S(1)}, bf16[528,512]{1,0:T(8,128)(2,1)S(1)}, u32[]{:S(2)}, u32[]{:S(2)}) collective-permute-start(bf16[528,512]{1,0:T(8,128)(2,1)S(1)} %get-tuple-element.20), channel_id=1, source_target_pairs={{1,2},{2,1},{3,4},{4,3},{5,6},{6,5},{7,8},{8,7},{9,10},{10,9},{11,... | collective-permute-start | bytes 1622024 | tf_op jit(solution)/shard_map/ppermute | solution.py:663
  6.8 8.4 %collective-permute-start.2 = (bf16[528,512]{1,0:T(8,128)(2,1)S(1)}, bf16[528,512]{1,0:T(8,128)(2,1)S(1)}, u32[]{:S(2)}, u32[]{:S(2)}) collective-permute-start(bf16[528,512]{1,0:T(8,128)(2,1)S(1)} %get-tuple-element.21), channel_id=1, source_target_pairs={{0,1},{1,0},{2,3},{3,2},{4,5},{5,4},{6,7},{7,6},{8,9},{9,8},{10,11... | collective-permute-start | bytes 1622024 | tf_op jit(solution)/shard_map/ppermute | solution.py:663
  11.6 3.5 %collective-permute-start = (f32[8,128]{1,0:T(8,128)S(1)}, f32[8,128]{1,0:T(8,128)S(1)}, u32[]{:S(2)}, u32[]{:S(2)}) collective-permute-start(f32[8,128]{1,0:T(8,128)S(1)} %get-tuple-element.16.refs_4_.line_ref.refs_3_), channel_id=1, source_target_pairs={{0,128},{128,256},{256,384},{1,129},{129,257},{257,385},{2,130},{1... | collective-permute-start | bytes 12296 | tf_op jit(solution)/shard_map/ppermute | solution.py:637
  13.6 0.7 %copy-start.5 = (s32[1,16]{1,0:T(1,128)S(1)}, s32[1,16]{1,0:T(1,128)}, u32[]{:S(2)}) copy-start(s32[1,16]{1,0:T(1,128)} %refs_0_.1) | copy-start | bytes 196
  14.3 0.9 %copy-start.4 = (s32[1,16,2,64]{3,2,1,0:T(2,128)S(1)}, s32[1,16,2,64]{3,2,1,0:T(2,128)}, u32[]{:S(2)}) copy-start(s32[1,16,2,64]{3,2,1,0:T(2,128)} %offsets_ref.3) | copy-start | bytes 24580
  37.6 10.4 %all-to-all-start.1 = ((f32[16,24,128]{2,1,0:T(8,128)}), f32[16,24,128]{2,1,0:T(8,128)S(1)}, u32[]{:S(2)}, u32[]{:S(2)}) async-start(f32[16,24,128]{2,1,0:T(8,128)} %copies.1), calls=%async_computation.1 | async-start | bytes 393216 | tf_op jit(solution)/shard_map/all_to_all | solution.py:749
  45.5 6.8 %collective-permute-start.3 = (f32[16,128]{1,0:T(8,128)S(1)}, f32[16,128]{1,0:T(8,128)S(1)}, u32[]{:S(2)}, u32[]{:S(2)}) collective-permute-start(f32[16,128]{1,0:T(8,128)S(1)} %get-tuple-element.25.refs_5_), channel_id=1, source_target_pairs={{0,128},{128,256},{256,384},{1,129},{129,257},{257,385},{2,130},{1... | collective-permute-start | bytes 24584 | tf_op jit(solution)/shard_map/ppermute | solution.py:637
